TPU v7x, 32 devices: a whole 2x2x4 slice. The times are simulated.
32 devices in a mesh: ctx: 8 (over z, x), fsdp: 4 (over y, core).
Axes of the slice: x: 2, y: 2, z: 4, core: 2. Of those that a mesh axis runs over, the one named last changes fastest.
Arguments:
- tokens: bfloat16 [4, 1024, 2048], P('fsdp', 'ctx'), may hold values from -6 to 6
- doc_lengths: int32 [4, 16], P('fsdp'), may hold values from 1 to 512, 1024 in all within a row
- routes: int32 [4, 1024, 3], P('fsdp', 'ctx'), may hold values from 0 to 5, all different within a row
- slot_order: int32 [4, 1024, 3], P('fsdp', 'ctx'), may hold values from 0 to 383, as said below
- attn_gain: bfloat16 [2048], P('fsdp'), may hold values from 0.5 to 1.5
- w_qkv: bfloat16 [2048, 6144], P('fsdp'), may hold values from -0.125 to 0.125
- q_gain: bfloat16 [2048], P('fsdp'), may hold values from 0.5 to 1.5
- k_gain: bfloat16 [2048], P('fsdp'), may hold values from 0.5 to 1.5
- w_out: bfloat16 [2048, 2048], P('fsdp'), may hold values from -0.375 to 0.375
- ffn_gain: bfloat16 [2048], P('fsdp'), may hold values from 0.5 to 1.5
- w_router: bfloat16 [2048, 6], P('fsdp'), may hold values from -0.09375 to 0.09375
- w_gate: bfloat16 [6, 2048, 1024], P(None, None, 'fsdp'), may hold values from -0.125 to 0.125
- w_up: bfloat16 [6, 2048, 1024], P(None, None, 'fsdp'), may hold values from -0.125 to 0.125
- w_down: bfloat16 [6, 1024, 2048], P(None, 'fsdp'), may hold values from -0.75 to 0.75
- cotangent: bfloat16 [4, 1024, 2048], P('fsdp', 'ctx'), may hold values from -6 to 6
Outputs:
- activations: bfloat16 [4, 1024, 2048], P('fsdp', 'ctx')
- input_grad: float32 [4, 1024, 2048], P('fsdp', 'ctx')
- g_attn_gain: float32 [2048], P('fsdp')
- g_qkv: float32 [2048, 6144], P('fsdp', 'ctx')
- g_q_gain: float32 [2048], P('fsdp')
- g_k_gain: float32 [2048], P('fsdp')
- g_out: float32 [2048, 2048], P('fsdp', 'ctx')
- g_ffn_gain: float32 [2048], P('fsdp')
- g_router: float32 [2048, 6], P('fsdp')
- g_gate: float32 [6, 2048, 1024], P(None, 'ctx', 'fsdp')
- g_up: float32 [6, 2048, 1024], P(None, 'ctx', 'fsdp')
- g_down: float32 [6, 1024, 2048], P(None, 'fsdp', 'ctx')
Inputs may be any that keep to these rules, and one draw needn't show every extreme that they name: `slot_order`: within each aligned block of 128 rows of a stream the 384 values are a permutation. `doc_lengths`: the lengths of a stream sum to 1024; the longest is 512. `routes`: each row names 3 different experts.
All inputs are finite; a program needn't handle non-finite values.
Results may differ from a plain program's by a relative error of at most 0.02.
Values may be sent and summed in bfloat16 or wider, within the bound.
A program may use at most 448 MiB of HBM per device.

v0:
```python
import math

import jax
import jax.numpy as jnp
from jax import lax
from jax.sharding import PartitionSpec as P

HEADS = 16


EPSILON = 1e-05
ROPE_BASE = 10000.0
MASKED = -1e30


def rms_scale(values, gain_vector):
    return (
        values
        * lax.rsqrt(jnp.mean(values * values, axis=-1, keepdims=True) + EPSILON)
        * gain_vector
    )


def rotate(values, inner_pos):
    half_dim = values.shape[-1] // 2
    freq_table = ROPE_BASE ** (-2.0 * jnp.arange(half_dim, dtype=jnp.float32) / values.shape[-1])
    angles = inner_pos.astype(jnp.float32)[:, None] * freq_table[None, :]
    cosine = jnp.cos(angles)[:, None, :]
    sine_part = jnp.sin(angles)[:, None, :]
    first_half = values[..., :half_dim]
    second_half = values[..., half_dim:]
    return jnp.concatenate(
        [
            first_half * cosine - second_half * sine_part,
            second_half * cosine + first_half * sine_part,
        ],
        axis=-1,
    )


def dealt_position(flat_index, per_device, device_count):
    device_index = flat_index // per_device
    within = flat_index % per_device
    half_rows = per_device // 2
    return jnp.where(
        within < half_rows,
        device_index * half_rows + within,
        (2 * device_count - 1 - device_index) * half_rows + within - half_rows,
    )


def document_info(positions, lengths):
    doc_ends = jnp.cumsum(lengths)
    passed = doc_ends[None, :] <= positions[:, None]
    doc_ids = jnp.sum(passed.astype(jnp.int32), axis=1)
    inner_pos = positions - jnp.sum(jnp.where(passed, lengths[None, :], 0), axis=1)
    return (doc_ids, inner_pos)


def slot_table(route_ids, order_ids, capacity, expert_count):
    pair_count = route_ids.shape[0] * route_ids.shape[1]
    expert_flat = route_ids.reshape(pair_count)
    rank_flat = order_ids.reshape(pair_count)
    earlier = (expert_flat[None, :] == expert_flat[:, None]) & (
        rank_flat[None, :] < rank_flat[:, None]
    )
    slot_index = jnp.sum(earlier.astype(jnp.int32), axis=1)
    placed = jnp.where(
        slot_index < capacity, expert_flat * capacity + slot_index, expert_count * capacity
    )
    source = (
        jnp.full((expert_count * capacity + 1,), pair_count, jnp.int32)
        .at[placed]
        .set(jnp.arange(pair_count, dtype=jnp.int32))
    )
    return (placed, source[: expert_count * capacity])


def masked_scores(query_block, key_block, query_pos, query_doc, key_pos, key_doc, score_scale):
    scores = (
        jnp.einsum("qhd,khd->hqk", query_block, key_block, preferred_element_type=jnp.float32)
        * score_scale
    )
    allowed = (query_doc[:, None] == key_doc[None, :]) & (key_pos[None, :] <= query_pos[:, None])
    return jnp.where(allowed[None], scores, MASKED)


def silu_parts(hidden_grad, slot_gate, slot_up):
    sigma = jax.nn.sigmoid(slot_gate)
    gate_grad_low = (hidden_grad * slot_up * sigma * (1.0 + slot_gate * (1.0 - sigma))).astype(
        jnp.bfloat16
    )
    up_grad_low = (hidden_grad * slot_gate * sigma).astype(jnp.bfloat16)
    return (gate_grad_low, up_grad_low)


def on_device(
    tokens,
    doc_lengths,
    routes,
    slot_order,
    attn_gain,
    w_qkv,
    q_gain,
    k_gain,
    w_out,
    ffn_gain,
    w_router,
    w_gate,
    w_up,
    w_down,
    cotangent,
):
    row_count = tokens.shape[1]
    model_width = tokens.shape[2]
    head_count = HEADS
    head_dim = model_width // head_count
    score_scale = head_dim ** (-0.5)
    ctx_count = lax.axis_size("ctx")
    ctx_index = lax.axis_index("ctx")
    total_rows = row_count * ctx_count
    lengths = doc_lengths[0]
    local_pos = dealt_position(
        ctx_index * row_count + jnp.arange(row_count, dtype=jnp.int32), row_count, ctx_count
    )
    local_doc, local_inner = document_info(local_pos, lengths)
    stream_pos = dealt_position(jnp.arange(total_rows, dtype=jnp.int32), row_count, ctx_count)
    stream_doc, stream_inner = document_info(stream_pos, lengths)
    block_rows = math.gcd(total_rows, 512)
    block_count = total_rows // block_rows
    block_ids = jnp.arange(block_count, dtype=jnp.int32)
    gain_one, qkv_weight, gain_query, gain_key, out_weight = (
        lax.all_gather(attn_gain, "fsdp", axis=0, tiled=True),
        lax.all_gather(w_qkv, "fsdp", axis=0, tiled=True),
        lax.all_gather(q_gain, "fsdp", axis=0, tiled=True),
        lax.all_gather(k_gain, "fsdp", axis=0, tiled=True),
        lax.all_gather(w_out, "fsdp", axis=0, tiled=True),
    )
    gain_two, router_weight, gate_weight, up_weight, down_weight = (
        lax.all_gather(ffn_gain, "fsdp", axis=0, tiled=True),
        lax.all_gather(w_router, "fsdp", axis=0, tiled=True),
        lax.all_gather(w_gate, "fsdp", axis=2, tiled=True),
        lax.all_gather(w_up, "fsdp", axis=2, tiled=True),
        lax.all_gather(w_down, "fsdp", axis=1, tiled=True),
    )
    inputs = tokens[0].astype(jnp.float32)
    normed_f, norm_one_pull = jax.vjp(rms_scale, inputs, gain_one.astype(jnp.float32))
    normed_low = normed_f.astype(jnp.bfloat16)
    projected = jnp.dot(normed_low, qkv_weight, preferred_element_type=jnp.float32)
    query_lin = projected[:, :model_width]
    key_lin = projected[:, model_width : 2 * model_width]
    value_low = (
        projected[:, 2 * model_width :]
        .astype(jnp.bfloat16)
        .reshape(row_count, head_count, head_dim)
    )

    def head_shape(values, gain_vector):
        return rotate(
            rms_scale(values, gain_vector).reshape(row_count, head_count, head_dim), local_inner
        )

    query_f, query_pull = jax.vjp(head_shape, query_lin, gain_query.astype(jnp.float32))
    key_f, key_pull = jax.vjp(head_shape, key_lin, gain_key.astype(jnp.float32))
    query_low = query_f.astype(jnp.bfloat16)
    key_low = key_f.astype(jnp.bfloat16)
    keys_all, values_all = (
        lax.all_gather(key_low, "ctx", axis=0, tiled=True),
        lax.all_gather(value_low, "ctx", axis=0, tiled=True),
    )

    def key_slice(block_index):
        first_row = block_index * block_rows
        return (
            lax.dynamic_slice_in_dim(keys_all, first_row, block_rows, 0),
            lax.dynamic_slice_in_dim(values_all, first_row, block_rows, 0),
            lax.dynamic_slice_in_dim(stream_pos, first_row, block_rows, 0),
            lax.dynamic_slice_in_dim(stream_doc, first_row, block_rows, 0),
        )

    def stats_step(carry, block_index):
        running_top, running_total = carry
        key_block, value_block, key_pos, key_doc = key_slice(block_index)
        scores = masked_scores(
            query_low, key_block, local_pos, local_doc, key_pos, key_doc, score_scale
        )
        new_top = jnp.maximum(running_top, jnp.max(scores, axis=-1))
        running_total = running_total * jnp.exp(running_top - new_top) + jnp.sum(
            jnp.exp(scores - new_top[..., None]), axis=-1
        )
        return ((new_top, running_total), None)

    start_stats = (
        jnp.full((head_count, row_count), MASKED, jnp.float32),
        jnp.zeros((head_count, row_count), jnp.float32),
    )
    (score_top, score_total), _ = lax.scan(stats_step, start_stats, block_ids)
    log_total = score_top + jnp.log(score_total)

    def output_step(accum, block_index):
        key_block, value_block, key_pos, key_doc = key_slice(block_index)
        scores = masked_scores(
            query_low, key_block, local_pos, local_doc, key_pos, key_doc, score_scale
        )
        prob_block = jnp.exp(scores - log_total[..., None]).astype(jnp.bfloat16)
        return (
            accum
            + jnp.einsum(
                "hqk,khd->qhd", prob_block, value_block, preferred_element_type=jnp.float32
            ),
            None,
        )

    attended_f, _ = lax.scan(
        output_step, jnp.zeros((row_count, head_count, head_dim), jnp.float32), block_ids
    )
    attended_low = attended_f.reshape(row_count, model_width).astype(jnp.bfloat16)
    mixed = inputs + jnp.dot(attended_low, out_weight, preferred_element_type=jnp.float32)
    normed_two_f, norm_two_pull = jax.vjp(rms_scale, mixed, gain_two.astype(jnp.float32))
    normed_two = normed_two_f.astype(jnp.bfloat16)
    expert_count = gate_weight.shape[0]
    route_ids = routes[0]
    top_count = route_ids.shape[1]
    pair_count = row_count * top_count
    capacity = pair_count // expert_count
    logits = jnp.dot(normed_two, router_weight, preferred_element_type=jnp.float32)
    router_probs = jax.nn.softmax(logits, axis=-1)
    chosen = (
        route_ids[:, :, None] == jnp.arange(expert_count, dtype=jnp.int32)[None, None, :]
    ).astype(jnp.float32)
    gate_values = jnp.sum(chosen * router_probs[:, None, :], axis=-1)
    placed, source = slot_table(route_ids, slot_order[0], capacity, expert_count)
    padded_in = jnp.concatenate([normed_two, jnp.zeros((1, model_width), jnp.bfloat16)], axis=0)
    expert_in = padded_in[source // top_count].reshape(expert_count, capacity, model_width)
    gate_pre = jnp.einsum(
        "ecd,edh->ech", expert_in, gate_weight, preferred_element_type=jnp.float32
    )
    up_pre = jnp.einsum("ecd,edh->ech", expert_in, up_weight, preferred_element_type=jnp.float32)
    hidden_low = (jax.nn.silu(gate_pre) * up_pre).astype(jnp.bfloat16)
    expert_out = jnp.einsum(
        "ech,ehd->ecd", hidden_low, down_weight, preferred_element_type=jnp.float32
    )
    out_padded = jnp.concatenate(
        [
            expert_out.reshape(expert_count * capacity, model_width),
            jnp.zeros((1, model_width), jnp.float32),
        ],
        axis=0,
    )
    per_pair = out_padded[placed].reshape(row_count, top_count, model_width)
    layer_out = mixed + jnp.sum(gate_values[:, :, None] * per_pair, axis=1)
    out_grad = cotangent[0].astype(jnp.float32)
    gate_grad = jnp.sum(out_grad[:, None, :] * per_pair, axis=-1)
    pair_grad = (gate_values[:, :, None] * out_grad[:, None, :]).reshape(pair_count, model_width)
    pair_padded = jnp.concatenate([pair_grad, jnp.zeros((1, model_width), jnp.float32)], axis=0)
    slot_grad = (
        pair_padded[source].reshape(expert_count, capacity, model_width).astype(jnp.bfloat16)
    )

    def expert_step(carry, pieces):
        slot_in, slot_hidden, slot_dy, slot_gate, slot_up, gate_matrix, up_matrix, down_matrix = (
            pieces
        )
        hidden_grad = jnp.einsum(
            "cd,hd->ch", slot_dy, down_matrix, preferred_element_type=jnp.float32
        )
        gate_grad_low, up_grad_low = silu_parts(hidden_grad, slot_gate, slot_up)
        in_grad = jnp.einsum(
            "ch,dh->cd", gate_grad_low, gate_matrix, preferred_element_type=jnp.float32
        ) + jnp.einsum("ch,dh->cd", up_grad_low, up_matrix, preferred_element_type=jnp.float32)
        gate_term = jnp.einsum(
            "cd,ch->dh", slot_in, gate_grad_low, preferred_element_type=jnp.float32
        )
        up_term = jnp.einsum("cd,ch->dh", slot_in, up_grad_low, preferred_element_type=jnp.float32)
        down_term = jnp.einsum(
            "ch,cd->hd", slot_hidden, slot_dy, preferred_element_type=jnp.float32
        )
        gate_shard, up_shard, down_shard = (
            lax.psum_scatter(
                gate_term.astype(jnp.bfloat16), "fsdp", scatter_dimension=1, tiled=True
            ).astype(jnp.float32),
            lax.psum_scatter(
                up_term.astype(jnp.bfloat16), "fsdp", scatter_dimension=1, tiled=True
            ).astype(jnp.float32),
            lax.psum_scatter(
                down_term.astype(jnp.bfloat16), "fsdp", scatter_dimension=0, tiled=True
            ).astype(jnp.float32),
        )
        gate_part, up_part, down_part = (
            lax.psum_scatter(
                gate_shard.astype(jnp.bfloat16), "ctx", scatter_dimension=0, tiled=True
            ).astype(jnp.float32),
            lax.psum_scatter(
                up_shard.astype(jnp.bfloat16), "ctx", scatter_dimension=0, tiled=True
            ).astype(jnp.float32),
            lax.psum_scatter(
                down_shard.astype(jnp.bfloat16), "ctx", scatter_dimension=1, tiled=True
            ).astype(jnp.float32),
        )
        return (carry, (in_grad, gate_part, up_part, down_part))

    _, (expert_in_grad, gate_parts, up_parts, down_parts) = lax.scan(
        expert_step,
        None,
        (expert_in, hidden_low, slot_grad, gate_pre, up_pre, gate_weight, up_weight, down_weight),
    )
    in_padded = jnp.concatenate(
        [
            expert_in_grad.reshape(expert_count * capacity, model_width),
            jnp.zeros((1, model_width), jnp.float32),
        ],
        axis=0,
    )
    normed_two_grad = jnp.sum(in_padded[placed].reshape(row_count, top_count, model_width), axis=1)
    prob_grad_router = jnp.sum(chosen * gate_grad[:, :, None], axis=1)
    logit_grad = (
        router_probs
        * (prob_grad_router - jnp.sum(router_probs * prob_grad_router, axis=-1, keepdims=True))
    ).astype(jnp.bfloat16)
    normed_two_grad = normed_two_grad + jnp.einsum(
        "te,de->td", logit_grad, router_weight, preferred_element_type=jnp.float32
    )
    router_grad = jnp.einsum(
        "td,te->de", normed_two, logit_grad, preferred_element_type=jnp.float32
    )
    mixed_norm_grad, gain_two_grad = norm_two_pull(normed_two_grad)
    mixed_grad = out_grad + mixed_norm_grad
    mixed_low = mixed_grad.astype(jnp.bfloat16)
    out_weight_grad = jnp.einsum(
        "td,te->de", attended_low, mixed_low, preferred_element_type=jnp.float32
    )
    output_grad = (
        jnp.einsum("te,de->td", mixed_low, out_weight, preferred_element_type=jnp.float32)
        .astype(jnp.bfloat16)
        .reshape(row_count, head_count, head_dim)
    )
    row_delta = jnp.sum(output_grad.astype(jnp.float32) * attended_f, axis=-1).T

    def query_grad_step(accum, block_index):
        key_block, value_block, key_pos, key_doc = key_slice(block_index)
        scores = masked_scores(
            query_low, key_block, local_pos, local_doc, key_pos, key_doc, score_scale
        )
        prob_block = jnp.exp(scores - log_total[..., None])
        prob_grad = jnp.einsum(
            "qhd,khd->hqk", output_grad, value_block, preferred_element_type=jnp.float32
        )
        score_grad = (prob_block * (prob_grad - row_delta[..., None])).astype(jnp.bfloat16)
        return (
            accum
            + jnp.einsum("hqk,khd->qhd", score_grad, key_block, preferred_element_type=jnp.float32)
            * score_scale,
            None,
        )

    query_grad, _ = lax.scan(
        query_grad_step, jnp.zeros((row_count, head_count, head_dim), jnp.float32), block_ids
    )
    inner_rows = math.gcd(row_count * lax.axis_size("ctx"), 512)

    def piece_step(carry, piece_index):
        first_row = piece_index * inner_rows
        key_block = lax.dynamic_slice_in_dim(keys_all, first_row, inner_rows, 0)
        value_block = lax.dynamic_slice_in_dim(values_all, first_row, inner_rows, 0)
        key_pos = lax.dynamic_slice_in_dim(stream_pos, first_row, inner_rows, 0)
        key_doc = lax.dynamic_slice_in_dim(stream_doc, first_row, inner_rows, 0)
        scores = masked_scores(
            query_low, key_block, local_pos, local_doc, key_pos, key_doc, score_scale
        )
        prob_block = jnp.exp(scores - log_total[..., None])
        prob_grad = jnp.einsum(
            "qhd,khd->hqk", output_grad, value_block, preferred_element_type=jnp.float32
        )
        score_grad = (prob_block * (prob_grad - row_delta[..., None])).astype(jnp.bfloat16)
        value_part = jnp.einsum(
            "hqk,qhd->khd",
            prob_block.astype(jnp.bfloat16),
            output_grad,
            preferred_element_type=jnp.float32,
        )
        key_part = (
            jnp.einsum("hqk,qhd->khd", score_grad, query_low, preferred_element_type=jnp.float32)
            * score_scale
        )
        return (
            carry,
            jnp.concatenate(
                [
                    key_part.reshape(inner_rows, model_width),
                    value_part.reshape(inner_rows, model_width),
                ],
                axis=1,
            ),
        )

    _, stacked = lax.scan(
        piece_step,
        None,
        jnp.arange(row_count * lax.axis_size("ctx") // inner_rows, dtype=jnp.int32),
    )
    key_value_grad = lax.psum_scatter(
        stacked.reshape(row_count * lax.axis_size("ctx"), 2 * model_width).astype(jnp.bfloat16),
        "ctx",
        scatter_dimension=0,
        tiled=True,
    ).astype(jnp.float32)
    key_grad = key_value_grad[:, :model_width].reshape(row_count, head_count, head_dim)
    value_grad = key_value_grad[:, model_width:]
    query_lin_grad, gain_query_grad = query_pull(query_grad)
    key_lin_grad, gain_key_grad = key_pull(key_grad)
    proj_grad = jnp.concatenate(
        [
            query_lin_grad.astype(jnp.bfloat16),
            key_lin_grad.astype(jnp.bfloat16),
            value_grad.astype(jnp.bfloat16),
        ],
        axis=1,
    )
    qkv_weight_grad = jnp.einsum(
        "td,te->de", normed_low, proj_grad, preferred_element_type=jnp.float32
    )
    normed_grad = jnp.einsum("te,de->td", proj_grad, qkv_weight, preferred_element_type=jnp.float32)
    input_norm_grad, gain_one_grad = norm_one_pull(normed_grad)
    input_grad = mixed_grad + input_norm_grad
    qkv_shard, out_shard = (
        lax.psum_scatter(
            qkv_weight_grad.astype(jnp.bfloat16), "fsdp", scatter_dimension=0, tiled=True
        ).astype(jnp.float32),
        lax.psum_scatter(
            out_weight_grad.astype(jnp.bfloat16), "fsdp", scatter_dimension=0, tiled=True
        ).astype(jnp.float32),
    )
    qkv_part, out_part = (
        lax.psum_scatter(
            qkv_shard.astype(jnp.bfloat16), "ctx", scatter_dimension=1, tiled=True
        ).astype(jnp.float32),
        lax.psum_scatter(
            out_shard.astype(jnp.bfloat16), "ctx", scatter_dimension=1, tiled=True
        ).astype(jnp.float32),
    )
    gain_one_sum, gain_query_sum, gain_key_sum, gain_two_sum, router_sum = lax.psum(
        (gain_one_grad, gain_query_grad, gain_key_grad, gain_two_grad, router_grad), ("ctx", "fsdp")
    )
    shard_rows = model_width // lax.axis_size("fsdp")
    shard_start = lax.axis_index("fsdp") * shard_rows

    def own_rows(full_array):
        return lax.dynamic_slice_in_dim(full_array, shard_start, shard_rows, 0)

    return (
        layer_out.astype(jnp.bfloat16)[None],
        input_grad[None],
        own_rows(gain_one_sum),
        qkv_part,
        own_rows(gain_query_sum),
        own_rows(gain_key_sum),
        out_part,
        own_rows(gain_two_sum),
        own_rows(router_sum),
        gate_parts,
        up_parts,
        down_parts,
    )


def solution(mesh):
    in_specs = (
        P("fsdp", "ctx", None),
        P("fsdp", None),
        P("fsdp", "ctx", None),
        P("fsdp", "ctx", None),
        P("fsdp"),
        P("fsdp", None),
        P("fsdp"),
        P("fsdp"),
        P("fsdp", None),
        P("fsdp"),
        P("fsdp", None),
        P(None, None, "fsdp"),
        P(None, None, "fsdp"),
        P(None, "fsdp", None),
        P("fsdp", "ctx", None),
    )
    out_specs = (
        P("fsdp", "ctx", None),
        P("fsdp", "ctx", None),
        P("fsdp"),
        P("fsdp", "ctx"),
        P("fsdp"),
        P("fsdp"),
        P("fsdp", "ctx"),
        P("fsdp"),
        P("fsdp", None),
        P(None, "ctx", "fsdp"),
        P(None, "ctx", "fsdp"),
        P(None, "fsdp", "ctx"),
    )
    return jax.shard_map(
        on_device, mesh=mesh, in_specs=in_specs, out_specs=out_specs, check_vma=False
    )
```

profile of v0, /device:TPU:5, one launch (start us, length us, event | category | flops | bytes accessed | tf_op | source)
XLA Modules:
  0.0 3808.9 jit_solution(1907969964048741439)
XLA Ops:
  24.9 140.0 %all-gather.12.cloned.1.call-done = bf16[2048,6144]{1,0:T(8,128)(2,1)} async-done(((bf16[512,6144]{1,0:T(8,128)(2,1)}), bf16[2048,6144]{1,0:T(8,128)(2,1)}) %all-gather.12.cloned.1.call-update) | async-done | bytes 25165840 | tf_op jit(solution)/shard_map/all_gather | solution.py:134
  165.0 10.2 fusion.142
  215.4 46.1 %all-gather.16.cloned.1.call-done = bf16[1024,16,128]{0,2,1:T(8,128)(2,1)} async-done(((bf16[128,16,128]{0,2,1:T(8,128)(2,1)}), bf16[1024,16,128]{0,2,1:T(8,128)(2,1)}) %all-gather.16.cloned.1.call-update) | async-done | bytes 4194320 | tf_op jit(solution)/shard_map/all_gather | solution.py:168
  261.4 6.4 copy.178
  267.8 18.3 while.64
  286.1 48.9 %all-gather.14.cloned.1.call-done = bf16[1024,16,128]{2,1,0:T(8,128)(2,1)} async-done(((bf16[128,16,128]{2,1,0:T(8,128)(2,1)}), bf16[1024,16,128]{2,1,0:T(8,128)(2,1)}) %all-gather.14.cloned.1.call-update) | async-done | bytes 4194320 | tf_op jit(solution)/shard_map/all_gather | solution.py:169
  335.0 18.2 while.65
  354.7 38.7 %all-gather.18.cloned.1.call-done = bf16[2048,2048]{1,0:T(8,128)(2,1)} async-done(((bf16[512,2048]{1,0:T(8,128)(2,1)}), bf16[2048,2048]{1,0:T(8,128)(2,1)}) %all-gather.18.cloned.1.call-update) | async-done | bytes 8388624 | tf_op jit(solution)/shard_map/all_gather | solution.py:137
  402.5 150.5 %all-gather.20.cloned.1.call-done = bf16[6,2048,1024]{2,1,0:T(8,128)(2,1)} async-done(((bf16[6,2048,256]{2,1,0:T(8,128)(2,1)}), bf16[6,2048,1024]{2,1,0:T(8,128)(2,1)}) %all-gather.20.cloned.1.call-update) | async-done | bytes 25165840 | tf_op jit(solution)/shard_map/all_gather | solution.py:142
  553.0 12.1 fusion.174
  565.1 147.5 %all-gather.22.cloned.1.call-done = bf16[6,2048,1024]{2,1,0:T(8,128)(2,1)} async-done(((bf16[6,2048,256]{2,1,0:T(8,128)(2,1)}), bf16[6,2048,1024]{2,1,0:T(8,128)(2,1)}) %all-gather.22.cloned.1.call-update) | async-done | bytes 25165840 | tf_op jit(solution)/shard_map/all_gather | solution.py:143
  712.7 14.2 multiply_convert_fusion
  726.9 142.2 %all-gather.24.cloned.1.call-done = bf16[6,1024,2048]{2,1,0:T(8,128)(2,1)} async-done(((bf16[6,256,2048]{2,1,0:T(8,128)(2,1)}), bf16[6,1024,2048]{2,1,0:T(8,128)(2,1)}) %all-gather.24.cloned.1.call-update) | async-done | bytes 25165840 | tf_op jit(solution)/shard_map/all_gather | solution.py:144
  869.1 10.5 fusion.175
  890.8 6.8 multiply_reduce_fusion
  900.6 2080.5 %while.62 = (s32[]{:T(128)}, f32[6,64,2048]{2,1,0:T(8,128)}, f32[6,256,256]{2,1,0:T(8,128)}, f32[6,256,256]{2,1,0:T(8,128)}, f32[6,256,256]{2,1,0:T(8,128)}, /*i...) while((s32[]{:T(128)}, f32[6,64,2048]{2,1,0:T(8,128)}, ...), condition=%wide.region_27.28_spmd, body=%wide.region_20.27_spmd.sunk | while | flops 1618083840 | bytes 88215448 | solution.py:302
  917.3 35.9 reduce-scatter.22.cloned.1.call-done
  953.3 47.0 %reduce-scatter.26.cloned.1.call-done = bf16[2048,256]{1,0:T(8,128)(2,1)} async-done(((bf16[2048,1024]{1,0:T(8,128)(2,1)}), bf16[2048,256]{1,0:T(8,128)(2,1)}) %reduce-scatter.26.cloned.1.call-update) | async-done | bytes 1048592 | tf_op jit(solution)/shard_map/while/body/eval_jaxpr/reduce_scatter | solution.py:282
  1000.3 47.0 %reduce-scatter.30.cloned.1.call-done = bf16[256,2048]{1,0:T(8,128)(2,1)} async-done(((bf16[1024,2048]{1,0:T(8,128)(2,1)}), bf16[256,2048]{1,0:T(8,128)(2,1)}) %reduce-scatter.30.cloned.1.call-update) | async-done | bytes 1048592 | tf_op jit(solution)/shard_map/while/body/eval_jaxpr/reduce_scatter | solution.py:285
  1055.4 58.4 %reduce-scatter.24.cloned.1.call-done = bf16[256,256]{1,0:T(8,128)(2,1)} async-done(((bf16[2048,256]{1,0:T(8,128)(2,1)}), bf16[256,256]{1,0:T(8,128)(2,1)}) %reduce-scatter.24.cloned.1.call-update) | async-done | bytes 131088 | tf_op jit(solution)/shard_map/while/body/eval_jaxpr/reduce_scatter | solution.py:290
  1115.4 64.6 %reduce-scatter.28.cloned.1.call-done = bf16[256,256]{1,0:T(8,128)(2,1)} async-done(((bf16[2048,256]{1,0:T(8,128)(2,1)}), bf16[256,256]{1,0:T(8,128)(2,1)}) %reduce-scatter.28.cloned.1.call-update) | async-done | bytes 131088 | tf_op jit(solution)/shard_map/while/body/eval_jaxpr/reduce_scatter | solution.py:293
  1181.6 64.7 %reduce-scatter.32.cloned.1.call-done = bf16[256,256]{1,0:T(8,128)(2,1)} async-done(((bf16[256,2048]{1,0:T(8,128)(2,1)}), bf16[256,256]{1,0:T(8,128)(2,1)}) %reduce-scatter.32.cloned.1.call-update) | async-done | bytes 131088 | tf_op jit(solution)/shard_map/while/body/eval_jaxpr/reduce_scatter | solution.py:296
  1264.3 35.7 reduce-scatter.22.cloned.1.call-done
  1300.1 46.9 %reduce-scatter.26.cloned.1.call-done = bf16[2048,256]{1,0:T(8,128)(2,1)} async-done(((bf16[2048,1024]{1,0:T(8,128)(2,1)}), bf16[2048,256]{1,0:T(8,128)(2,1)}) %reduce-scatter.26.cloned.1.call-update) | async-done | bytes 1048592 | tf_op jit(solution)/shard_map/while/body/eval_jaxpr/reduce_scatter | solution.py:282
  1347.1 47.0 %reduce-scatter.30.cloned.1.call-done = bf16[256,2048]{1,0:T(8,128)(2,1)} async-done(((bf16[1024,2048]{1,0:T(8,128)(2,1)}), bf16[256,2048]{1,0:T(8,128)(2,1)}) %reduce-scatter.30.cloned.1.call-update) | async-done | bytes 1048592 | tf_op jit(solution)/shard_map/while/body/eval_jaxpr/reduce_scatter | solution.py:285
  1402.1 58.1 %reduce-scatter.24.cloned.1.call-done = bf16[256,256]{1,0:T(8,128)(2,1)} async-done(((bf16[2048,256]{1,0:T(8,128)(2,1)}), bf16[256,256]{1,0:T(8,128)(2,1)}) %reduce-scatter.24.cloned.1.call-update) | async-done | bytes 131088 | tf_op jit(solution)/shard_map/while/body/eval_jaxpr/reduce_scatter | solution.py:290
  1461.9 64.5 %reduce-scatter.28.cloned.1.call-done = bf16[256,256]{1,0:T(8,128)(2,1)} async-done(((bf16[2048,256]{1,0:T(8,128)(2,1)}), bf16[256,256]{1,0:T(8,128)(2,1)}) %reduce-scatter.28.cloned.1.call-update) | async-done | bytes 131088 | tf_op jit(solution)/shard_map/while/body/eval_jaxpr/reduce_scatter | solution.py:293
  1528.0 64.7 %reduce-scatter.32.cloned.1.call-done = bf16[256,256]{1,0:T(8,128)(2,1)} async-done(((bf16[256,2048]{1,0:T(8,128)(2,1)}), bf16[256,256]{1,0:T(8,128)(2,1)}) %reduce-scatter.32.cloned.1.call-update) | async-done | bytes 131088 | tf_op jit(solution)/shard_map/while/body/eval_jaxpr/reduce_scatter | solution.py:296
  1610.8 35.7 reduce-scatter.22.cloned.1.call-done
  1646.6 47.0 %reduce-scatter.26.cloned.1.call-done = bf16[2048,256]{1,0:T(8,128)(2,1)} async-done(((bf16[2048,1024]{1,0:T(8,128)(2,1)}), bf16[2048,256]{1,0:T(8,128)(2,1)}) %reduce-scatter.26.cloned.1.call-update) | async-done | bytes 1048592 | tf_op jit(solution)/shard_map/while/body/eval_jaxpr/reduce_scatter | solution.py:282
  1693.7 47.2 %reduce-scatter.30.cloned.1.call-done = bf16[256,2048]{1,0:T(8,128)(2,1)} async-done(((bf16[1024,2048]{1,0:T(8,128)(2,1)}), bf16[256,2048]{1,0:T(8,128)(2,1)}) %reduce-scatter.30.cloned.1.call-update) | async-done | bytes 1048592 | tf_op jit(solution)/shard_map/while/body/eval_jaxpr/reduce_scatter | solution.py:285
  1748.9 58.3 %reduce-scatter.24.cloned.1.call-done = bf16[256,256]{1,0:T(8,128)(2,1)} async-done(((bf16[2048,256]{1,0:T(8,128)(2,1)}), bf16[256,256]{1,0:T(8,128)(2,1)}) %reduce-scatter.24.cloned.1.call-update) | async-done | bytes 131088 | tf_op jit(solution)/shard_map/while/body/eval_jaxpr/reduce_scatter | solution.py:290
  1808.8 64.4 %reduce-scatter.28.cloned.1.call-done = bf16[256,256]{1,0:T(8,128)(2,1)} async-done(((bf16[2048,256]{1,0:T(8,128)(2,1)}), bf16[256,256]{1,0:T(8,128)(2,1)}) %reduce-scatter.28.cloned.1.call-update) | async-done | bytes 131088 | tf_op jit(solution)/shard_map/while/body/eval_jaxpr/reduce_scatter | solution.py:293
  1874.8 64.7 %reduce-scatter.32.cloned.1.call-done = bf16[256,256]{1,0:T(8,128)(2,1)} async-done(((bf16[256,2048]{1,0:T(8,128)(2,1)}), bf16[256,256]{1,0:T(8,128)(2,1)}) %reduce-scatter.32.cloned.1.call-update) | async-done | bytes 131088 | tf_op jit(solution)/shard_map/while/body/eval_jaxpr/reduce_scatter | solution.py:296
  1957.6 35.7 reduce-scatter.22.cloned.1.call-done
  1993.4 46.9 %reduce-scatter.26.cloned.1.call-done = bf16[2048,256]{1,0:T(8,128)(2,1)} async-done(((bf16[2048,1024]{1,0:T(8,128)(2,1)}), bf16[2048,256]{1,0:T(8,128)(2,1)}) %reduce-scatter.26.cloned.1.call-update) | async-done | bytes 1048592 | tf_op jit(solution)/shard_map/while/body/eval_jaxpr/reduce_scatter | solution.py:282
  2040.3 47.1 %reduce-scatter.30.cloned.1.call-done = bf16[256,2048]{1,0:T(8,128)(2,1)} async-done(((bf16[1024,2048]{1,0:T(8,128)(2,1)}), bf16[256,2048]{1,0:T(8,128)(2,1)}) %reduce-scatter.30.cloned.1.call-update) | async-done | bytes 1048592 | tf_op jit(solution)/shard_map/while/body/eval_jaxpr/reduce_scatter | solution.py:285
  2095.5 58.3 %reduce-scatter.24.cloned.1.call-done = bf16[256,256]{1,0:T(8,128)(2,1)} async-done(((bf16[2048,256]{1,0:T(8,128)(2,1)}), bf16[256,256]{1,0:T(8,128)(2,1)}) %reduce-scatter.24.cloned.1.call-update) | async-done | bytes 131088 | tf_op jit(solution)/shard_map/while/body/eval_jaxpr/reduce_scatter | solution.py:290
  2155.4 64.6 %reduce-scatter.28.cloned.1.call-done = bf16[256,256]{1,0:T(8,128)(2,1)} async-done(((bf16[2048,256]{1,0:T(8,128)(2,1)}), bf16[256,256]{1,0:T(8,128)(2,1)}) %reduce-scatter.28.cloned.1.call-update) | async-done | bytes 131088 | tf_op jit(solution)/shard_map/while/body/eval_jaxpr/reduce_scatter | solution.py:293
  2221.5 64.7 %reduce-scatter.32.cloned.1.call-done = bf16[256,256]{1,0:T(8,128)(2,1)} async-done(((bf16[256,2048]{1,0:T(8,128)(2,1)}), bf16[256,256]{1,0:T(8,128)(2,1)}) %reduce-scatter.32.cloned.1.call-update) | async-done | bytes 131088 | tf_op jit(solution)/shard_map/while/body/eval_jaxpr/reduce_scatter | solution.py:296
  2304.3 35.7 reduce-scatter.22.cloned.1.call-done
  2340.1 46.8 %reduce-scatter.26.cloned.1.call-done = bf16[2048,256]{1,0:T(8,128)(2,1)} async-done(((bf16[2048,1024]{1,0:T(8,128)(2,1)}), bf16[2048,256]{1,0:T(8,128)(2,1)}) %reduce-scatter.26.cloned.1.call-update) | async-done | bytes 1048592 | tf_op jit(solution)/shard_map/while/body/eval_jaxpr/reduce_scatter | solution.py:282
  2387.0 47.2 %reduce-scatter.30.cloned.1.call-done = bf16[256,2048]{1,0:T(8,128)(2,1)} async-done(((bf16[1024,2048]{1,0:T(8,128)(2,1)}), bf16[256,2048]{1,0:T(8,128)(2,1)}) %reduce-scatter.30.cloned.1.call-update) | async-done | bytes 1048592 | tf_op jit(solution)/shard_map/while/body/eval_jaxpr/reduce_scatter | solution.py:285
  2442.2 58.2 %reduce-scatter.24.cloned.1.call-done = bf16[256,256]{1,0:T(8,128)(2,1)} async-done(((bf16[2048,256]{1,0:T(8,128)(2,1)}), bf16[256,256]{1,0:T(8,128)(2,1)}) %reduce-scatter.24.cloned.1.call-update) | async-done | bytes 131088 | tf_op jit(solution)/shard_map/while/body/eval_jaxpr/reduce_scatter | solution.py:290
  2502.0 64.6 %reduce-scatter.28.cloned.1.call-done = bf16[256,256]{1,0:T(8,128)(2,1)} async-done(((bf16[2048,256]{1,0:T(8,128)(2,1)}), bf16[256,256]{1,0:T(8,128)(2,1)}) %reduce-scatter.28.cloned.1.call-update) | async-done | bytes 131088 | tf_op jit(solution)/shard_map/while/body/eval_jaxpr/reduce_scatter | solution.py:293
  2568.2 64.5 %reduce-scatter.32.cloned.1.call-done = bf16[256,256]{1,0:T(8,128)(2,1)} async-done(((bf16[256,2048]{1,0:T(8,128)(2,1)}), bf16[256,256]{1,0:T(8,128)(2,1)}) %reduce-scatter.32.cloned.1.call-update) | async-done | bytes 131088 | tf_op jit(solution)/shard_map/while/body/eval_jaxpr/reduce_scatter | solution.py:296
  2650.8 35.7 reduce-scatter.22.cloned.1.call-done
  2686.6 46.8 %reduce-scatter.26.cloned.1.call-done = bf16[2048,256]{1,0:T(8,128)(2,1)} async-done(((bf16[2048,1024]{1,0:T(8,128)(2,1)}), bf16[2048,256]{1,0:T(8,128)(2,1)}) %reduce-scatter.26.cloned.1.call-update) | async-done | bytes 1048592 | tf_op jit(solution)/shard_map/while/body/eval_jaxpr/reduce_scatter | solution.py:282
  2733.5 47.1 %reduce-scatter.30.cloned.1.call-done = bf16[256,2048]{1,0:T(8,128)(2,1)} async-done(((bf16[1024,2048]{1,0:T(8,128)(2,1)}), bf16[256,2048]{1,0:T(8,128)(2,1)}) %reduce-scatter.30.cloned.1.call-update) | async-done | bytes 1048592 | tf_op jit(solution)/shard_map/while/body/eval_jaxpr/reduce_scatter | solution.py:285
  2788.7 58.2 %reduce-scatter.24.cloned.1.call-done = bf16[256,256]{1,0:T(8,128)(2,1)} async-done(((bf16[2048,256]{1,0:T(8,128)(2,1)}), bf16[256,256]{1,0:T(8,128)(2,1)}) %reduce-scatter.24.cloned.1.call-update) | async-done | bytes 131088 | tf_op jit(solution)/shard_map/while/body/eval_jaxpr/reduce_scatter | solution.py:290
  2848.5 64.7 %reduce-scatter.28.cloned.1.call-done = bf16[256,256]{1,0:T(8,128)(2,1)} async-done(((bf16[2048,256]{1,0:T(8,128)(2,1)}), bf16[256,256]{1,0:T(8,128)(2,1)}) %reduce-scatter.28.cloned.1.call-update) | async-done | bytes 131088 | tf_op jit(solution)/shard_map/while/body/eval_jaxpr/reduce_scatter | solution.py:293
  2914.9 64.6 %reduce-scatter.32.cloned.1.call-done = bf16[256,256]{1,0:T(8,128)(2,1)} async-done(((bf16[256,2048]{1,0:T(8,128)(2,1)}), bf16[256,256]{1,0:T(8,128)(2,1)}) %reduce-scatter.32.cloned.1.call-update) | async-done | bytes 131088 | tf_op jit(solution)/shard_map/while/body/eval_jaxpr/reduce_scatter | solution.py:296
  3000.9 6.7 convolution_convert_fusion.5
  3015.4 42.0 %while.63 = (s32[]{:T(128)}, bf16[2,512,4096]{1,2,0:T(8,128)(2,1)}, s32[128]{0:T(128)S(1)}, s32[2]{0:T(128)S(1)}, s32[1024]{0:T(1024)S(1)}, /*index=5*/s32[1024]...) while((s32[]{:T(128)}, bf16[2,512,4096]{1,2,0:T(8,128)(2,1)}, ...), condition=%wide.region_38.39_spmd.clone, body=%wide.region_37.38_spmd.clone.sunk | while | flops 1094913536 | bytes 35887336 | solution.py:396
  3057.4 11.4 copy.198
  3076.8 23.8 while.66
  3101.6 117.0 %reduce-scatter.12.cloned.1.call-done = bf16[128,4096]{1,0:T(8,128)(2,1)} async-done(((bf16[1024,4096]{1,0:T(8,128)(2,1)}), bf16[128,4096]{1,0:T(8,128)(2,1)}) %reduce-scatter.12.cloned.1.call-update) | async-done | bytes 1048592 | tf_op jit(solution)/shard_map/reduce_scatter | solution.py:401
  3236.3 13.7 convolution_convert_fusion.3
  3251.9 15.4 fusion.128
  3267.3 23.6 reduce-scatter.18.cloned.1.call-done
  3291.0 182.8 %reduce-scatter.14.cloned.1.call-done = bf16[512,6144]{1,0:T(8,128)(2,1)} async-done(((bf16[2048,6144]{1,0:T(8,128)(2,1)}), bf16[512,6144]{1,0:T(8,128)(2,1)}) %reduce-scatter.14.cloned.1.call-update) | async-done | bytes 6291472 | tf_op jit(solution)/shard_map/reduce_scatter | solution.py:426
  3475.1 130.7 %all-reduce.11.cloned.1.call-done = (f32[2048]{0:T(1024)}, f32[2048]{0:T(1024)}, f32[2048]{0:T(1024)}, f32[2048]{0:T(1024)}, f32[2048,6]{0,1:T(8,128)}) async-done(((f32[2048]{0:T(1024)}, f32[2048]{0:T(1024)}, f32[2048]{0:T(1024)}, f32[2048]{0:T(1024)}, f32[2048,6]{0,1:T(8,128)}), (f32[2048]{0:T(1024)}, f32[2048]{0:T(1024)}, f32[2048]{0:T(1024)}, f32[2048]{0:T(1024)}, ...) | async-done | bytes 81936 | tf_op jit(solution)/shard_map/psum | solution.py:441
  3612.5 65.1 %reduce-scatter.20.cloned.1.call-done = bf16[512,256]{1,0:T(8,128)(2,1)} async-done(((bf16[512,2048]{1,0:T(8,128)(2,1)}), bf16[512,256]{1,0:T(8,128)(2,1)}) %reduce-scatter.20.cloned.1.call-update) | async-done | bytes 262160 | tf_op jit(solution)/shard_map/reduce_scatter | solution.py:437
  3679.4 120.2 %reduce-scatter.16.cloned.1.call-done = bf16[512,768]{1,0:T(8,128)(2,1)} async-done(((bf16[512,6144]{1,0:T(8,128)(2,1)}), bf16[512,768]{1,0:T(8,128)(2,1)}) %reduce-scatter.16.cloned.1.call-update) | async-done | bytes 786448 | tf_op jit(solution)/shard_map/reduce_scatter | solution.py:434
  (477 shorter events, 422.5 us)
Async XLA Ops:
  7.2 157.7 %all-gather.12.cloned.1.call-start = ((), (), s32[]{:S(2)}) async-start(), calls=%async_computation.11 | async-start | bytes 31457280 | tf_op jit(solution)/shard_map/all_gather | solution.py:134
  8.0 253.5 %all-gather.16.cloned.1.call-start = ((), (), s32[]{:S(2)}) async-start(), calls=%async_computation.13 | async-start | bytes 4718592 | tf_op jit(solution)/shard_map/all_gather | solution.py:168
  13.7 161.5 %copy-start.34 = (f32[4,1,512]{2,1,0:T(1,128)}, f32[4,1,512]{2,1,0:T(1,128)S(1)}, u32[]{:S(2)}) copy-start(f32[4,1,512]{2,1,0:T(1,128)S(1)} %convert_element_type.185) | copy-start | bytes 24580
  18.9 156.6 %copy-start.40 = (f32[4,1,512]{2,1,0:T(1,128)}, f32[4,1,512]{2,1,0:T(1,128)S(1)}, u32[]{:S(2)}) copy-start(f32[4,1,512]{2,1,0:T(1,128)S(1)} %convert_element_type.186) | copy-start | bytes 24580
  24.1 151.4 %copy-start.42 = (f32[4,1,512]{2,1,0:T(1,128)}, f32[4,1,512]{2,1,0:T(1,128)S(1)}, u32[]{:S(2)}) copy-start(f32[4,1,512]{2,1,0:T(1,128)S(1)} %convert_element_type.187) | copy-start | bytes 24580
  24.7 140.3 %copy-start.64 = (f32[128]{0:T(128)}, f32[128]{0:T(128)S(1)}, u32[]{:S(2)}) copy-start(f32[128]{0:T(128)S(1)} %fusion.134) | copy-start | bytes 1540
  24.7 150.5 %copy-start.44 = (f32[128]{0:T(128)}, f32[128]{0:T(128)S(1)}, u32[]{:S(2)}) copy-start(f32[128]{0:T(128)S(1)} %fusion.167) | copy-start | bytes 1540
  24.9 157.6 %copy-start.36 = (f32[128,64]{0,1:T(8,128)}, f32[128,64]{0,1:T(8,128)S(1)}, u32[]{:S(2)}) copy-start(f32[128,64]{0,1:T(8,128)S(1)} %get-tuple-element.886) | copy-start | bytes 98308
  24.9 157.6 %copy-start.38 = (f32[128,64]{0,1:T(8,128)}, f32[128,64]{0,1:T(8,128)S(1)}, u32[]{:S(2)}) copy-start(f32[128,64]{0,1:T(8,128)S(1)} %get-tuple-element.887) | copy-start | bytes 98308
  185.9 149.0 %all-gather.14.cloned.1.call-start = ((), (), s32[]{:S(2)}) async-start(), calls=%async_computation.12 | async-start | bytes 4718592 | tf_op jit(solution)/shard_map/all_gather | solution.py:169
  187.0 206.4 %all-gather.18.cloned.1.call-start = ((), (), s32[]{:S(2)}) async-start(), calls=%async_computation.14 | async-start | bytes 10485760 | tf_op jit(solution)/shard_map/all_gather | solution.py:137
  187.6 365.4 %all-gather.20.cloned.1.call-start = ((), (), s32[]{:S(2)}) async-start(), calls=%async_computation.15 | async-start | bytes 31457280 | tf_op jit(solution)/shard_map/all_gather | solution.py:142
  188.2 524.5 %all-gather.22.cloned.1.call-start = ((), (), s32[]{:S(2)}) async-start(), calls=%async_computation.16 | async-start | bytes 31457280 | tf_op jit(solution)/shard_map/all_gather | solution.py:143
  188.8 680.3 %all-gather.24.cloned.1.call-start = ((), (), s32[]{:S(2)}) async-start(), calls=%async_computation.17 | async-start | bytes 31457280 | tf_op jit(solution)/shard_map/all_gather | solution.py:144
  335.0 58.5 %copy-start.13 = (bf16[1,128,2048]{2,1,0:T(8,128)(2,1)S(1)}, bf16[1,128,2048]{2,1,0:T(8,128)(2,1)}, u32[]{:S(2)}) copy-start(bf16[1,128,2048]{2,1,0:T(8,128)(2,1)} %param.25) | copy-start | bytes 1572868
  402.5 310.2 %copy-start.4 = (bf16[384,2048]{1,0:T(8,128)(2,1)}, bf16[384,2048]{1,0:T(8,128)(2,1)S(1)}, u32[]{:S(2)}) copy-start(bf16[384,2048]{1,0:T(8,128)(2,1)S(1)} %gather_fusion) | copy-start | bytes 4718596
  726.9 152.7 %copy-start.23 = (bf16[6,64,1024]{2,1,0:T(8,128)(2,1)}, bf16[6,64,1024]{2,1,0:T(8,128)(2,1)S(1)}, u32[]{:S(2)}) copy-start(bf16[6,64,1024]{2,1,0:T(8,128)(2,1)S(1)} %get-tuple-element.1370) | copy-start | bytes 2359300
  900.8 52.4 %reduce-scatter.22.cloned.1.call-start = ((), (), s32[]{:S(2)}) async-start(), calls=%async_computation.24 | async-start | bytes 5242880 | tf_op jit(solution)/shard_map/while/body/eval_jaxpr/reduce_scatter | solution.py:279
  908.8 91.5 %reduce-scatter.26.cloned.1.call-start = ((), (), s32[]{:S(2)}) async-start(), calls=%async_computation.26 | async-start | bytes 5242880 | tf_op jit(solution)/shard_map/while/body/eval_jaxpr/reduce_scatter | solution.py:282
  913.0 134.3 %reduce-scatter.30.cloned.1.call-start = ((), (), s32[]{:S(2)}) async-start(), calls=%async_computation.28 | async-start | bytes 5242880 | tf_op jit(solution)/shard_map/while/body/eval_jaxpr/reduce_scatter | solution.py:285
  917.2 196.5 %reduce-scatter.24.cloned.1.call-start = ((), (), s32[]{:S(2)}) async-start(), calls=%async_computation.25 | async-start | bytes 1179648 | tf_op jit(solution)/shard_map/while/body/eval_jaxpr/reduce_scatter | solution.py:290
  953.2 226.7 %reduce-scatter.28.cloned.1.call-start = ((), (), s32[]{:S(2)}) async-start(), calls=%async_computation.27 | async-start | bytes 1179648 | tf_op jit(solution)/shard_map/while/body/eval_jaxpr/reduce_scatter | solution.py:293
  1000.3 246.0 %reduce-scatter.32.cloned.1.call-start = ((), (), s32[]{:S(2)}) async-start(), calls=%async_computation.29 | async-start | bytes 1179648 | tf_op jit(solution)/shard_map/while/body/eval_jaxpr/reduce_scatter | solution.py:296
  1247.9 52.2 %reduce-scatter.22.cloned.1.call-start = ((), (), s32[]{:S(2)}) async-start(), calls=%async_computation.24 | async-start | bytes 5242880 | tf_op jit(solution)/shard_map/while/body/eval_jaxpr/reduce_scatter | solution.py:279
  1255.8 91.2 %reduce-scatter.26.cloned.1.call-start = ((), (), s32[]{:S(2)}) async-start(), calls=%async_computation.26 | async-start | bytes 5242880 | tf_op jit(solution)/shard_map/while/body/eval_jaxpr/reduce_scatter | solution.py:282
  1260.0 134.0 %reduce-scatter.30.cloned.1.call-start = ((), (), s32[]{:S(2)}) async-start(), calls=%async_computation.28 | async-start | bytes 5242880 | tf_op jit(solution)/shard_map/while/body/eval_jaxpr/reduce_scatter | solution.py:285
  1264.2 196.0 %reduce-scatter.24.cloned.1.call-start = ((), (), s32[]{:S(2)}) async-start(), calls=%async_computation.25 | async-start | bytes 1179648 | tf_op jit(solution)/shard_map/while/body/eval_jaxpr/reduce_scatter | solution.py:290
  1300.1 226.4 %reduce-scatter.28.cloned.1.call-start = ((), (), s32[]{:S(2)}) async-start(), calls=%async_computation.27 | async-start | bytes 1179648 | tf_op jit(solution)/shard_map/while/body/eval_jaxpr/reduce_scatter | solution.py:293
  1347.0 245.8 %reduce-scatter.32.cloned.1.call-start = ((), (), s32[]{:S(2)}) async-start(), calls=%async_computation.29 | async-start | bytes 1179648 | tf_op jit(solution)/shard_map/while/body/eval_jaxpr/reduce_scatter | solution.py:296
  1594.4 52.2 %reduce-scatter.22.cloned.1.call-start = ((), (), s32[]{:S(2)}) async-start(), calls=%async_computation.24 | async-start | bytes 5242880 | tf_op jit(solution)/shard_map/while/body/eval_jaxpr/reduce_scatter | solution.py:279
  1602.3 91.3 %reduce-scatter.26.cloned.1.call-start = ((), (), s32[]{:S(2)}) async-start(), calls=%async_computation.26 | async-start | bytes 5242880 | tf_op jit(solution)/shard_map/while/body/eval_jaxpr/reduce_scatter | solution.py:282
  1606.6 134.3 %reduce-scatter.30.cloned.1.call-start = ((), (), s32[]{:S(2)}) async-start(), calls=%async_computation.28 | async-start | bytes 5242880 | tf_op jit(solution)/shard_map/while/body/eval_jaxpr/reduce_scatter | solution.py:285
  1610.8 196.4 %reduce-scatter.24.cloned.1.call-start = ((), (), s32[]{:S(2)}) async-start(), calls=%async_computation.25 | async-start | bytes 1179648 | tf_op jit(solution)/shard_map/while/body/eval_jaxpr/reduce_scatter | solution.py:290
  1646.6 226.6 %reduce-scatter.28.cloned.1.call-start = ((), (), s32[]{:S(2)}) async-start(), calls=%async_computation.27 | async-start | bytes 1179648 | tf_op jit(solution)/shard_map/while/body/eval_jaxpr/reduce_scatter | solution.py:293
  1693.7 245.9 %reduce-scatter.32.cloned.1.call-start = ((), (), s32[]{:S(2)}) async-start(), calls=%async_computation.29 | async-start | bytes 1179648 | tf_op jit(solution)/shard_map/while/body/eval_jaxpr/reduce_scatter | solution.py:296
  1941.1 52.2 %reduce-scatter.22.cloned.1.call-start = ((), (), s32[]{:S(2)}) async-start(), calls=%async_computation.24 | async-start | bytes 5242880 | tf_op jit(solution)/shard_map/while/body/eval_jaxpr/reduce_scatter | solution.py:279
  1949.1 91.2 %reduce-scatter.26.cloned.1.call-start = ((), (), s32[]{:S(2)}) async-start(), calls=%async_computation.26 | async-start | bytes 5242880 | tf_op jit(solution)/shard_map/while/body/eval_jaxpr/reduce_scatter | solution.py:282
  1953.3 134.1 %reduce-scatter.30.cloned.1.call-start = ((), (), s32[]{:S(2)}) async-start(), calls=%async_computation.28 | async-start | bytes 5242880 | tf_op jit(solution)/shard_map/while/body/eval_jaxpr/reduce_scatter | solution.py:285
  1957.5 196.2 %reduce-scatter.24.cloned.1.call-start = ((), (), s32[]{:S(2)}) async-start(), calls=%async_computation.25 | async-start | bytes 1179648 | tf_op jit(solution)/shard_map/while/body/eval_jaxpr/reduce_scatter | solution.py:290
  1993.3 226.6 %reduce-scatter.28.cloned.1.call-start = ((), (), s32[]{:S(2)}) async-start(), calls=%async_computation.27 | async-start | bytes 1179648 | tf_op jit(solution)/shard_map/while/body/eval_jaxpr/reduce_scatter | solution.py:293
  2040.3 246.0 %reduce-scatter.32.cloned.1.call-start = ((), (), s32[]{:S(2)}) async-start(), calls=%async_computation.29 | async-start | bytes 1179648 | tf_op jit(solution)/shard_map/while/body/eval_jaxpr/reduce_scatter | solution.py:296
  2287.9 52.2 %reduce-scatter.22.cloned.1.call-start = ((), (), s32[]{:S(2)}) async-start(), calls=%async_computation.24 | async-start | bytes 5242880 | tf_op jit(solution)/shard_map/while/body/eval_jaxpr/reduce_scatter | solution.py:279
  2295.8 91.1 %reduce-scatter.26.cloned.1.call-start = ((), (), s32[]{:S(2)}) async-start(), calls=%async_computation.26 | async-start | bytes 5242880 | tf_op jit(solution)/shard_map/while/body/eval_jaxpr/reduce_scatter | solution.py:282
  2300.0 134.1 %reduce-scatter.30.cloned.1.call-start = ((), (), s32[]{:S(2)}) async-start(), calls=%async_computation.28 | async-start | bytes 5242880 | tf_op jit(solution)/shard_map/while/body/eval_jaxpr/reduce_scatter | solution.py:285
  2304.3 196.1 %reduce-scatter.24.cloned.1.call-start = ((), (), s32[]{:S(2)}) async-start(), calls=%async_computation.25 | async-start | bytes 1179648 | tf_op jit(solution)/shard_map/while/body/eval_jaxpr/reduce_scatter | solution.py:290
  2340.0 226.5 %reduce-scatter.28.cloned.1.call-start = ((), (), s32[]{:S(2)}) async-start(), calls=%async_computation.27 | async-start | bytes 1179648 | tf_op jit(solution)/shard_map/while/body/eval_jaxpr/reduce_scatter | solution.py:293
  2387.0 245.8 %reduce-scatter.32.cloned.1.call-start = ((), (), s32[]{:S(2)}) async-start(), calls=%async_computation.29 | async-start | bytes 1179648 | tf_op jit(solution)/shard_map/while/body/eval_jaxpr/reduce_scatter | solution.py:296
  2634.4 52.2 %reduce-scatter.22.cloned.1.call-start = ((), (), s32[]{:S(2)}) async-start(), calls=%async_computation.24 | async-start | bytes 5242880 | tf_op jit(solution)/shard_map/while/body/eval_jaxpr/reduce_scatter | solution.py:279
  2642.3 91.1 %reduce-scatter.26.cloned.1.call-start = ((), (), s32[]{:S(2)}) async-start(), calls=%async_computation.26 | async-start | bytes 5242880 | tf_op jit(solution)/shard_map/while/body/eval_jaxpr/reduce_scatter | solution.py:282
  2646.6 134.1 %reduce-scatter.30.cloned.1.call-start = ((), (), s32[]{:S(2)}) async-start(), calls=%async_computation.28 | async-start | bytes 5242880 | tf_op jit(solution)/shard_map/while/body/eval_jaxpr/reduce_scatter | solution.py:285
  2650.8 196.2 %reduce-scatter.24.cloned.1.call-start = ((), (), s32[]{:S(2)}) async-start(), calls=%async_computation.25 | async-start | bytes 1179648 | tf_op jit(solution)/shard_map/while/body/eval_jaxpr/reduce_scatter | solution.py:290
  2686.6 226.7 %reduce-scatter.28.cloned.1.call-start = ((), (), s32[]{:S(2)}) async-start(), calls=%async_computation.27 | async-start | bytes 1179648 | tf_op jit(solution)/shard_map/while/body/eval_jaxpr/reduce_scatter | solution.py:293
  2733.5 246.0 %reduce-scatter.32.cloned.1.call-start = ((), (), s32[]{:S(2)}) async-start(), calls=%async_computation.29 | async-start | bytes 1179648 | tf_op jit(solution)/shard_map/while/body/eval_jaxpr/reduce_scatter | solution.py:296
  2981.1 237.5 %reduce-scatter.12.cloned.1.call-start = ((), (), s32[]{:S(2)}) async-start(), calls=%async_computation.18 | async-start | bytes 9437184 | tf_op jit(solution)/shard_map/reduce_scatter | solution.py:401
  3068.8 222.1 %reduce-scatter.18.cloned.1.call-start = ((), (), s32[]{:S(2)}) async-start(), calls=%async_computation.21 | async-start | bytes 10485760 | tf_op jit(solution)/shard_map/reduce_scatter | solution.py:429
  3075.7 398.0 %reduce-scatter.14.cloned.1.call-start = ((), (), s32[]{:S(2)}) async-start(), calls=%async_computation.19 | async-start | bytes 31457280 | tf_op jit(solution)/shard_map/reduce_scatter | solution.py:426
  3101.6 119.6 %copy-start.37 = (f32[128,64]{0,1:T(8,128)S(1)}, f32[128,64]{0,1:T(8,128)}, u32[]{:S(2)}) copy-start(f32[128,64]{0,1:T(8,128)} %copy-done.36) | copy-start | bytes 98308
  3101.6 119.6 %copy-start.39 = (f32[128,64]{0,1:T(8,128)S(1)}, f32[128,64]{0,1:T(8,128)}, u32[]{:S(2)}) copy-start(f32[128,64]{0,1:T(8,128)} %copy-done.38) | copy-start | bytes 98308
  3250.1 355.8 %all-reduce.11.cloned.1.call-start = ((), (), s32[]{:S(2)}) async-start(), calls=%async_computation.23 | async-start | bytes 196608 | tf_op jit(solution)/shard_map/psum | solution.py:441
  3267.3 410.3 %reduce-scatter.20.cloned.1.call-start = ((), (), s32[]{:S(2)}) async-start(), calls=%async_computation.22 | async-start | bytes 2359296 | tf_op jit(solution)/shard_map/reduce_scatter | solution.py:437
  3290.9 182.9 %copy-start.65 = (f32[128]{0:T(128)S(1)}, f32[128]{0:T(128)}, u32[]{:S(2)}) copy-start(f32[128]{0:T(128)} %copy-done.64) | copy-start | bytes 1540
  3290.9 182.9 %copy-start.11 = (f32[128,2048]{1,0:T(8,128)S(1)}, f32[128,2048]{1,0:T(8,128)}, u32[]{:S(2)}) copy-start(f32[128,2048]{1,0:T(8,128)} %copy-done.9) | copy-start | bytes 3145732
  3290.9 182.9 %copy-start.31 = (f32[128,2048]{1,0:T(8,128)S(1)}, f32[128,2048]{1,0:T(8,128)}, u32[]{:S(2)}) copy-start(f32[128,2048]{1,0:T(8,128)} %get-tuple-element.895) | copy-start | bytes 3145732
  3290.9 508.6 %reduce-scatter.16.cloned.1.call-start = ((), (), s32[]{:S(2)}) async-start(), calls=%async_computation.20 | async-start | bytes 7077888 | tf_op jit(solution)/shard_map/reduce_scatter | solution.py:434
  (51 other events, 459.8 us)
Sparse Core Ops, SparseCore 0:
  9.6 155.2 all-gather.11
  186.1 75.3 all-gather.15
  264.1 70.7 all-gather.13
  336.4 57.0 all-gather.17
  394.9 158.1 all-gather.19
  554.5 158.1 all-gather.21
  714.2 154.8 all-gather.23
  908.9 44.2 reduce-scatter.21
  955.7 44.4 reduce-scatter.25
  1002.8 44.5 reduce-scatter.29
  1050.8 62.9 reduce-scatter.23
  1117.4 62.5 reduce-scatter.27
  1183.4 62.8 reduce-scatter.31
  1255.9 44.0 reduce-scatter.21
  1302.4 44.5 reduce-scatter.25
  1349.5 44.5 reduce-scatter.29
  1397.3 62.8 reduce-scatter.23
  1463.9 62.4 reduce-scatter.27
  1529.8 62.8 reduce-scatter.31
  1602.4 44.0 reduce-scatter.21
  1649.1 44.5 reduce-scatter.25
  1696.3 44.5 reduce-scatter.29
  1744.3 62.8 reduce-scatter.23
  1810.8 62.3 reduce-scatter.27
  1876.6 62.8 reduce-scatter.31
  1949.2 44.0 reduce-scatter.21
  1995.7 44.5 reduce-scatter.25
  2042.9 44.4 reduce-scatter.29
  2090.9 62.8 reduce-scatter.23
  2157.4 62.5 reduce-scatter.27
  2223.3 62.8 reduce-scatter.31
  2295.9 44.0 reduce-scatter.21
  2342.4 44.4 reduce-scatter.25
  2389.6 44.5 reduce-scatter.29
  2437.6 62.7 reduce-scatter.23
  2504.0 62.5 reduce-scatter.27
  2569.8 62.8 reduce-scatter.31
  2642.4 44.0 reduce-scatter.21
  2688.9 44.4 reduce-scatter.25
  2736.1 44.4 reduce-scatter.29
  2784.1 62.8 reduce-scatter.23
  2850.7 62.4 reduce-scatter.27
  2916.5 62.9 reduce-scatter.31
  3068.9 149.5 reduce-scatter.11
  3221.2 69.6 reduce-scatter.17
  3293.3 180.3 reduce-scatter.13
  3482.3 123.4 all-reduce.10
  3609.6 67.9 reduce-scatter.19
  3681.4 118.0 reduce-scatter.15
where the time goes:
time: 3820 us; the launch traced here: 3810 us
  waiting for transfers between devices  3260 us (85%)
  matrix products  310 us (8%)
  local copies, waits for them, and re-layouts  106 us (3%)
  other arithmetic  82.6 us (2%)
    reduce_scatter x6, waiting for transfers between devices, expert_step(): lax.psum_scatter(down_shard.astype(jnp.bfloat16), 'ctx', scatter_dimensio...  388 us
    reduce_scatter x6, waiting for transfers between devices, expert_step(): lax.psum_scatter(up_shard.astype(jnp.bfloat16), 'ctx', scatter_dimension=...  387 us
    reduce_scatter x6, waiting for transfers between devices, expert_step(): lax.psum_scatter(gate_shard.astype(jnp.bfloat16), 'ctx', scatter_dimensio...  349 us
    reduce_scatter x6, waiting for transfers between devices, expert_step(): lax.psum_scatter(down_term.astype(jnp.bfloat16), 'fsdp', scatter_dimensio...  283 us
    reduce_scatter x6, waiting for transfers between devices, expert_step(): lax.psum_scatter(up_term.astype(jnp.bfloat16), 'fsdp', scatter_dimension=...  281 us
    reduce_scatter x6, waiting for transfers between devices, expert_step(): lax.psum_scatter(gate_term.astype(jnp.bfloat16), 'fsdp', scatter_dimensio...  215 us
    reduce_scatter x1, waiting for transfers between devices, on_device(): lax.psum_scatter(qkv_weight_grad.astype(jnp.bfloat16), 'fsdp', scatter_di...  183 us
    all_gather x1, waiting for transfers between devices, on_device(): lax.all_gather(w_gate, 'fsdp', axis=2, tiled=True)  151 us
  transfers between devices with their start and end apart: 49, of which 49 were waited for; matrix products, arithmetic and copies ran while one was open for 8% of the time, Pallas kernels for 0%

commit v1 on v0

--- a/solution.py
+++ b/solution.py
@@ -50,7 +50,7 @@
 
 
 def document_info(positions, lengths):
-    doc_ends = jnp.cumsum(lengths)
+    doc_ends = jnp.sum(jnp.where(jnp.arange(lengths.shape[0])[:, None] >= jnp.arange(lengths.shape[0])[None, :], lengths[None, :], 0), axis=1)
     passed = doc_ends[None, :] <= positions[:, None]
     doc_ids = jnp.sum(passed.astype(jnp.int32), axis=1)
     inner_pos = positions - jnp.sum(jnp.where(passed, lengths[None, :], 0), axis=1)
@@ -463,6 +463,299 @@
     )
 
 
+def rms_unit(values):
+    return lax.rsqrt(jnp.mean(values * values, axis=-1, keepdims=True) + EPSILON)
+
+
+def rope_tables(inner_pos, head_dim):
+    half_dim = head_dim // 2
+    freq_table = ROPE_BASE ** (-2.0 * jnp.arange(half_dim, dtype=jnp.float32) / head_dim)
+    angles = inner_pos.astype(jnp.float32)[:, None] * freq_table[None, :]
+    return (jnp.cos(angles), jnp.sin(angles))
+
+
+def turn(values, cosine, sine_part):
+    half_dim = cosine.shape[-1]
+    cosine, sine_part = cosine[:, None, :], sine_part[:, None, :]
+    first_half, second_half = values[..., :half_dim], values[..., half_dim:]
+    return jnp.concatenate(
+        [
+            first_half * cosine - second_half * sine_part,
+            second_half * cosine + first_half * sine_part,
+        ],
+        axis=-1,
+    )
+
+
+def slot_of_pairs(route_ids, order_ids):
+    pair_count = route_ids.shape[0] * route_ids.shape[1]
+    expert_flat = route_ids.reshape(pair_count)
+    rank_flat = order_ids.reshape(pair_count)
+    earlier = (expert_flat[None, :] == expert_flat[:, None]) & (
+        rank_flat[None, :] < rank_flat[:, None]
+    )
+    return jnp.sum(earlier.astype(jnp.int32), axis=1).reshape(route_ids.shape)
+
+
+def dot32(spec, left, right):
+    return jnp.einsum(spec, left, right, preferred_element_type=jnp.float32)
+
+
+def on_device_heads(
+    tokens,
+    doc_lengths,
+    routes,
+    slot_order,
+    attn_gain,
+    w_qkv,
+    q_gain,
+    k_gain,
+    w_out,
+    ffn_gain,
+    w_router,
+    w_gate,
+    w_up,
+    w_down,
+    cotangent,
+):
+    rows, width = tokens.shape[1], tokens.shape[2]
+    ctx, fsdp = lax.axis_size("ctx"), lax.axis_size("fsdp")
+    me, mine = lax.axis_index("ctx"), lax.axis_index("fsdp")
+    head_dim = width // HEADS
+    heads = HEADS // ctx
+    cols = heads * head_dim
+    part = width // fsdp
+    total = rows * ctx
+    score_scale = head_dim ** (-0.5)
+    lengths = doc_lengths[0]
+    bf16, f32 = jnp.bfloat16, jnp.float32
+
+    tokens_all = lax.all_gather(tokens[0], "ctx", axis=0, tiled=True)
+    small = jnp.concatenate(
+        [jnp.stack([attn_gain, q_gain, k_gain, ffn_gain]), w_router.T], axis=0
+    )
+    small = lax.all_gather(small, "fsdp", axis=1, tiled=True)
+    gain_one, gain_query, gain_key, gain_two = (small[i].astype(f32) for i in range(4))
+    router_weight = small[4:]
+    own_cols = jnp.concatenate(
+        [
+            lax.dynamic_slice_in_dim(w_qkv, kind * width + me * cols, cols, 1)
+            for kind in range(3)
+        ],
+        axis=1,
+    )
+    qkv_weight = lax.all_gather(own_cols, "fsdp", axis=0, tiled=True)
+    dy_all = lax.all_gather(cotangent[0], "fsdp", axis=0, tiled=True)
+    pairs_all = lax.all_gather(jnp.stack([routes[0], slot_order[0]]), "fsdp", axis=0)
+
+    stream_pos = dealt_position(jnp.arange(total, dtype=jnp.int32), rows, ctx)
+    stream_doc, stream_inner = document_info(stream_pos, lengths)
+    cosine, sine_part = rope_tables(stream_inner, head_dim)
+    inputs_all = tokens_all.astype(f32)
+    unit_all = inputs_all * rms_unit(inputs_all)
+    normed_all = (unit_all * gain_one).astype(bf16)
+    projected = dot32("td,de->te", normed_all, qkv_weight)
+    query_lin, key_lin = projected[:, :cols], projected[:, cols : 2 * cols]
+    value_low = projected[:, 2 * cols :].astype(bf16).reshape(total, heads, head_dim)
+    squares = jnp.stack(
+        [jnp.sum(query_lin * query_lin, axis=1), jnp.sum(key_lin * key_lin, axis=1)]
+    )
+    scales = lax.rsqrt(lax.psum(squares, "ctx") / width + EPSILON)
+    own_gain_query = lax.dynamic_slice_in_dim(gain_query, me * cols, cols, 0)
+    own_gain_key = lax.dynamic_slice_in_dim(gain_key, me * cols, cols, 0)
+    query_unit = query_lin * scales[0][:, None]
+    key_unit = key_lin * scales[1][:, None]
+
+    def by_head(values):
+        return values.reshape(total, heads, head_dim)
+
+    query_low = turn(by_head(query_unit * own_gain_query), cosine, sine_part).astype(bf16)
+    key_low = turn(by_head(key_unit * own_gain_key), cosine, sine_part).astype(bf16)
+    scores = masked_scores(
+        query_low, key_low, stream_pos, stream_doc, stream_pos, stream_doc, score_scale
+    )
+    weights = jnp.exp(scores - jnp.max(scores, axis=-1, keepdims=True))
+    probs = weights / jnp.sum(weights, axis=-1, keepdims=True)
+    prob_low = probs.astype(bf16)
+    attended = dot32("hqk,khd->qhd", prob_low, value_low)
+
+    def to_rows(values):
+        values = lax.all_to_all(values, "ctx", 0, 1, tiled=True)
+        return lax.all_to_all(values, "fsdp", 1, 0, tiled=True)
+
+    def to_heads(values):
+        values = lax.all_to_all(values, "fsdp", 0, 1, tiled=True)
+        return lax.all_to_all(values, "ctx", 1, 0, tiled=True)
+
+    attended_part = to_rows(attended.reshape(total, cols).astype(bf16))
+    mixed_part = dot32("td,de->te", attended_part, w_out).astype(bf16)
+    inputs = tokens[0].astype(f32)
+    mixed = inputs + lax.psum_scatter(
+        mixed_part, "fsdp", scatter_dimension=0, tiled=True
+    ).astype(f32)
+    scale_two = rms_unit(mixed)
+    unit_two = mixed * scale_two
+    normed_two = (unit_two * gain_two).astype(bf16)
+    group = lax.all_gather(normed_two, "fsdp", axis=0, tiled=True)
+
+    experts = w_gate.shape[0]
+    top = routes.shape[2]
+    capacity = rows * top // experts
+    slots = jax.vmap(slot_of_pairs)(pairs_all[:, 0], pairs_all[:, 1])
+    expert_ids = jnp.arange(experts, dtype=jnp.int32)
+    chosen = pairs_all[:, 0][:, :, :, None] == expert_ids
+    slot_by_expert = jnp.sum(jnp.where(chosen, slots[..., None] + 1, 0), axis=2) - 1
+    spread = (
+        slot_by_expert.transpose(0, 2, 1)[:, :, None, :]
+        == jnp.arange(capacity, dtype=jnp.int32)[None, None, :, None]
+    )
+    disp = spread.astype(bf16).reshape(fsdp, experts * capacity, rows)
+    logits = dot32("td,ed->te", group, router_weight)
+    router_probs = jax.nn.softmax(logits, axis=-1).reshape(fsdp, rows, experts)
+    slot_gate_value = jnp.sum(
+        jnp.where(spread, router_probs.transpose(0, 2, 1)[:, :, None, :], 0.0), axis=-1
+    )
+    slot_gate_value = slot_gate_value.transpose(1, 0, 2).reshape(experts, fsdp * capacity)
+
+    def dispatch(values):
+        picked = dot32("bst,btd->bsd", disp, values.reshape(fsdp, rows, width)).astype(bf16)
+        picked = picked.reshape(fsdp, experts, capacity, width).transpose(1, 0, 2, 3)
+        return picked.reshape(experts, fsdp * capacity, width)
+
+    def combine(values):
+        values = values.reshape(experts, fsdp, capacity, width).transpose(1, 0, 2, 3)
+        return dot32("bst,bsd->btd", disp, values.reshape(fsdp, experts * capacity, width))
+
+    expert_in = dispatch(group)
+    gate_pre = dot32("ecd,edh->ech", expert_in, w_gate)
+    up_pre = dot32("ecd,edh->ech", expert_in, w_up)
+    hidden = (jax.nn.silu(gate_pre) * up_pre).astype(bf16)
+    expert_out = dot32("ech,ehd->ecd", hidden, w_down) * slot_gate_value[..., None]
+    moved = lax.psum_scatter(
+        combine(expert_out.astype(bf16)).reshape(fsdp * rows, width).astype(bf16),
+        "fsdp",
+        scatter_dimension=0,
+        tiled=True,
+    )
+    activations = (mixed + moved.astype(f32)).astype(bf16)
+
+    slot_dy = dispatch(dy_all)
+    raw_grad = dot32("ecd,ehd->ech", slot_dy, w_down)
+    slot_gate_grad = jnp.sum(hidden.astype(f32) * raw_grad, axis=-1)
+    hidden_grad = raw_grad * slot_gate_value[..., None]
+    gate_low, up_low = silu_parts(hidden_grad, gate_pre, up_pre)
+    in_grad = dot32("ech,edh->ecd", gate_low, w_gate) + dot32("ech,edh->ecd", up_low, w_up)
+    g_gate = dot32("ecd,ech->edh", expert_in, gate_low).astype(bf16)
+    g_up = dot32("ecd,ech->edh", expert_in, up_low).astype(bf16)
+    scaled_hidden = (hidden.astype(f32) * slot_gate_value[..., None]).astype(bf16)
+    g_down = dot32("ech,ecd->ehd", scaled_hidden, slot_dy).astype(bf16)
+    prob_grad = jnp.sum(
+        jnp.where(
+            spread,
+            slot_gate_grad.reshape(experts, fsdp, capacity).transpose(1, 0, 2)[..., None],
+            0.0,
+        ),
+        axis=2,
+    ).transpose(0, 2, 1)
+    logit_grad = (
+        router_probs * (prob_grad - jnp.sum(router_probs * prob_grad, axis=-1, keepdims=True))
+    ).reshape(fsdp * rows, experts).astype(bf16)
+    group_grad = combine(in_grad.astype(bf16)).reshape(fsdp * rows, width) + dot32(
+        "te,ed->td", logit_grad, router_weight
+    )
+    g_router = dot32("te,td->ed", logit_grad, group)
+    normed_two_grad = lax.psum_scatter(
+        group_grad.astype(bf16), "fsdp", scatter_dimension=0, tiled=True
+    ).astype(f32)
+    g_ffn_gain = jnp.sum(normed_two_grad * unit_two, axis=0)
+    pulled = normed_two_grad * gain_two
+    out_grad = cotangent[0].astype(f32)
+    mixed_grad = out_grad + scale_two * (
+        pulled - unit_two * jnp.mean(unit_two * pulled, axis=-1, keepdims=True)
+    )
+    mixed_all = lax.all_gather(mixed_grad.astype(bf16), "fsdp", axis=0, tiled=True)
+    output_part = dot32("te,de->td", mixed_all, w_out).astype(bf16)
+    g_out = dot32("td,te->de", attended_part, mixed_all).astype(bf16)
+    output_grad = by_head(to_heads(output_part))
+
+    row_delta = jnp.sum(output_grad.astype(f32) * attended, axis=-1).T
+    prob_grad_attn = dot32("qhd,khd->hqk", output_grad, value_low)
+    score_grad = (probs * (prob_grad_attn - row_delta[..., None])).astype(bf16)
+    query_grad = dot32("hqk,khd->qhd", score_grad, key_low) * score_scale
+    key_grad = dot32("hqk,qhd->khd", score_grad, query_low) * score_scale
+    value_grad = dot32("hqk,qhd->khd", prob_low, output_grad)
+    query_back = turn(query_grad, cosine, -sine_part).reshape(total, cols)
+    key_back = turn(key_grad, cosine, -sine_part).reshape(total, cols)
+    own_g_query = jnp.sum(query_back * query_unit, axis=0)
+    own_g_key = jnp.sum(key_back * key_unit, axis=0)
+    query_back = query_back * own_gain_query
+    key_back = key_back * own_gain_key
+    inner_sums = lax.psum(
+        jnp.stack(
+            [jnp.sum(query_back * query_unit, axis=1), jnp.sum(key_back * key_unit, axis=1)]
+        ),
+        "ctx",
+    ) / width
+    proj_grad = jnp.concatenate(
+        [
+            scales[0][:, None] * (query_back - query_unit * inner_sums[0][:, None]),
+            scales[1][:, None] * (key_back - key_unit * inner_sums[1][:, None]),
+            value_grad.reshape(total, cols),
+        ],
+        axis=1,
+    ).astype(bf16)
+    g_qkv = dot32("td,te->de", normed_all, proj_grad).astype(bf16)
+    normed_grad_part = dot32("te,de->td", proj_grad, qkv_weight)
+    g_attn_gain = jnp.sum(normed_grad_part * unit_all, axis=0)
+    normed_grad = lax.psum_scatter(
+        normed_grad_part.astype(bf16), "ctx", scatter_dimension=0, tiled=True
+    ).astype(f32)
+    scale_one = rms_unit(inputs)
+    unit_one = inputs * scale_one
+    pulled_one = normed_grad * gain_one
+    input_grad = mixed_grad + scale_one * (
+        pulled_one - unit_one * jnp.mean(unit_one * pulled_one, axis=-1, keepdims=True)
+    )
+
+    gate_parts = lax.psum_scatter(g_gate, "ctx", scatter_dimension=1, tiled=True).astype(f32)
+    up_parts = lax.psum_scatter(g_up, "ctx", scatter_dimension=1, tiled=True).astype(f32)
+    down_parts = lax.psum_scatter(g_down, "ctx", scatter_dimension=2, tiled=True).astype(f32)
+    out_part = lax.psum_scatter(g_out, "ctx", scatter_dimension=1, tiled=True).astype(f32)
+    qkv_shard = lax.psum_scatter(g_qkv, "fsdp", scatter_dimension=0, tiled=True)
+    qkv_full = lax.all_gather(qkv_shard, "ctx", axis=0)
+    qkv_full = qkv_full.reshape(ctx, part, 3, cols).transpose(1, 2, 0, 3).reshape(part, 3 * width)
+    qkv_part = lax.dynamic_slice_in_dim(
+        qkv_full, me * (3 * width // ctx), 3 * width // ctx, 1
+    ).astype(f32)
+
+    def placed_cols(values):
+        return lax.dynamic_update_slice_in_dim(jnp.zeros((width,), f32), values, me * cols, 0)
+
+    sums = jnp.concatenate(
+        [
+            jnp.stack([g_attn_gain, placed_cols(own_g_query), placed_cols(own_g_key), g_ffn_gain]),
+            g_router,
+        ],
+        axis=0,
+    )
+    sums = lax.psum(sums, ("ctx", "fsdp"))
+    sums = lax.dynamic_slice_in_dim(sums, mine * part, part, 1)
+    return (
+        activations[None],
+        input_grad[None],
+        sums[0],
+        qkv_part,
+        sums[1],
+        sums[2],
+        out_part,
+        sums[3],
+        sums[4:].T,
+        gate_parts,
+        up_parts,
+        down_parts,
+    )
+
+
 def solution(mesh):
     in_specs = (
         P("fsdp", "ctx", None),
@@ -495,6 +788,7 @@
         P(None, "ctx", "fsdp"),
         P(None, "fsdp", "ctx"),
     )
+    body = on_device_heads if HEADS % mesh.shape["ctx"] == 0 else on_device
     return jax.shard_map(
-        on_device, mesh=mesh, in_specs=in_specs, out_specs=out_specs, check_vma=False
-    )
+        body, mesh=mesh, in_specs=in_specs, out_specs=out_specs, check_vma=False
+    )

time: 3820 us -> 1360 us (0.36)
  waiting for transfers between devices: 3260 us -> 966 us
  matrix products: 310 us -> 147 us
  blocking collectives: 26.7 us -> 105 us
  local copies, waits for them, and re-layouts: 106 us -> 58.8 us
    reduce_scatter x41 -> x9, waiting for transfers between devices: 2410 us -> 607 us  [the longest x1 121 us: on_device_heads(): lax.psum_scatter(g_down, 'ctx', scatter_dimension=2, tiled=True).astype(f32)]
    all_gather x7 -> x6, waiting for transfers between devices: 714 us -> 241 us  [the longest x1 98.6 us: on_device_heads(): qkv_full = lax.all_gather(qkv_shard, 'ctx', axis=0)]
    dot_general x62 -> x27, matrix products: 310 us -> 138 us  [dot32(): return jnp.einsum(spec, left, right, preferred_element_type=jnp.float32)]
    all_to_all x0 -> x4, blocking collectives: none -> 58.5 us  [the longest x1 19.3 us: to_heads(): return lax.all_to_all(values, 'ctx', 1, 0, tiled=True)]
  transfers between devices with their start and end apart: 49 -> 16, of which waited for: 49 -> 15; matrix products, arithmetic and copies ran while one was open for 8% -> 6% of each run, Pallas kernels for 0% -> 0%
where the time goes in v1:
time: 1360 us; the launch traced here: 1350 us
  waiting for transfers between devices  966 us (71%)
  matrix products  147 us (11%)
  blocking collectives  105 us (8%)
  local copies, waits for them, and re-layouts  58.8 us (4%)
  other arithmetic  57.6 us (4%)
  between operations  15.2 us (1%)
    dot_general x27, matrix products, dot32(): return jnp.einsum(spec, left, right, preferred_element_type=jnp.float32)  138 us
    reduce_scatter x1, waiting for transfers between devices, on_device_heads(): lax.psum_scatter(g_down, 'ctx', scatter_dimension=2, tiled=True).astype(f32)  121 us
    reduce_scatter x1, waiting for transfers between devices, on_device_heads(): lax.psum_scatter(g_gate, 'ctx', scatter_dimension=1, tiled=True).astype(f32)  119 us
    reduce_scatter x1, waiting for transfers between devices, on_device_heads(): lax.psum_scatter(g_up, 'ctx', scatter_dimension=1, tiled=True).astype(f32)  119 us
    psum x1, waiting for transfers between devices, on_device_heads(): sums = lax.psum(sums, ('ctx', 'fsdp'))  116 us
    all_gather x1, waiting for transfers between devices, on_device_heads(): qkv_full = lax.all_gather(qkv_shard, 'ctx', axis=0)  98.6 us
    reduce_scatter x1, waiting for transfers between devices, on_device_heads(): lax.psum_scatter(normed_grad_part.astype(bf16), 'ctx', scatter_dimension=...  89.4 us
    reduce_scatter x1, waiting for transfers between devices, on_device_heads(): lax.psum_scatter(g_out, 'ctx', scatter_dimension=1, tiled=True).astype(f32)  67.1 us
  transfers between devices with their start and end apart: 16, of which 15 were waited for; matrix products, arithmetic and copies ran while one was open for 6% of the time, Pallas kernels for 0%

profile of v1, /device:TPU:5, one launch (start us, length us, event | category | flops | bytes accessed | tf_op | source)
XLA Modules:
  0.0 1351.2 jit_solution(8376949881958865182)
XLA Ops:
  10.5 5.7 all_gather.31
  16.5 3.1 fusion.50
  21.6 62.1 %all-gather.17.cloned.1.call-done = bf16[1,1024,2048]{2,1,0:T(8,128)(2,1)} async-done(((bf16[1,128,2048]{2,1,0:T(8,128)(2,1)}), bf16[1,1024,2048]{2,1,0:T(8,128)(2,1)}) %all-gather.17.cloned.1.call-update) | async-done | bytes 4194320 | tf_op jit(solution)/shard_map/all_gather | solution.py:533
  83.7 3.1 fusion.6
  86.8 26.3 %all-gather.11.cloned.1.call-done = bf16[2048,768]{1,0:T(8,128)(2,1)} async-done(((bf16[512,768]{1,0:T(8,128)(2,1)}), bf16[2048,768]{1,0:T(8,128)(2,1)}) %all-gather.11.cloned.1.call-update) | async-done | bytes 3145744 | tf_op jit(solution)/shard_map/all_gather | solution.py:547
  113.1 6.6 fusion.22
  122.3 18.6 %psum.21 = f32[2,1024]{1,0:T(2,128)S(1)} all-reduce(f32[2,1024]{1,0:T(2,128)S(1)} %pad_maximum_fusion.8), channel_id=1, replica_groups=mesh['ctx'=8,'fsdp'=4] {'ctx'}, use_global_device_ids=true, to_apply=%region_5.6 | all-reduce | flops 2048 | bytes 16384 | tf_op jit(solution)/shard_map/psum | solution.py:563
  144.6 2.4 copy.315
  149.3 2.4 copy.314
  153.0 3.8 subtract_convert_fusion.1
  156.8 8.7 fusion.100
  165.6 4.7 fusion.12
  172.7 12.6 all_to_all.64
  185.4 15.7 %all_to_all.65 = bf16[128,4,512]{0,2,1:T(8,128)(2,1)S(1)} all-to-all(bf16[128,4,512]{0,2,1:T(8,128)(2,1)S(1)} %bitcast.265), channel_id=1, replica_groups=mesh['ctx'=8,'fsdp'=4] {'fsdp'}, dimensions={1} | all-to-all | bytes 1048576 | tf_op jit(solution)/shard_map/all_to_all | solution.py:584
  201.3 2.6 convolution_convert_fusion.8
  204.5 29.1 %reduce-scatter.10.cloned.1.call-done = bf16[128,2048]{1,0:T(8,128)(2,1)} async-done(((bf16[512,2048]{1,0:T(8,128)(2,1)}), bf16[128,2048]{1,0:T(8,128)(2,1)}) %reduce-scatter.10.cloned.1.call-update) | async-done | bytes 524304 | tf_op jit(solution)/shard_map/reduce_scatter | solution.py:593
  237.2 5.5 all-gather.1
  245.1 12.8 all-gather.19.cloned.1.call-done
  258.0 3.4 convolution_convert_fusion
  261.3 3.2 copy.263
  264.5 18.2 %all-gather.13.cloned.1.call-done = bf16[512,2048]{1,0:T(8,128)(2,1)} async-done(((bf16[128,2048]{1,0:T(8,128)(2,1)}), bf16[512,2048]{1,0:T(8,128)(2,1)}) %all-gather.13.cloned.1.call-update) | async-done | bytes 2097168 | tf_op jit(solution)/shard_map/all_gather | solution.py:599
  285.0 3.4 convolution_convert_fusion.1
  289.2 7.4 fusion.104
  296.6 6.8 fusion.103
  303.5 8.8 fusion.13
  313.0 3.1 multiply_convert_fusion.2
  316.1 9.8 fusion.105
  325.9 10.9 add_convert_fusion
  336.8 3.4 copy.266
  340.2 3.4 fusion.106
  343.5 4.3 fusion.8
  347.9 31.3 %reduce-scatter.14.cloned.1.call-done = bf16[128,2048]{1,0:T(8,128)(2,1)} async-done(((bf16[512,2048]{1,0:T(8,128)(2,1)}), bf16[128,2048]{1,0:T(8,128)(2,1)}) %reduce-scatter.14.cloned.1.call-update) | async-done | bytes 524304 | tf_op jit(solution)/shard_map/reduce_scatter | solution.py:667
  380.8 2.4 fusion.93
  383.3 22.9 %all-gather.15.cloned.1.call-done = bf16[512,2048]{1,0:T(8,128)(2,1)} async-done(((bf16[128,2048]{1,0:T(8,128)(2,1)}), bf16[512,2048]{1,0:T(8,128)(2,1)}) %all-gather.15.cloned.1.call-update) | async-done | bytes 2097168 | tf_op jit(solution)/shard_map/all_gather | solution.py:676
  406.3 3.7 convolution_convert_fusion.10
  411.2 11.0 all_to_all.66
  422.2 19.3 %all_to_all.67 = bf16[128,8,256]{0,2,1:T(8,128)(2,1)S(1)} all-to-all(bf16[128,8,256]{0,2,1:T(8,128)(2,1)S(1)} %bitcast.267), channel_id=1, replica_groups=mesh['ctx'=8,'fsdp'=4] {'ctx'}, dimensions={1} | all-to-all | bytes 1048576 | tf_op jit(solution)/shard_map/all_to_all | solution.py:588
  442.1 4.6 convolution_convert_fusion.9
  446.8 4.8 multiply_convert_fusion.1
  460.0 2.5 pad_maximum_fusion.2
  466.3 16.7 %psum.22 = f32[2,1024]{1,0:T(2,128)S(1)} all-reduce(f32[2,1024]{1,0:T(2,128)S(1)} %pad_maximum_fusion.9), channel_id=1, replica_groups=mesh['ctx'=8,'fsdp'=4] {'ctx'}, use_global_device_ids=true, to_apply=%region_26.27 | all-reduce | flops 2048 | bytes 16384 | tf_op jit(solution)/shard_map/psum | solution.py:693
  486.3 5.6 convolution_convert_fusion.5
  492.6 10.3 fusion.5
  505.2 4.2 convolution_convert_fusion.6
  509.4 7.4 convolution_convert_fusion.2
  518.0 7.6 convolution_convert_fusion.3
  526.8 7.6 convolution_convert_fusion.4
  535.0 4.7 multiply_convert_fusion
  540.8 2.6 convolution_convert_fusion.7
  544.1 116.1 %all-reduce.2.cloned.1.call-done = f32[10,2048]{1,0:T(8,128)} async-done(((f32[10,2048]{1,0:T(8,128)}), f32[10,2048]{1,0:T(8,128)}) %all-reduce.2.cloned.1.call-update) | async-done | bytes 81936 | tf_op jit(solution)/shard_map/psum | solution.py:741
  663.2 67.1 %reduce-scatter.20.cloned.1.call-done = bf16[512,256]{1,0:T(8,128)(2,1)} async-done(((bf16[512,2048]{1,0:T(8,128)(2,1)}), bf16[512,256]{1,0:T(8,128)(2,1)}) %reduce-scatter.20.cloned.1.call-update) | async-done | bytes 262160 | tf_op jit(solution)/shard_map/reduce_scatter | solution.py:723
  732.1 120.7 %reduce-scatter.26.cloned.1.call-done = bf16[6,256,256]{2,1,0:T(8,128)(2,1)} async-done(((bf16[6,256,2048]{2,1,0:T(8,128)(2,1)}), bf16[6,256,256]{2,1,0:T(8,128)(2,1)}) %reduce-scatter.26.cloned.1.call-update) | async-done | bytes 786448 | tf_op jit(solution)/shard_map/reduce_scatter | solution.py:722
  852.8 2.4 convert_element_type.208
  855.2 119.0 %reduce-scatter.24.cloned.1.call-done = bf16[6,256,256]{2,1,0:T(8,128)(2,1)} async-done(((bf16[6,2048,256]{2,1,0:T(8,128)(2,1)}), bf16[6,256,256]{2,1,0:T(8,128)(2,1)}) %reduce-scatter.24.cloned.1.call-update) | async-done | bytes 786448 | tf_op jit(solution)/shard_map/reduce_scatter | solution.py:721
  974.2 2.4 convert_element_type.205
  976.6 119.1 %reduce-scatter.22.cloned.1.call-done = bf16[6,256,256]{2,1,0:T(8,128)(2,1)} async-done(((bf16[6,2048,256]{2,1,0:T(8,128)(2,1)}), bf16[6,256,256]{2,1,0:T(8,128)(2,1)}) %reduce-scatter.22.cloned.1.call-update) | async-done | bytes 786448 | tf_op jit(solution)/shard_map/reduce_scatter | solution.py:720
  1095.8 2.4 convert_element_type.203
  1098.2 89.4 %reduce-scatter.16.cloned.1.call-done = bf16[128,2048]{1,0:T(8,128)(2,1)} async-done(((bf16[1024,2048]{1,0:T(8,128)(2,1)}), bf16[128,2048]{1,0:T(8,128)(2,1)}) %reduce-scatter.16.cloned.1.call-update) | async-done | bytes 524304 | tf_op jit(solution)/shard_map/reduce_scatter | solution.py:710
  1189.0 31.2 %reduce-scatter.12.cloned.1.call-done = bf16[128,2048]{1,0:T(8,128)(2,1)} async-done(((bf16[512,2048]{1,0:T(8,128)(2,1)}), bf16[128,2048]{1,0:T(8,128)(2,1)}) %reduce-scatter.12.cloned.1.call-update) | async-done | bytes 524304 | tf_op jit(solution)/shard_map/reduce_scatter | solution.py:634
  1220.2 3.2 fusion.32
  1223.3 98.6 %all-gather.21.cloned.1.call-done = bf16[4096,768]{1,0:T(8,128)(2,1)} async-done(((bf16[512,768]{1,0:T(8,128)(2,1)}), bf16[4096,768]{1,0:T(8,128)(2,1)}) %all-gather.21.cloned.1.call-update) | async-done | bytes 6291472 | tf_op jit(solution)/shard_map/all_gather | solution.py:725
  1322.0 8.7 copy.285
  1330.7 7.0 copy.321
  1341.4 3.0 copy.291
  (220 shorter events, 64.7 us)
Async XLA Ops:
  7.2 194.1 %copy-start = (bf16[512,2048]{1,0:T(8,128)(2,1)S(1)}, bf16[512,2048]{1,0:T(8,128)(2,1)}, u32[]{:S(2)}) copy-start(bf16[512,2048]{1,0:T(8,128)(2,1)} %param.23) | copy-start | bytes 6291460
  7.2 3.0 copy-start.41
  7.2 3.0 copy-start.42
  7.2 3.1 copy-start.43
  7.2 3.1 copy-start.44
  7.2 3.1 copy-start.36
  7.2 9.0 copy-start.45
  7.3 76.4 %all-gather.17.cloned.1.call-start = ((), (), s32[]{:S(2)}) async-start(), calls=%async_computation.26 | async-start | bytes 4718592 | tf_op jit(solution)/shard_map/all_gather | solution.py:533
  8.0 105.1 %all-gather.11.cloned.1.call-start = ((), (), s32[]{:S(2)}) async-start(), calls=%async_computation.13 | async-start | bytes 3932160 | tf_op jit(solution)/shard_map/all_gather | solution.py:547
  10.2 223.4 %reduce-scatter.10.cloned.1.call-start = ((), (), s32[]{:S(2)}) async-start(), calls=%async_computation.14 | async-start | bytes 2621440 | tf_op jit(solution)/shard_map/reduce_scatter | solution.py:593
  19.6 133.4 %copy-start.16 = (f32[1024,64]{1,0:T(8,128)}, f32[1024,64]{1,0:T(8,128)S(1)}, u32[]{:S(2)}) copy-start(f32[1024,64]{1,0:T(8,128)S(1)} %get-tuple-element.122) | copy-start | bytes 786436
  119.7 1.7 copy-start.5
  156.8 8.7 copy-start.23
  165.6 4.7 copy-start.37
  165.6 4.7 copy-start.29
  170.3 2.4 copy-start.3
  201.2 2.6 copy-start.34
  201.2 32.4 %copy-start.4 = (bf16[1,128,2048]{2,1,0:T(8,128)(2,1)S(1)}, bf16[1,128,2048]{2,1,0:T(8,128)(2,1)}, u32[]{:S(2)}) copy-start(bf16[1,128,2048]{2,1,0:T(8,128)(2,1)} %param.15) | copy-start | bytes 1572868
  203.8 33.2 %copy-start.39 = (s32[1,128,3]{1,0,2:T(1,128)S(1)}, s32[1,128,3]{1,0,2:T(1,128)}, u32[]{:S(2)}) copy-start(s32[1,128,3]{1,0,2:T(1,128)} %param.17) | copy-start | bytes 4612
  203.8 33.2 %copy-start.40 = (s32[1,128,3]{1,0,2:T(1,128)S(1)}, s32[1,128,3]{1,0,2:T(1,128)}, u32[]{:S(2)}) copy-start(s32[1,128,3]{1,0,2:T(1,128)} %param.18) | copy-start | bytes 4612
  203.9 54.1 %all-gather.19.cloned.1.call-start = ((), (), s32[]{:S(2)}) async-start(), calls=%async_computation.27 | async-start | bytes 2621440 | tf_op jit(solution)/shard_map/all_gather | solution.py:548
  204.4 78.2 %all-gather.13.cloned.1.call-start = ((), (), s32[]{:S(2)}) async-start(), calls=%async_computation.15 | async-start | bytes 2621440 | tf_op jit(solution)/shard_map/all_gather | solution.py:599
  237.0 142.2 %reduce-scatter.14.cloned.1.call-start = ((), (), s32[]{:S(2)}) async-start(), calls=%async_computation.17 | async-start | bytes 2621440 | tf_op jit(solution)/shard_map/reduce_scatter | solution.py:667
  245.1 39.9 %copy-start.14 = (pred[4,384,128]{2,1,0:T(32,128)(4,1)}, pred[4,384,128]{2,1,0:T(32,128)(4,1)S(1)}, u32[]{:S(2)}) copy-start(pred[4,384,128]{2,1,0:T(32,128)(4,1)S(1)} %bitcast_compare_fusion) | copy-start | bytes 589828
  289.2 7.4 copy-start.2
  296.6 6.8 copy-start.13
  316.1 9.8 copy-start.8
  316.1 9.8 copy-start.11
  336.7 3.4 copy-start.15
  343.5 35.7 %copy-start.7 = (bf16[128,2048]{1,0:T(8,128)(2,1)S(1)}, bf16[128,2048]{1,0:T(8,128)(2,1)}, u32[]{:S(2)}) copy-start(bf16[128,2048]{1,0:T(8,128)(2,1)} %reduce-scatter.10.cloned.1.call-done) | copy-start | bytes 1572868
  347.9 58.4 %all-gather.15.cloned.1.call-start = ((), (), s32[]{:S(2)}) async-start(), calls=%async_computation.18 | async-start | bytes 2621440 | tf_op jit(solution)/shard_map/all_gather | solution.py:676
  383.3 160.5 %reduce-scatter.18.cloned.1.call-start = ((), (), s32[]{:S(2)}) async-start(), calls=%async_computation.21 | async-start | bytes 3932160 | tf_op jit(solution)/shard_map/reduce_scatter | solution.py:724
  422.2 24.5 %copy-start.22 = (f32[1024,2,128]{0,2,1:T(8,128)S(1)}, f32[1024,2,128]{0,2,1:T(8,128)}, u32[]{:S(2)}) copy-start(f32[1024,2,128]{0,2,1:T(8,128)} %get-tuple-element.126) | copy-start | bytes 3145732
  441.8 5.0 copy-start.38
  442.1 4.7 copy-start.30
  446.8 4.9 copy-start.26
  446.8 4.9 copy-start.27
  451.7 1.4 copy-start.24
  451.7 1.4 copy-start.25
  453.1 2.0 copy-start.17
  453.1 2.0 copy-start.28
  457.1 2.9 copy-start.20
  483.0 3.3 copy-start.21
  483.0 3.3 copy-start.31
  485.3 0.8 copy-start.32
  485.3 1.0 copy-start.33
  486.3 5.8 copy-start.6
  491.9 168.4 %all-reduce.2.cloned.1.call-start = ((), (), s32[]{:S(2)}) async-start(), calls=%async_computation.20 | async-start | bytes 262144 | tf_op jit(solution)/shard_map/psum | solution.py:741
  492.6 12.6 copy-start.35
  502.9 6.6 copy-start.10
  505.1 225.2 %reduce-scatter.20.cloned.1.call-start = ((), (), s32[]{:S(2)}) async-start(), calls=%async_computation.22 | async-start | bytes 2359296 | tf_op jit(solution)/shard_map/reduce_scatter | solution.py:723
  509.4 343.4 %reduce-scatter.26.cloned.1.call-start = ((), (), s32[]{:S(2)}) async-start(), calls=%async_computation.25 | async-start | bytes 7077888 | tf_op jit(solution)/shard_map/reduce_scatter | solution.py:722
  516.9 1.2 copy-start.12
  516.9 457.3 %reduce-scatter.24.cloned.1.call-start = ((), (), s32[]{:S(2)}) async-start(), calls=%async_computation.24 | async-start | bytes 7077888 | tf_op jit(solution)/shard_map/reduce_scatter | solution.py:721
  525.6 1.2 copy-start.9
  525.6 570.2 %reduce-scatter.22.cloned.1.call-start = ((), (), s32[]{:S(2)}) async-start(), calls=%async_computation.23 | async-start | bytes 7077888 | tf_op jit(solution)/shard_map/reduce_scatter | solution.py:720
  534.4 653.2 %reduce-scatter.16.cloned.1.call-start = ((), (), s32[]{:S(2)}) async-start(), calls=%async_computation.19 | async-start | bytes 4718592 | tf_op jit(solution)/shard_map/reduce_scatter | solution.py:710
  535.0 685.2 %reduce-scatter.12.cloned.1.call-start = ((), (), s32[]{:S(2)}) async-start(), calls=%async_computation.16 | async-start | bytes 2621440 | tf_op jit(solution)/shard_map/reduce_scatter | solution.py:634
  543.5 778.5 %all-gather.21.cloned.1.call-start = ((), (), s32[]{:S(2)}) async-start(), calls=%async_computation.28 | async-start | bytes 7077888 | tf_op jit(solution)/shard_map/all_gather | solution.py:725
  732.1 488.1 %copy-start.18 = (bf16[128,2048]{1,0:T(8,128)(2,1)S(1)}, bf16[128,2048]{1,0:T(8,128)(2,1)}, u32[]{:S(2)}) copy-start(bf16[128,2048]{1,0:T(8,128)(2,1)} %reduce-scatter.14.cloned.1.call-done) | copy-start | bytes 1572868
  732.1 488.1 %copy-start.19 = (bf16[1,128,2048]{2,1,0:T(8,128)(2,1)S(1)}, bf16[1,128,2048]{2,1,0:T(8,128)(2,1)}, u32[]{:S(2)}) copy-start(bf16[1,128,2048]{2,1,0:T(8,128)(2,1)} %param.29) | copy-start | bytes 1572868
  1337.6 6.7 copy-start.1
Sparse Core Ops, SparseCore 0:
  10.2 73.4 all-gather.16
  85.8 27.2 all-gather.10
  204.0 29.5 reduce-scatter.9
  235.1 22.8 all-gather.18
  260.0 22.5 all-gather.12
  348.0 31.1 reduce-scatter.13
  383.4 22.8 all-gather.14
  492.0 38.3 reduce-scatter.17
  537.5 122.7 all-reduce.1
  664.0 66.2 reduce-scatter.19
  734.3 118.4 reduce-scatter.25
  856.7 117.4 reduce-scatter.23
  978.3 117.4 reduce-scatter.21
  1099.7 87.8 reduce-scatter.15
  1190.0 30.1 reduce-scatter.11
  1222.4 99.4 all-gather.20

commit v2 on v1

--- a/solution.py
+++ b/solution.py
@@ -3,10 +3,15 @@
 import jax
 import jax.numpy as jnp
 from jax import lax
+from jax.experimental import pallas as pl
+from jax.experimental.pallas import tpu as pltpu
 from jax.sharding import PartitionSpec as P
 
 HEADS = 16
-
+MESH = pl.DeviceIdType.MESH
+ANY = pl.BlockSpec(memory_space=pl.ANY)
+VMEM = pl.BlockSpec(memory_space=pltpu.VMEM)
+DMA = pltpu.SemaphoreType.DMA
 
 EPSILON = 1e-05
 ROPE_BASE = 10000.0
@@ -501,6 +506,363 @@
     return jnp.einsum(spec, left, right, preferred_element_type=jnp.float32)
 
 
+def greet(peers):
+    barrier = pltpu.get_barrier_semaphore()
+    for peer in peers:
+        pl.semaphore_signal(barrier, inc=1, device_id=peer, device_id_type=MESH)
+    pl.semaphore_wait(barrier, len(peers))
+
+
+def send(source, target, send_sem, recv_sem, peer):
+    copy = pltpu.make_async_remote_copy(
+        source, target, send_sem, recv_sem, device_id=peer, device_id_type=MESH
+    )
+    copy.start()
+    return copy
+
+
+def comm_call(kernel, name, collective_id, out_shape, in_specs, out_specs, scratch_shapes, cost):
+    return pl.pallas_call(
+        kernel,
+        out_shape=out_shape,
+        in_specs=in_specs,
+        out_specs=out_specs,
+        scratch_shapes=scratch_shapes,
+        compiler_params=pltpu.CompilerParams(
+            collective_id=collective_id, has_side_effects=True, vmem_limit_bytes=48 * 2**20
+        ),
+        cost_estimate=pl.CostEstimate(flops=0, bytes_accessed=cost, transcendentals=0),
+        name=name,
+    )
+
+
+def ctx_sum(values, collective_id):
+    ctx = lax.axis_size("ctx")
+
+    def kernel(own_ref, out_ref, held, send_sems, recv_sems):
+        me, mine = lax.axis_index("ctx"), lax.axis_index("fsdp")
+        peers = [(lax.rem(me + step, ctx), mine) for step in range(1, ctx)]
+        greet(peers)
+        copies = [
+            send(own_ref, held.at[i], send_sems.at[i], recv_sems.at[i], peer)
+            for i, peer in enumerate(peers)
+        ]
+        total = own_ref[...]
+        for i, copy in enumerate(copies):
+            copy.wait_recv()
+            total = total + held[i]
+        out_ref[...] = total
+        for copy in copies:
+            copy.wait_send()
+
+    return comm_call(
+        kernel,
+        "ctx_sum",
+        collective_id,
+        jax.ShapeDtypeStruct(values.shape, values.dtype),
+        [VMEM],
+        VMEM,
+        [
+            pltpu.VMEM((ctx - 1,) + values.shape, values.dtype),
+            DMA((ctx - 1,)),
+            DMA((ctx - 1,)),
+        ],
+        20 * 2**20,
+    )(values)
+
+
+def mesh_sum(values, collective_id):
+    ctx, fsdp = lax.axis_size("ctx"), lax.axis_size("fsdp")
+    rows, part = values.shape[0], values.shape[1] // fsdp
+
+    def kernel(own_ref, out_ref, parts, sums, held, part_send, part_recv, send_sems, recv_sems):
+        me, mine = lax.axis_index("ctx"), lax.axis_index("fsdp")
+        near = [lax.rem(mine + step, fsdp) for step in range(1, fsdp)]
+        peers = [(lax.rem(me + step, ctx), mine) for step in range(1, ctx)]
+        greet([(me, other) for other in near] + peers)
+
+        def columns(index):
+            return pl.ds(pl.multiple_of(index * part, part), part)
+
+        copies = [
+            send(
+                own_ref.at[:, columns(other)],
+                parts.at[i],
+                part_send.at[i],
+                part_recv.at[i],
+                (me, other),
+            )
+            for i, other in enumerate(near)
+        ]
+        total = own_ref[:, columns(mine)]
+        for i, copy in enumerate(copies):
+            copy.wait_recv()
+            total = total + parts[i]
+        sums[...] = total
+        wide = [
+            send(sums, held.at[i], send_sems.at[i], recv_sems.at[i], peer)
+            for i, peer in enumerate(peers)
+        ]
+        for i, copy in enumerate(wide):
+            copy.wait_recv()
+            total = total + held[i]
+        out_ref[...] = total
+        for copy in copies + wide:
+            copy.wait_send()
+
+    return comm_call(
+        kernel,
+        "mesh_sum",
+        collective_id,
+        jax.ShapeDtypeStruct((rows, part), values.dtype),
+        [VMEM],
+        VMEM,
+        [
+            pltpu.VMEM((fsdp - 1, rows, part), values.dtype),
+            pltpu.VMEM((rows, part), values.dtype),
+            pltpu.VMEM((ctx - 1, rows, part), values.dtype),
+            DMA((fsdp - 1,)),
+            DMA((fsdp - 1,)),
+            DMA((ctx - 1,)),
+            DMA((ctx - 1,)),
+        ],
+        30 * 2**20,
+    )(values)
+
+
+def heads_to_rows(values, collective_id):
+    ctx, fsdp = lax.axis_size("ctx"), lax.axis_size("fsdp")
+    rows, cols = values.shape[0] // ctx, values.shape[1]
+    share = ctx // fsdp
+
+    def kernel(own_ref, out_ref, send_sems, recv_sems):
+        me, mine = lax.axis_index("ctx"), lax.axis_index("fsdp")
+        keeper, place = me // share, lax.rem(me, share)
+        own_keeper = (keeper == mine).astype(jnp.int32)
+        barrier = pltpu.get_barrier_semaphore()
+        for step in range(share * fsdp):
+            source, stream = mine * share + step // fsdp, step % fsdp
+
+            @pl.when(jnp.logical_or(source != me, stream != mine))
+            def _():
+                pl.semaphore_signal(
+                    barrier, inc=1, device_id=(source, stream), device_id_type=MESH
+                )
+
+        pl.semaphore_wait(barrier, ctx - own_keeper)
+
+        def block(index):
+            return own_ref.at[pl.ds(pl.multiple_of(index * rows, rows), rows), :]
+
+        def landing(stream, position):
+            return out_ref.at[
+                pl.ds(pl.multiple_of(stream * rows, rows), rows),
+                pl.ds(pl.multiple_of(position * cols, cols), cols),
+            ]
+
+        slot = place * fsdp + mine
+
+        def copy_to(step):
+            other = lax.rem(me + step, ctx)
+            return pltpu.make_async_remote_copy(
+                block(other),
+                landing(mine, place),
+                send_sems.at[step],
+                recv_sems.at[slot],
+                device_id=(other, keeper),
+                device_id_type=MESH,
+            )
+
+        kept = pltpu.make_async_copy(block(me), landing(mine, place), send_sems.at[0])
+        for step in range(1, ctx):
+            copy_to(step).start()
+
+        @pl.when(own_keeper == 0)
+        def _():
+            copy_to(0).start()
+
+        @pl.when(own_keeper == 1)
+        def _():
+            kept.start()
+            kept.wait()
+
+        for step in range(share * fsdp):
+
+            @pl.when(
+                jnp.logical_or(mine * share + step // fsdp != me, step % fsdp != mine)
+            )
+            def _():
+                pltpu.make_async_copy(
+                    block(0), landing(step % fsdp, step // fsdp), recv_sems.at[step]
+                ).wait()
+
+        for step in range(1, ctx):
+            copy_to(step).wait_send()
+
+        @pl.when(own_keeper == 0)
+        def _():
+            copy_to(0).wait_send()
+
+    return comm_call(
+        kernel,
+        "heads_to_rows",
+        collective_id,
+        jax.ShapeDtypeStruct((fsdp * rows, share * cols), values.dtype),
+        [ANY],
+        ANY,
+        [DMA((ctx,)), DMA((share * fsdp,))],
+        40 * 2**20,
+    )(values)
+
+
+def rows_to_heads(values, collective_id):
+    ctx, fsdp = lax.axis_size("ctx"), lax.axis_size("fsdp")
+    share = ctx // fsdp
+    rows, cols = values.shape[0] // fsdp, values.shape[1] // share
+
+    def kernel(own_ref, out_ref, send_sems, recv_sems):
+        me, mine = lax.axis_index("ctx"), lax.axis_index("fsdp")
+        keeper, place = me // share, lax.rem(me, share)
+        own_keeper = (keeper == mine).astype(jnp.int32)
+        barrier = pltpu.get_barrier_semaphore()
+        for step in range(ctx):
+            source = lax.rem(me + step, ctx)
+
+            @pl.when(jnp.logical_or(source != me, keeper != mine))
+            def _():
+                pl.semaphore_signal(
+                    barrier, inc=1, device_id=(source, keeper), device_id_type=MESH
+                )
+
+        pl.semaphore_wait(barrier, share * fsdp - own_keeper)
+
+        def block(stream, position):
+            return own_ref.at[
+                pl.ds(pl.multiple_of(stream * rows, rows), rows),
+                pl.ds(pl.multiple_of(position * cols, cols), cols),
+            ]
+
+        def landing(index):
+            return out_ref.at[pl.ds(pl.multiple_of(index * rows, rows), rows), :]
+
+        def copy_to(step):
+            return pltpu.make_async_remote_copy(
+                block(step % fsdp, step // fsdp),
+                landing(me),
+                send_sems.at[step],
+                recv_sems.at[me],
+                device_id=(mine * share + step // fsdp, step % fsdp),
+                device_id_type=MESH,
+            )
+
+        def is_far(step):
+            return jnp.logical_or(mine * share + step // fsdp != me, step % fsdp != mine)
+
+        for step in range(share * fsdp):
+            pl.when(is_far(step))(copy_to(step).start)
+
+        @pl.when(own_keeper == 1)
+        def _():
+            kept = pltpu.make_async_copy(block(mine, place), landing(me), recv_sems.at[me])
+            kept.start()
+            kept.wait()
+
+        for step in range(ctx):
+            source = lax.rem(me + step, ctx)
+
+            @pl.when(jnp.logical_or(source != me, keeper != mine))
+            def _():
+                pltpu.make_async_copy(block(0, 0), landing(source), recv_sems.at[source]).wait()
+
+        for step in range(share * fsdp):
+            pl.when(is_far(step))(copy_to(step).wait_send)
+
+    return comm_call(
+        kernel,
+        "rows_to_heads",
+        collective_id,
+        jax.ShapeDtypeStruct((ctx * rows, cols), values.dtype),
+        [ANY],
+        ANY,
+        [DMA((share * fsdp,)), DMA((ctx,))],
+        40 * 2**20,
+    )(values)
+
+
+def deal_columns(values, collective_id):
+    ctx = lax.axis_size("ctx")
+    kinds = values.shape[0]
+
+    def kernel(own_ref, out_ref, send_sems, recv_sems):
+        me, mine = lax.axis_index("ctx"), lax.axis_index("fsdp")
+        greet([(lax.rem(me + step, ctx), mine) for step in range(1, ctx)])
+
+        def copy_to(kind):
+            index = kind * ctx + me
+            return pltpu.make_async_remote_copy(
+                own_ref.at[kind],
+                out_ref.at[lax.rem(index, kinds)],
+                send_sems.at[kind],
+                recv_sems.at[lax.rem(index, kinds)],
+                device_id=(index // kinds, mine),
+                device_id_type=MESH,
+            )
+
+        def keep(kind):
+            slot = lax.rem(kind * ctx + me, kinds)
+            return pltpu.make_async_copy(own_ref.at[kind], out_ref.at[slot], send_sems.at[kind])
+
+        def is_far(kind):
+            return (kind * ctx + me) // kinds != me
+
+        for kind in range(kinds):
+            pl.when(is_far(kind))(copy_to(kind).start)
+            pl.when(jnp.logical_not(is_far(kind)))(keep(kind).start)
+        for kind in range(kinds):
+            pl.when(is_far(kind))(copy_to(kind).wait_send)
+            pl.when(jnp.logical_not(is_far(kind)))(keep(kind).wait)
+        for slot in range(kinds):
+
+            @pl.when(lax.rem(me * kinds + slot, ctx) != me)
+            def _():
+                pltpu.make_async_copy(
+                    own_ref.at[slot], out_ref.at[slot], recv_sems.at[slot]
+                ).wait()
+
+    return comm_call(
+        kernel,
+        "deal_columns",
+        collective_id,
+        jax.ShapeDtypeStruct(values.shape, values.dtype),
+        [ANY],
+        ANY,
+        [DMA((kinds,)), DMA((kinds,))],
+        40 * 2**20,
+    )(values)
+
+
+def swap(values, axis, bit):
+    return lax.ppermute(values, axis, [(i, i ^ bit) for i in range(lax.axis_size(axis))])
+
+
+def halved(values, dim, axis, bit):
+    own = (lax.axis_index(axis) // bit) % 2
+    given = lax.dynamic_index_in_dim(values, 1 - own, dim, keepdims=False).astype(jnp.bfloat16)
+    kept = lax.dynamic_index_in_dim(values, own, dim, keepdims=False)
+    return kept.astype(jnp.float32) + swap(given, axis, bit).astype(jnp.float32)
+
+
+def scatter_sum(values, dim, axis, bits):
+    count = len(bits)
+    shape = values.shape
+    values = values.reshape(
+        shape[:dim] + (2,) * count + (shape[dim] // 2**count,) + shape[dim + 1 :]
+    )
+    for left in range(count - 1, -1, -1):
+        values = halved(values, dim + left, axis, bits[count - 1 - left])
+    return values
+
+
 def on_device_heads(
     tokens,
     doc_lengths,
@@ -520,7 +882,7 @@
 ):
     rows, width = tokens.shape[1], tokens.shape[2]
     ctx, fsdp = lax.axis_size("ctx"), lax.axis_size("fsdp")
-    me, mine = lax.axis_index("ctx"), lax.axis_index("fsdp")
+    me = lax.axis_index("ctx")
     head_dim = width // HEADS
     heads = HEADS // ctx
     cols = heads * head_dim
@@ -560,7 +922,8 @@
     squares = jnp.stack(
         [jnp.sum(query_lin * query_lin, axis=1), jnp.sum(key_lin * key_lin, axis=1)]
     )
-    scales = lax.rsqrt(lax.psum(squares, "ctx") / width + EPSILON)
+    squares = ctx_sum(squares.reshape(-1, 128), 1).reshape(2, total)
+    scales = lax.rsqrt(squares / width + EPSILON)
     own_gain_query = lax.dynamic_slice_in_dim(gain_query, me * cols, cols, 0)
     own_gain_key = lax.dynamic_slice_in_dim(gain_key, me * cols, cols, 0)
     query_unit = query_lin * scales[0][:, None]
@@ -579,15 +942,7 @@
     prob_low = probs.astype(bf16)
     attended = dot32("hqk,khd->qhd", prob_low, value_low)
 
-    def to_rows(values):
-        values = lax.all_to_all(values, "ctx", 0, 1, tiled=True)
-        return lax.all_to_all(values, "fsdp", 1, 0, tiled=True)
-
-    def to_heads(values):
-        values = lax.all_to_all(values, "fsdp", 0, 1, tiled=True)
-        return lax.all_to_all(values, "ctx", 1, 0, tiled=True)
-
-    attended_part = to_rows(attended.reshape(total, cols).astype(bf16))
+    attended_part = heads_to_rows(attended.reshape(total, cols).astype(bf16), 2)
     mixed_part = dot32("td,de->te", attended_part, w_out).astype(bf16)
     inputs = tokens[0].astype(f32)
     mixed = inputs + lax.psum_scatter(
@@ -601,14 +956,18 @@
     experts = w_gate.shape[0]
     top = routes.shape[2]
     capacity = rows * top // experts
-    slots = jax.vmap(slot_of_pairs)(pairs_all[:, 0], pairs_all[:, 1])
     expert_ids = jnp.arange(experts, dtype=jnp.int32)
-    chosen = pairs_all[:, 0][:, :, :, None] == expert_ids
-    slot_by_expert = jnp.sum(jnp.where(chosen, slots[..., None] + 1, 0), axis=2) - 1
-    spread = (
-        slot_by_expert.transpose(0, 2, 1)[:, :, None, :]
-        == jnp.arange(capacity, dtype=jnp.int32)[None, None, :, None]
-    )
+
+    def spread_of(pairs):
+        slots = jax.vmap(slot_of_pairs)(pairs[:, 0], pairs[:, 1])
+        chosen = pairs[:, 0][:, :, :, None] == expert_ids
+        slot_by_expert = jnp.sum(jnp.where(chosen, slots[..., None] + 1, 0), axis=2) - 1
+        return (
+            slot_by_expert.transpose(0, 2, 1)[:, :, None, :]
+            == jnp.arange(capacity, dtype=jnp.int32)[None, None, :, None]
+        )
+
+    spread = spread_of(pairs_all)
     disp = spread.astype(bf16).reshape(fsdp, experts * capacity, rows)
     logits = dot32("td,ed->te", group, router_weight)
     router_probs = jax.nn.softmax(logits, axis=-1).reshape(fsdp, rows, experts)
@@ -645,10 +1004,36 @@
     hidden_grad = raw_grad * slot_gate_value[..., None]
     gate_low, up_low = silu_parts(hidden_grad, gate_pre, up_pre)
     in_grad = dot32("ech,edh->ecd", gate_low, w_gate) + dot32("ech,edh->ecd", up_low, w_up)
-    g_gate = dot32("ecd,ech->edh", expert_in, gate_low).astype(bf16)
-    g_up = dot32("ecd,ech->edh", expert_in, up_low).astype(bf16)
     scaled_hidden = (hidden.astype(f32) * slot_gate_value[..., None]).astype(bf16)
-    g_down = dot32("ech,ecd->ehd", scaled_hidden, slot_dy).astype(bf16)
+
+    def both(values):
+        return jnp.concatenate([values, swap(values, "ctx", 1)], axis=1)
+
+    def half(values, which):
+        values = values.reshape(-1, ctx // 2, 2, cols)
+        return lax.dynamic_index_in_dim(values, which, 2, keepdims=False).reshape(-1, width // 2)
+
+    def half_of_both(values):
+        other = swap(half(values, 1 - me % 2), "ctx", 1)
+        values = jnp.concatenate([half(values, me % 2), other], axis=0)
+        picked = dot32("bst,btd->bsd", disp_both, values.reshape(2 * fsdp, rows, width // 2))
+        picked = picked.astype(bf16).reshape(2 * fsdp, experts, capacity, width // 2)
+        return picked.transpose(1, 0, 2, 3).reshape(experts, 2 * fsdp * capacity, width // 2)
+
+    disp_both = jnp.concatenate(
+        [disp, spread_of(swap(pairs_all, "ctx", 1)).astype(bf16).reshape(disp.shape)], axis=0
+    )
+    high_bits = [2**i for i in range(1, ctx.bit_length() - 1)]
+    half_in, half_dy = half_of_both(group), half_of_both(dy_all)
+    down_parts = scatter_sum(
+        dot32("ech,ecd->ehd", both(scaled_hidden), half_dy).astype(bf16), 2, "ctx", high_bits
+    )
+    gate_parts = scatter_sum(
+        dot32("ecd,ech->edh", half_in, both(gate_low)).astype(bf16), 1, "ctx", high_bits
+    )
+    up_parts = scatter_sum(
+        dot32("ecd,ech->edh", half_in, both(up_low)).astype(bf16), 1, "ctx", high_bits
+    )
     prob_grad = jnp.sum(
         jnp.where(
             spread,
@@ -676,7 +1061,7 @@
     mixed_all = lax.all_gather(mixed_grad.astype(bf16), "fsdp", axis=0, tiled=True)
     output_part = dot32("te,de->td", mixed_all, w_out).astype(bf16)
     g_out = dot32("td,te->de", attended_part, mixed_all).astype(bf16)
-    output_grad = by_head(to_heads(output_part))
+    output_grad = by_head(rows_to_heads(output_part, 3))
 
     row_delta = jnp.sum(output_grad.astype(f32) * attended, axis=-1).T
     prob_grad_attn = dot32("qhd,khd->hqk", output_grad, value_low)
@@ -690,12 +1075,10 @@
     own_g_key = jnp.sum(key_back * key_unit, axis=0)
     query_back = query_back * own_gain_query
     key_back = key_back * own_gain_key
-    inner_sums = lax.psum(
-        jnp.stack(
-            [jnp.sum(query_back * query_unit, axis=1), jnp.sum(key_back * key_unit, axis=1)]
-        ),
-        "ctx",
-    ) / width
+    inner_sums = jnp.stack(
+        [jnp.sum(query_back * query_unit, axis=1), jnp.sum(key_back * key_unit, axis=1)]
+    )
+    inner_sums = ctx_sum(inner_sums.reshape(-1, 128), 1).reshape(2, total) / width
     proj_grad = jnp.concatenate(
         [
             scales[0][:, None] * (query_back - query_unit * inner_sums[0][:, None]),
@@ -717,16 +1100,10 @@
         pulled_one - unit_one * jnp.mean(unit_one * pulled_one, axis=-1, keepdims=True)
     )
 
-    gate_parts = lax.psum_scatter(g_gate, "ctx", scatter_dimension=1, tiled=True).astype(f32)
-    up_parts = lax.psum_scatter(g_up, "ctx", scatter_dimension=1, tiled=True).astype(f32)
-    down_parts = lax.psum_scatter(g_down, "ctx", scatter_dimension=2, tiled=True).astype(f32)
-    out_part = lax.psum_scatter(g_out, "ctx", scatter_dimension=1, tiled=True).astype(f32)
-    qkv_shard = lax.psum_scatter(g_qkv, "fsdp", scatter_dimension=0, tiled=True)
-    qkv_full = lax.all_gather(qkv_shard, "ctx", axis=0)
-    qkv_full = qkv_full.reshape(ctx, part, 3, cols).transpose(1, 2, 0, 3).reshape(part, 3 * width)
-    qkv_part = lax.dynamic_slice_in_dim(
-        qkv_full, me * (3 * width // ctx), 3 * width // ctx, 1
-    ).astype(f32)
+    out_part = scatter_sum(g_out, 1, "ctx", [1] + high_bits)
+    qkv_shard = scatter_sum(g_qkv, 0, "fsdp", [2**i for i in range(fsdp.bit_length() - 1)])
+    qkv_shard = qkv_shard.astype(bf16).reshape(part, 3, cols).transpose(1, 0, 2)
+    qkv_part = deal_columns(qkv_shard, 4).transpose(1, 0, 2).reshape(part, 3 * cols).astype(f32)
 
     def placed_cols(values):
         return lax.dynamic_update_slice_in_dim(jnp.zeros((width,), f32), values, me * cols, 0)
@@ -738,8 +1115,7 @@
         ],
         axis=0,
     )
-    sums = lax.psum(sums, ("ctx", "fsdp"))
-    sums = lax.dynamic_slice_in_dim(sums, mine * part, part, 1)
+    sums = mesh_sum(jnp.pad(sums, ((0, -sums.shape[0] % 8), (0, 0))), 5)
     return (
         activations[None],
         input_grad[None],
@@ -749,7 +1125,7 @@
         sums[2],
         out_part,
         sums[3],
-        sums[4:].T,
+        sums[4 : 4 + experts].T,
         gate_parts,
         up_parts,
         down_parts,
@@ -788,7 +1164,9 @@
         P(None, "ctx", "fsdp"),
         P(None, "fsdp", "ctx"),
     )
-    body = on_device_heads if HEADS % mesh.shape["ctx"] == 0 else on_device
+    ctx, fsdp = mesh.shape["ctx"], mesh.shape["fsdp"]
+    by_heads = HEADS % ctx == 0 and ctx % fsdp == 0 and ctx & (ctx - 1) == 0 and fsdp == 4
+    body = on_device_heads if by_heads else on_device
     return jax.shard_map(
         body, mesh=mesh, in_specs=in_specs, out_specs=out_specs, check_vma=False
     )

time: 1360 us -> 838 us (0.62)
  waiting for transfers between devices: 966 us -> 334 us
  blocking collectives: 105 us -> 11.2 us
  Pallas kernels: 0 us -> 86.1 us
  local copies, waits for them, and re-layouts: 58.8 us -> 136 us
  starting transfers between devices: 1.04 us -> 24 us
  other arithmetic: 57.6 us -> 79.6 us
    reduce_scatter x5 -> x0, waiting for transfers between devices: 426 us -> none  [the longest x1 121 us: on_device_heads(): lax.psum_scatter(g_down, 'ctx', scatter_dimension=2, tiled=True).astype(f32)]
    ppermute x0 -> x17, waiting for transfers between devices: none -> 146 us  [swap(): lax.ppermute(values, axis, [(i, i ^ bit) for i in range(lax.axis_size(axi...]
    psum x1 -> x0, waiting for transfers between devices: 116 us -> none  [on_device_heads(): sums = lax.psum(sums, ('ctx', 'fsdp'))]
    all_gather x1 -> x0, waiting for transfers between devices: 98.6 us -> none  [on_device_heads(): qkv_full = lax.all_gather(qkv_shard, 'ctx', axis=0)]
    reduce_scatter x1, waiting for transfers between devices: 89.4 us -> 0.01 us  [on_device_heads(): lax.psum_scatter(normed_grad_part.astype(bf16), 'ctx', scatter_dimension=...]
    pallas_call x0 -> x6, Pallas kernels: none -> 86.1 us  [the longest x1 23.4 us: rows_to_heads(): comm_call(kernel, 'rows_to_heads', collective_id, jax.ShapeDtypeStruct((c...]
    all_to_all x4 -> x0, blocking collectives: 58.5 us -> none  [the longest x1 19.3 us: to_heads(): return lax.all_to_all(values, 'ctx', 1, 0, tiled=True)]
    dynamic_slice x0 -> x12, local copies, waits for them, and re-layouts: none -> 37.4 us  [the longest x5 21.5 us: halved(): kept = lax.dynamic_index_in_dim(values, own, dim, keepdims=False)]
  transfers between devices with their start and end apart: 16 -> 26, of which waited for: 15 -> 16; matrix products, arithmetic and copies ran while one was open for 6% -> 23% of each run, Pallas kernels for 0% -> 4%
where the time goes in v2:
time: 838 us; the launch traced here: 827 us
  waiting for transfers between devices  334 us (40%)
  matrix products  140 us (17%)
  local copies, waits for them, and re-layouts  136 us (16%)
  Pallas kernels  86.1 us (10%)
  other arithmetic  79.6 us (9%)
  starting transfers between devices  24 us (3%)
  between operations  15.6 us (2%)
  blocking collectives  11.2 us (1%)
    ppermute x17, waiting for transfers between devices, swap(): lax.ppermute(values, axis, [(i, i ^ bit) for i in range(lax.axis_size(axi...  146 us
    dot_general x29, matrix products, dot32(): return jnp.einsum(spec, left, right, preferred_element_type=jnp.float32)  131 us
    all_gather x1, waiting for transfers between devices, on_device_heads(): tokens_all = lax.all_gather(tokens[0], 'ctx', axis=0, tiled=True)  61.8 us
    reduce_scatter x1, waiting for transfers between devices, on_device_heads(): lax.psum_scatter(mixed_part, 'fsdp', scatter_dimension=0, tiled=True)  32.6 us
    reduce_scatter x1, waiting for transfers between devices, on_device_heads(): lax.psum_scatter(group_grad.astype(bf16), 'fsdp', scatter_dimension=0, ti...  31.3 us
    unnamed x189, local copies, waits for them, and re-layouts  31.1 us
    all_gather x1, waiting for transfers between devices, on_device_heads(): qkv_weight = lax.all_gather(own_cols, 'fsdp', axis=0, tiled=True)  26.3 us
    pallas_call x1, Pallas kernels, rows_to_heads(): comm_call(kernel, 'rows_to_heads', collective_id, jax.ShapeDtypeStruct((c...  23.4 us
  transfers between devices with their start and end apart: 26, of which 16 were waited for; matrix products, arithmetic and copies ran while one was open for 23% of the time, Pallas kernels for 4%

profile of v2, /device:TPU:5, one launch (start us, length us, event | category | flops | bytes accessed | tf_op | source)
XLA Modules:
  0.0 826.6 jit_solution(8104737942689328043)
XLA Ops:
  10.5 5.7 all_gather.25
  21.9 61.8 %all-gather.15.cloned.1.call-done = bf16[1,1024,2048]{2,1,0:T(8,128)(2,1)} async-done(((bf16[1,128,2048]{2,1,0:T(8,128)(2,1)}), bf16[1,1024,2048]{2,1,0:T(8,128)(2,1)}) %all-gather.15.cloned.1.call-update) | async-done | bytes 4194320 | tf_op jit(solution)/shard_map/all_gather | solution.py:895
  86.8 26.3 %all-gather.9.cloned.1.call-done = bf16[2048,768]{1,0:T(8,128)(2,1)} async-done(((bf16[512,768]{1,0:T(8,128)(2,1)}), bf16[2048,768]{1,0:T(8,128)(2,1)}) %all-gather.9.cloned.1.call-update) | async-done | bytes 3145744 | tf_op jit(solution)/shard_map/all_gather | solution.py:909
  113.1 6.9 fusion.32
  121.9 6.3 ctx_sum.2
  141.3 3.9 subtract_convert_fusion.1
  145.2 8.8 %fusion.116 = (f32[2,1024]{1,0:T(2,128)S(1)}, f32[2,1024,1024]{1,2,0:T(8,128)}) fusion(pred[1024,1024]{0,1:T(8,128)(4,1)} %compare_and_fusion, bf16[1024,2,64]{2,0,1:T(8,128)(2,1)} %get-tuple-element.126, bf16[1024,2,64]{2,0,1:T(8,128)(2,1)} %get-tuple-element.127, bf16[1024,2,64]{2,0,1:T(8,128)(2,1)} %get-tuple-element.107, ...), kind=kOutput, calls=%fused_computation.274 | convolution fusion | flops 547357696 | bytes 10493952 | tf_op jit(solution)/shard_map/sub | solution.py:940
  154.0 4.7 fusion.12
  161.2 14.6 %heads_to_rows.1 = bf16[512,512]{1,0:T(8,128)(2,1)S(1)} custom-call(bf16[1024,256]{1,0:T(8,128)(2,1)S(1)} %copy.375.own_ref), custom_call_target="tpu_custom_call" | custom-call | bytes 41943040 | tf_op jit(solution)/shard_map/heads_to_rows/pallas_call | solution.py:706
  180.4 32.6 %reduce-scatter.5.cloned.1.call-done = bf16[128,2048]{1,0:T(8,128)(2,1)} async-done(((bf16[512,2048]{1,0:T(8,128)(2,1)}), bf16[128,2048]{1,0:T(8,128)(2,1)}) %reduce-scatter.5.cloned.1.call-update) | async-done | bytes 524304 | tf_op jit(solution)/shard_map/reduce_scatter | solution.py:948
  216.5 5.5 all-gather.1
  230.6 5.1 collective-permute-done.5
  239.6 4.5 copy.313
  244.1 3.4 convolution_convert_fusion
  247.5 3.2 copy.314
  250.7 12.2 %all-gather.11.cloned.1.call-done = bf16[512,2048]{1,0:T(8,128)(2,1)} async-done(((bf16[128,2048]{1,0:T(8,128)(2,1)}), bf16[512,2048]{1,0:T(8,128)(2,1)}) %all-gather.11.cloned.1.call-update) | async-done | bytes 2097168 | tf_op jit(solution)/shard_map/all_gather | solution.py:954
  262.9 3.5 convolution_convert_fusion.1
  266.4 3.3 copy.307
  269.7 6.0 fusion.119
  275.7 6.0 fusion.120
  281.8 6.1 fusion.13
  291.4 5.0 multiply_convert_fusion.2
  296.4 9.5 %fusion.121 = f32[6,256,2048]{2,1,0:T(8,128)} fusion(bf16[6,256,256]{2,1,0:T(8,128)(2,1)} %get-tuple-element.95, bf16[6,2048,256]{2,1,0:T(8,128)(2,1)} %param.26), kind=kOutput, calls=%fused_computation.279 | convolution fusion | flops 1610612736 | bytes 19660800 | tf_op jit(solution)/shard_map/ech,edh->ecd/dot_general | solution.py:506
  305.8 11.2 %add_convert_fusion = bf16[6,256,2048]{2,1,0:T(8,128)(2,1)} fusion(f32[6,256,2048]{2,1,0:T(8,128)} %fusion.121, bf16[6,256,256]{2,1,0:T(8,128)(2,1)} %get-tuple-element.94, bf16[6,2048,256]{2,1,0:T(8,128)(2,1)} %param.27), kind=kOutput, calls=%fused_computation.2 | convolution fusion | flops 1616904192 | bytes 25952256 | tf_op jit(solution)/shard_map/ech,edh->ecd/dot_general | solution.py:506
  317.0 3.4 copy.315
  320.4 3.3 fusion.122
  323.7 4.4 fusion.8
  328.2 31.3 %reduce-scatter.9.cloned.1.call-done = bf16[128,2048]{1,0:T(8,128)(2,1)} async-done(((bf16[512,2048]{1,0:T(8,128)(2,1)}), bf16[128,2048]{1,0:T(8,128)(2,1)}) %reduce-scatter.9.cloned.1.call-update) | async-done | bytes 524304 | tf_op jit(solution)/shard_map/reduce_scatter | solution.py:1052
  364.7 22.9 %all-gather.13.cloned.1.call-done = bf16[512,2048]{1,0:T(8,128)(2,1)} async-done(((bf16[128,2048]{1,0:T(8,128)(2,1)}), bf16[512,2048]{1,0:T(8,128)(2,1)}) %all-gather.13.cloned.1.call-update) | async-done | bytes 2097168 | tf_op jit(solution)/shard_map/all_gather | solution.py:1061
  390.5 23.4 %rows_to_heads.1 = bf16[1024,256]{1,0:T(8,128)(2,1)S(1)} custom-call(bf16[512,512]{1,0:T(8,128)(2,1)S(1)} %convolution_convert_fusion.12.own_ref), custom_call_target="tpu_custom_call" | custom-call | bytes 41943040 | tf_op jit(solution)/shard_map/rows_to_heads/pallas_call | solution.py:780
  414.2 4.6 convolution_convert_fusion.11
  419.0 4.8 multiply_convert_fusion.1
  440.6 12.6 %ctx_sum.3 = f32[16,128]{1,0:T(8,128)S(1)} custom-call(f32[16,128]{1,0:T(8,128)S(1)} %reshape.501.own_ref), custom_call_target="tpu_custom_call" | custom-call | bytes 20971520 | tf_op jit(solution)/shard_map/ctx_sum/pallas_call | solution.py:558
  455.6 8.9 %fusion.5 = (f32[2048]{0:T(1024)}, bf16[1024,2048]{1,0:T(8,128)(2,1)}) fusion(bf16[1,1024,2048]{2,1,0:T(8,128)(2,1)S(1)} %copy-done.24, f32[1024]{0:T(1024)S(1)} %copy-done.69, bf16[2048,768]{1,0:T(8,128)(2,1)} %all-gather.9.cloned.1.call-done, bf16[1024,256]{0,1:T(8,128)(2,1)S(1)} %bitcast.369, bf16[1024,256]{0,1:T(8,128)(2,1)S(1)} %get-tuple-element.105, ...), kind=kOutput, calls=%fused_computation.9 | convolution fusion | flops 3236427776 | bytes 13119488 | tf_op jit(solution)/shard_map/te,de->td/dot_general | solution.py:506
  468.9 31.4 %collective-permute-done.14 = bf16[512,1024]{0,1:T(8,128)(2,1)S(1)} collective-permute-done((bf16[512,1024]{0,1:T(8,128)(2,1)}, bf16[512,1024]{0,1:T(8,128)(2,1)S(1)}, u32[]{:S(2)}, u32[]{:S(2)}) %collective-permute-start.14) | collective-permute-done | bytes 1048608 | tf_op jit(solution)/shard_map/ppermute | solution.py:845
  505.8 3.4 convolution_convert_fusion.2
  509.2 3.4 copy.355
  516.9 8.6 %constant_dynamic-slice_fusion.9 = (bf16[512,4,1,256]{3,2,1,0:T(2,128)(2,1)}, bf16[512,4,1,256]{3,2,1,0:T(2,128)(2,1)}) fusion(bf16[512,4,2,256]{3,2,1,0:T(2,128)(2,1)} %reshape.506, s32[]{:T(128)S(6)} %select_n.239, s32[]{:T(128)S(6)} %select_n.240), kind=kLoop, calls=%fused_computation.202 | loop fusion | bytes 4194312 | tf_op jit(solution)/shard_map/jit(dynamic_index_in_dim)/dynamic_slice | solution.py:1014
  525.5 5.8 copy.383
  531.3 4.9 multiply_convert_fusion
  541.0 6.0 copy.382
  547.0 6.8 convolution_convert_fusion.8
  553.8 6.2 reshape.520
  560.0 11.1 %constant_dynamic-slice_fusion.1 = (bf16[6,256,2,1,256]{4,3,2,1,0:T(2,128)(2,1)}, bf16[6,256,2,1,256]{4,3,2,1,0:T(2,128)(2,1)S(1)}) fusion(bf16[6,256,2,2,256]{4,3,2,1,0:T(2,128)(2,1)} %reshape.520, s32[]{:T(128)S(6)} %select_n.243, s32[]{:T(128)S(6)} %select_n.244), kind=kLoop, calls=%fused_computation.194 | loop fusion | bytes 6291464 | tf_op jit(solution)/shard_map/jit(dynamic_index_in_dim)/dynamic_slice | solution.py:851
  576.4 4.1 copy.346
  580.6 3.4 convolution_convert_fusion.3
  585.5 3.6 convolution_convert_fusion.10
  592.2 10.1 %collective-permute-done.10 = bf16[6,256,256]{2,1,0:T(8,128)(2,1)} collective-permute-done((bf16[6,256,256]{2,1,0:T(8,128)(2,1)}, bf16[6,256,256]{2,1,0:T(8,128)(2,1)}, u32[]{:S(2)}, u32[]{:S(2)}) %collective-permute-start.10) | collective-permute-done | bytes 786464 | tf_op jit(solution)/shard_map/ppermute | solution.py:845
  602.4 5.4 convolution_convert_fusion.9
  607.7 3.3 constant_dynamic-slice_fusion.5
  620.2 35.0 %collective-permute-done.8 = bf16[6,2,256,256]{3,2,0,1:T(8,128)(2,1)} collective-permute-done((bf16[6,2,256,256]{3,2,0,1:T(8,128)(2,1)}, bf16[6,2,256,256]{3,2,0,1:T(8,128)(2,1)}, u32[]{:S(2)}, u32[]{:S(2)}) %collective-permute-start.8) | collective-permute-done | bytes 1572896 | tf_op jit(solution)/shard_map/ppermute | solution.py:845
  661.1 37.7 %collective-permute-done.11 = bf16[6,2,256,256]{3,2,0,1:T(8,128)(2,1)} collective-permute-done((bf16[6,2,256,256]{3,2,0,1:T(8,128)(2,1)}, bf16[6,2,256,256]{3,2,0,1:T(8,128)(2,1)}, u32[]{:S(2)}, u32[]{:S(2)}) %collective-permute-start.11) | collective-permute-done | bytes 1572896 | tf_op jit(solution)/shard_map/ppermute | solution.py:845
  704.4 4.4 convolution_convert_fusion.4
  711.7 5.0 collective-permute-start
  716.8 4.2 convolution_convert_fusion.5
  721.0 3.3 reshape.505
  724.2 4.3 constant_dynamic-slice_fusion.11
  730.5 3.2 bitcast_add_fusion.1
  736.2 11.2 %collective-permute-done.12 = bf16[6,256,256]{2,1,0:T(8,128)(2,1)} collective-permute-done((bf16[6,256,256]{2,1,0:T(8,128)(2,1)}, bf16[6,256,256]{2,1,0:T(8,128)(2,1)}, u32[]{:S(2)}, u32[]{:S(2)}) %collective-permute-start.12) | collective-permute-done | bytes 786464 | tf_op jit(solution)/shard_map/ppermute | solution.py:845
  749.8 4.1 collective-permute-done.2
  757.7 14.8 %mesh_sum.1 = f32[16,512]{1,0:T(8,128)S(1)} custom-call(f32[16,2048]{1,0:T(8,128)S(1)} %pad.4.own_ref), custom_call_target="tpu_custom_call" | custom-call | bytes 31457280 | tf_op jit(solution)/shard_map/mesh_sum/pallas_call | solution.py:613
  781.0 10.0 %collective-permute-done.4 = bf16[512,256]{1,0:T(8,128)(2,1)S(1)} collective-permute-done((bf16[512,256]{1,0:T(8,128)(2,1)S(1)}, bf16[512,256]{1,0:T(8,128)(2,1)S(1)}, u32[]{:S(2)}, u32[]{:S(2)}) %collective-permute-start.4) | collective-permute-done | bytes 262176 | tf_op jit(solution)/shard_map/ppermute | solution.py:845
  793.1 14.4 %deal_columns.1 = bf16[3,512,256]{2,1,0:T(8,128)(2,1)S(1)} custom-call(bf16[3,512,256]{2,1,0:T(8,128)(2,1)S(1)} %bitcast.323), custom_call_target="tpu_custom_call" | custom-call | bytes 41943040 | tf_op jit(solution)/shard_map/deal_columns/pallas_call | solution.py:832
  816.4 3.5 fusion.42
  (372 shorter events, 162.7 us)
Async XLA Ops:
  7.2 169.5 %copy-start = (bf16[512,2048]{1,0:T(8,128)(2,1)S(1)}, bf16[512,2048]{1,0:T(8,128)(2,1)}, u32[]{:S(2)}) copy-start(bf16[512,2048]{1,0:T(8,128)(2,1)} %param.23) | copy-start | bytes 6291460
  7.2 9.1 %copy-start.80 = (s32[1,16]{1,0:T(1,128)S(1)}, s32[1,16]{1,0:T(1,128)}, u32[]{:S(2)}) copy-start(s32[1,16]{1,0:T(1,128)} %param.16) | copy-start | bytes 196
  7.3 76.4 %all-gather.15.cloned.1.call-start = ((), (), s32[]{:S(2)}) async-start(), calls=%async_computation.11 | async-start | bytes 4718592 | tf_op jit(solution)/shard_map/all_gather | solution.py:895
  8.0 105.1 %all-gather.9.cloned.1.call-start = ((), (), s32[]{:S(2)}) async-start(), calls=%async_computation.4 | async-start | bytes 3932160 | tf_op jit(solution)/shard_map/all_gather | solution.py:909
  10.2 202.8 %reduce-scatter.5.cloned.1.call-start = ((), (), s32[]{:S(2)}) async-start(), calls=%async_computation.5 | async-start | bytes 2621440 | tf_op jit(solution)/shard_map/reduce_scatter | solution.py:948
  16.3 96.8 %copy-start.49 = (f32[1,2048]{1,0:T(1,128)}, f32[1,2048]{1,0:T(1,128)S(1)}, u32[]{:S(2)}) copy-start(f32[1,2048]{1,0:T(1,128)S(1)} %get-tuple-element.141) | copy-start | bytes 24580
  16.3 112.0 %copy-start.56 = (f32[1,256]{1,0:T(1,128)}, f32[1,256]{1,0:T(1,128)S(1)}, u32[]{:S(2)}) copy-start(f32[1,256]{1,0:T(1,128)S(1)} %get-tuple-element.164) | copy-start | bytes 3076
  16.3 112.0 %copy-start.58 = (f32[1,256]{1,0:T(1,128)}, f32[1,256]{1,0:T(1,128)S(1)}, u32[]{:S(2)}) copy-start(f32[1,256]{1,0:T(1,128)S(1)} %get-tuple-element.165) | copy-start | bytes 3076
  20.0 121.3 %copy-start.21 = (f32[1024,64]{1,0:T(8,128)}, f32[1024,64]{1,0:T(8,128)S(1)}, u32[]{:S(2)}) copy-start(f32[1024,64]{1,0:T(8,128)S(1)} %get-tuple-element.153) | copy-start | bytes 786436
  86.8 33.3 %copy-start.68 = (f32[1024]{0:T(1024)}, f32[1024]{0:T(1024)S(1)}, u32[]{:S(2)}) copy-start(f32[1024]{0:T(1024)S(1)} %add_rsqrt_fusion.1) | copy-start | bytes 12292
  145.2 8.8 %copy-start.28 = (bf16[1024,2,64]{2,0,1:T(8,128)(2,1)}, bf16[1024,2,64]{2,0,1:T(8,128)(2,1)S(1)}, u32[]{:S(2)}) copy-start(bf16[1024,2,64]{2,0,1:T(8,128)(2,1)S(1)} %get-tuple-element.106) | copy-start | bytes 786436
  179.2 33.8 %copy-start.6 = (bf16[1,128,2048]{2,1,0:T(8,128)(2,1)S(1)}, bf16[1,128,2048]{2,1,0:T(8,128)(2,1)}, u32[]{:S(2)}) copy-start(bf16[1,128,2048]{2,1,0:T(8,128)(2,1)} %param.15) | copy-start | bytes 1572868
  179.2 37.2 %copy-start.73 = (s32[1,128,3]{1,0,2:T(1,128)S(1)}, s32[1,128,3]{1,0,2:T(1,128)}, u32[]{:S(2)}) copy-start(s32[1,128,3]{1,0,2:T(1,128)} %param.18) | copy-start | bytes 4612
  179.2 37.2 %copy-start.74 = (s32[1,128,3]{1,0,2:T(1,128)S(1)}, s32[1,128,3]{1,0,2:T(1,128)}, u32[]{:S(2)}) copy-start(s32[1,128,3]{1,0,2:T(1,128)} %param.17) | copy-start | bytes 4612
  179.3 60.4 %all-gather.17.cloned.1.call-start = ((), (), s32[]{:S(2)}) async-start(), calls=%async_computation.12 | async-start | bytes 2621440 | tf_op jit(solution)/shard_map/all_gather | solution.py:910
  180.3 82.5 %all-gather.11.cloned.1.call-start = ((), (), s32[]{:S(2)}) async-start(), calls=%async_computation.6 | async-start | bytes 2621440 | tf_op jit(solution)/shard_map/all_gather | solution.py:954
  214.3 7.7 copy-start.60
  216.4 143.1 %reduce-scatter.9.cloned.1.call-start = ((), (), s32[]{:S(2)}) async-start(), calls=%async_computation.8 | async-start | bytes 2621440 | tf_op jit(solution)/shard_map/reduce_scatter | solution.py:1052
  222.2 13.5 %collective-permute-start.5 = (s32[4,2,128,3]{3,2,0,1:T(8,128)S(1)}, s32[4,2,128,3]{3,2,0,1:T(8,128)}, u32[]{:S(2)}, u32[]{:S(2)}) collective-permute-start(s32[4,2,128,3]{3,2,0,1:T(8,128)S(1)} %copy.302), channel_id=1, source_target_pairs={{0,4},{4,0},{8,12},{12,8},{16,20},{20,16},{24,28},{28,24},{1,5},{5... | collective-permute-start | bytes 36872 | tf_op jit(solution)/shard_map/ppermute | solution.py:845
  262.9 6.8 slice-start.2
  269.7 6.0 copy-start.18
  269.7 12.0 %slice-start.4 = ((s8[6291456]{0:T(1024)(128)(4,1)}), s8[4194304]{0:T(1024)(128)(4,1)S(1)}, s32[]{:S(2)}) async-start(s8[6291456]{0:T(1024)(128)(4,1)} %bitcast.337), calls=%async_computation.17 | async-start | bytes 8388608
  269.7 12.0 %slice-start.6 = ((s8[6291456]{0:T(1024)(128)(4,1)}), s8[2097152]{0:T(1024)(128)(4,1)S(1)}, s32[]{:S(2)}) async-start(s8[6291456]{0:T(1024)(128)(4,1)} %bitcast.347), calls=%async_computation.19 | async-start | bytes 4194304
  281.8 6.3 copy-start.44
  281.8 8.6 %copy-start.48 = (s32[4,6,128]{2,1,0:T(8,128)S(1)}, s32[4,6,128]{2,1,0:T(8,128)}, u32[]{:S(2)}) copy-start(s32[4,6,128]{2,1,0:T(8,128)} %copy.306) | copy-start | bytes 36868
  290.3 6.1 copy-start.45
  323.7 35.8 %copy-start.8 = (bf16[128,2048]{1,0:T(8,128)(2,1)S(1)}, bf16[128,2048]{1,0:T(8,128)(2,1)}, u32[]{:S(2)}) copy-start(bf16[128,2048]{1,0:T(8,128)(2,1)} %reduce-scatter.5.cloned.1.call-done) | copy-start | bytes 1572868
  328.2 59.5 %all-gather.13.cloned.1.call-start = ((), (), s32[]{:S(2)}) async-start(), calls=%async_computation.9 | async-start | bytes 2621440 | tf_op jit(solution)/shard_map/all_gather | solution.py:1061
  364.7 450.3 %reduce-scatter.11.cloned.1.call-start = ((), (), s32[]{:S(2)}) async-start(), calls=%async_computation.10 | async-start | bytes 4718592 | tf_op jit(solution)/shard_map/reduce_scatter | solution.py:1093
  440.6 15.0 %copy-start.37 = (bf16[2,128,1024]{2,1,0:T(8,128)(2,1)S(1)}, bf16[2,128,1024]{2,1,0:T(8,128)(2,1)}, u32[]{:S(2)}) copy-start(bf16[2,128,1024]{2,1,0:T(8,128)(2,1)} %convolution_convert_fusion.11) | copy-start | bytes 1572868
  440.6 15.0 %copy-start.69 = (f32[1024]{0:T(1024)S(1)}, f32[1024]{0:T(1024)}, u32[]{:S(2)}) copy-start(f32[1024]{0:T(1024)} %copy-done.68) | copy-start | bytes 12292
  440.6 15.0 %copy-start.24 = (bf16[1,1024,2048]{2,1,0:T(8,128)(2,1)S(1)}, bf16[1,1024,2048]{2,1,0:T(8,128)(2,1)}, u32[]{:S(2)}) copy-start(bf16[1,1024,2048]{2,1,0:T(8,128)(2,1)} %all-gather.15.cloned.1.call-done) | copy-start | bytes 12582916
  455.5 9.0 %copy-start.39 = (bf16[1024,256]{0,1:T(8,128)(2,1)}, bf16[1024,256]{0,1:T(8,128)(2,1)S(1)}, u32[]{:S(2)}) copy-start(bf16[1024,256]{0,1:T(8,128)(2,1)S(1)} %get-tuple-element.104) | copy-start | bytes 1572868
  455.6 9.0 %copy-start.41 = (bf16[1024,256]{0,1:T(8,128)(2,1)}, bf16[1024,256]{0,1:T(8,128)(2,1)S(1)}, u32[]{:S(2)}) copy-start(bf16[1024,256]{0,1:T(8,128)(2,1)S(1)} %get-tuple-element.105) | copy-start | bytes 1572868
  464.6 351.8 %reduce-scatter.7.cloned.1.call-start = ((), (), s32[]{:S(2)}) async-start(), calls=%async_computation.7 | async-start | bytes 2621440 | tf_op jit(solution)/shard_map/reduce_scatter | solution.py:993
  467.6 32.8 %collective-permute-start.14 = (bf16[512,1024]{0,1:T(8,128)(2,1)}, bf16[512,1024]{0,1:T(8,128)(2,1)S(1)}, u32[]{:S(2)}, u32[]{:S(2)}) collective-permute-start(bf16[512,1024]{0,1:T(8,128)(2,1)} %bitcast.106), channel_id=1, source_target_pairs={{0,4},{4,0},{8,12},{12,8},{16,20},{20,16},{24,28},{28,24},{1,5},{5... | collective-permute-start | bytes 3145736 | tf_op jit(solution)/shard_map/ppermute | solution.py:845
  512.7 34.3 %collective-permute-start.13 = (bf16[6,256,256]{2,1,0:T(8,128)(2,1)}, bf16[6,256,256]{2,1,0:T(8,128)(2,1)}, u32[]{:S(2)}, u32[]{:S(2)}) collective-permute-start(bf16[6,256,256]{2,1,0:T(8,128)(2,1)} %get-tuple-element.146), channel_id=1, source_target_pairs={{0,4},{4,0},{8,12},{12,8},{16,20},{20,16},{24,28},{28,24},{1,5},{5... | collective-permute-start | bytes 2359304 | tf_op jit(solution)/shard_map/ppermute | solution.py:845
  531.3 42.3 %collective-permute-start.6 = (bf16[512,1024]{0,1:T(8,128)(2,1)}, bf16[512,1024]{0,1:T(8,128)(2,1)}, u32[]{:S(2)}, u32[]{:S(2)}) collective-permute-start(bf16[512,1024]{0,1:T(8,128)(2,1)} %bitcast.367), channel_id=1, source_target_pairs={{0,4},{4,0},{8,12},{12,8},{16,20},{20,16},{24,28},{28,24},{1,5},{5... | collective-permute-start | bytes 3145736 | tf_op jit(solution)/shard_map/ppermute | solution.py:845
  536.2 49.3 %collective-permute-start.7 = (bf16[6,256,256]{2,1,0:T(8,128)(2,1)}, bf16[6,256,256]{2,1,0:T(8,128)(2,1)}, u32[]{:S(2)}, u32[]{:S(2)}) collective-permute-start(bf16[6,256,256]{2,1,0:T(8,128)(2,1)} %get-tuple-element.95), channel_id=1, source_target_pairs={{0,4},{4,0},{8,12},{12,8},{16,20},{20,16},{24,28},{28,24},{1,5},{5... | collective-permute-start | bytes 2359304 | tf_op jit(solution)/shard_map/ppermute | solution.py:845
  537.7 64.6 %collective-permute-start.10 = (bf16[6,256,256]{2,1,0:T(8,128)(2,1)}, bf16[6,256,256]{2,1,0:T(8,128)(2,1)}, u32[]{:S(2)}, u32[]{:S(2)}) collective-permute-start(bf16[6,256,256]{2,1,0:T(8,128)(2,1)} %get-tuple-element.94), channel_id=1, source_target_pairs={{0,4},{4,0},{8,12},{12,8},{16,20},{20,16},{24,28},{28,24},{1,5},{5... | collective-permute-start | bytes 2359304 | tf_op jit(solution)/shard_map/ppermute | solution.py:845
  572.6 43.2 %collective-permute-start.15 = (bf16[6,256,2,256]{3,1,0,2:T(8,128)(2,1)}, bf16[6,256,2,256]{3,1,0,2:T(8,128)(2,1)}, u32[]{:S(2)}, u32[]{:S(2)}) collective-permute-start(bf16[6,256,2,256]{3,1,0,2:T(8,128)(2,1)} %bitcast.319), channel_id=1, source_target_pairs={{0,8},{4,12},{8,0},{12,4},{16,24},{20,28},{24,16},{28,20},{1,9},{5... | collective-permute-start | bytes 4718600 | tf_op jit(solution)/shard_map/ppermute | solution.py:845
  590.5 22.2 %slice-start = ((s8[6291456]{0:T(1024)(128)(4,1)}), s8[4194304]{0:T(1024)(128)(4,1)S(1)}, s32[]{:S(2)}) async-start(s8[6291456]{0:T(1024)(128)(4,1)} %bitcast.326), calls=%async_computation.13 | async-start | bytes 8388608
  591.8 20.9 %slice-start.1 = ((s8[6291456]{0:T(1024)(128)(4,1)}), s8[2097152]{0:T(1024)(128)(4,1)S(1)}, s32[]{:S(2)}) async-start(s8[6291456]{0:T(1024)(128)(4,1)} %bitcast.326), calls=%async_computation.14 | async-start | bytes 4194304
  591.8 63.3 %collective-permute-start.8 = (bf16[6,2,256,256]{3,2,0,1:T(8,128)(2,1)}, bf16[6,2,256,256]{3,2,0,1:T(8,128)(2,1)}, u32[]{:S(2)}, u32[]{:S(2)}) collective-permute-start(bf16[6,2,256,256]{3,2,0,1:T(8,128)(2,1)} %bitcast.321), channel_id=1, source_target_pairs={{0,8},{4,12},{8,0},{12,4},{16,24},{20,28},{24,16},{28,20},{1,9},{5... | collective-permute-start | bytes 4718600 | tf_op jit(solution)/shard_map/ppermute | solution.py:845
  612.3 86.5 %collective-permute-start.11 = (bf16[6,2,256,256]{3,2,0,1:T(8,128)(2,1)}, bf16[6,2,256,256]{3,2,0,1:T(8,128)(2,1)}, u32[]{:S(2)}, u32[]{:S(2)}) collective-permute-start(bf16[6,2,256,256]{3,2,0,1:T(8,128)(2,1)} %bitcast.320), channel_id=1, source_target_pairs={{0,8},{4,12},{8,0},{12,4},{16,24},{20,28},{24,16},{28,20},{1,9},{5... | collective-permute-start | bytes 4718600 | tf_op jit(solution)/shard_map/ppermute | solution.py:845
  615.8 39.3 %copy-start.19 = (bf16[6,2,1,256,256]{4,3,2,1,0:T(8,128)(2,1)S(1)}, bf16[6,2,1,256,256]{4,3,2,1,0:T(8,128)(2,1)}, u32[]{:S(2)}) copy-start(bf16[6,2,1,256,256]{4,3,2,1,0:T(8,128)(2,1)} %get-tuple-element.100) | copy-start | bytes 4718596
  618.7 38.4 %copy-start.13 = (f32[6,256,2,256]{3,1,0,2:T(8,128)}, f32[6,256,2,256]{3,1,0,2:T(8,128)S(1)}, u32[]{:S(2)}) copy-start(f32[6,256,2,256]{3,1,0,2:T(8,128)S(1)} %convert_add_fusion) | copy-start | bytes 9437188
  619.8 110.6 %collective-permute-start.16 = (bf16[6,256,256]{2,1,0:T(8,128)(2,1)}, bf16[6,256,256]{2,1,0:T(8,128)(2,1)}, u32[]{:S(2)}, u32[]{:S(2)}) collective-permute-start(bf16[6,256,256]{2,1,0:T(8,128)(2,1)} %fusion.56), channel_id=1, source_target_pairs={{0,16},{4,20},{8,24},{12,28},{16,0},{20,4},{24,8},{28,12},{1,17},{... | collective-permute-start | bytes 2359304 | tf_op jit(solution)/shard_map/ppermute | solution.py:845
  655.1 43.7 %copy-start.20 = (bf16[6,2,1,256,256]{4,3,2,1,0:T(8,128)(2,1)S(1)}, bf16[6,2,1,256,256]{4,3,2,1,0:T(8,128)(2,1)}, u32[]{:S(2)}) copy-start(bf16[6,2,1,256,256]{4,3,2,1,0:T(8,128)(2,1)} %get-tuple-element.98) | copy-start | bytes 4718596
  657.1 43.8 %copy-start.9 = (f32[6,2,256,256]{3,2,0,1:T(8,128)}, f32[6,2,256,256]{3,2,0,1:T(8,128)S(1)}, u32[]{:S(2)}) copy-start(f32[6,2,256,256]{3,2,0,1:T(8,128)S(1)} %convert_add_fusion.2) | copy-start | bytes 9437188
  658.1 75.5 %collective-permute-start.9 = (bf16[6,256,256]{2,1,0:T(8,128)(2,1)}, bf16[6,256,256]{2,1,0:T(8,128)(2,1)}, u32[]{:S(2)}, u32[]{:S(2)}) collective-permute-start(bf16[6,256,256]{2,1,0:T(8,128)(2,1)} %fusion.54), channel_id=1, source_target_pairs={{0,16},{4,20},{8,24},{12,28},{16,0},{20,4},{24,8},{28,12},{1,17},{... | collective-permute-start | bytes 2359304 | tf_op jit(solution)/shard_map/ppermute | solution.py:845
  702.8 44.5 %collective-permute-start.12 = (bf16[6,256,256]{2,1,0:T(8,128)(2,1)}, bf16[6,256,256]{2,1,0:T(8,128)(2,1)}, u32[]{:S(2)}, u32[]{:S(2)}) collective-permute-start(bf16[6,256,256]{2,1,0:T(8,128)(2,1)} %fusion.55), channel_id=1, source_target_pairs={{0,16},{4,20},{8,24},{12,28},{16,0},{20,4},{24,8},{28,12},{1,17},{... | collective-permute-start | bytes 2359304 | tf_op jit(solution)/shard_map/ppermute | solution.py:845
  710.2 6.6 copy-start.3
  711.7 62.6 %collective-permute-start = (bf16[2,512,768]{1,2,0:T(8,128)(2,1)}, bf16[2,512,768]{1,2,0:T(8,128)(2,1)}, u32[]{:S(2)}, u32[]{:S(2)}) collective-permute-start(bf16[2,512,768]{1,2,0:T(8,128)(2,1)} %bitcast.366), channel_id=1, source_target_pairs={{0,1},{1,0},{2,3},{3,2},{4,5},{5,4},{6,7},{7,6},{8,9},{9,8},{10,11... | collective-permute-start | bytes 4718600 | tf_op jit(solution)/shard_map/ppermute | solution.py:845
  728.9 18.4 %copy-start.12 = (f32[6,2,256,256]{3,2,0,1:T(8,128)S(1)}, f32[6,2,256,256]{3,2,0,1:T(8,128)}, u32[]{:S(2)}) copy-start(f32[6,2,256,256]{3,2,0,1:T(8,128)} %copy-done.11) | copy-start | bytes 9437188
  729.0 25.0 %collective-permute-start.2 = (bf16[512,2,2,256]{3,0,1,2:T(8,128)(2,1)S(1)}, bf16[512,2,2,256]{3,0,1,2:T(8,128)(2,1)S(1)}, u32[]{:S(2)}, u32[]{:S(2)}) collective-permute-start(bf16[512,2,2,256]{3,0,1,2:T(8,128)(2,1)S(1)} %bitcast.368), channel_id=1, source_target_pairs={{0,4},{4,0},{8,12},{12,8},{16,20},{20,16},{24,28},{28,24},{1,5},{5... | collective-permute-start | bytes 3145736 | tf_op jit(solution)/shard_map/ppermute | solution.py:845
  733.7 16.1 %copy-start.79 = (f32[128]{0:T(128)S(1)}, f32[128]{0:T(128)}, u32[]{:S(2)}) copy-start(f32[128]{0:T(128)} %get-tuple-element.82) | copy-start | bytes 1540
  733.7 16.1 %copy-start.67 = (f32[256]{0:T(256)S(1)}, f32[256]{0:T(256)}, u32[]{:S(2)}) copy-start(f32[256]{0:T(256)} %get-tuple-element.77) | copy-start | bytes 3076
  755.3 21.3 %collective-permute-start.3 = (bf16[512,2,256]{2,0,1:T(8,128)(2,1)}, bf16[512,2,256]{2,0,1:T(8,128)(2,1)}, u32[]{:S(2)}, u32[]{:S(2)}) collective-permute-start(bf16[512,2,256]{2,0,1:T(8,128)(2,1)} %fusion.62), channel_id=1, source_target_pairs={{0,8},{4,12},{8,0},{12,4},{16,24},{20,28},{24,16},{28,20},{1,9},{5... | collective-permute-start | bytes 1572872 | tf_op jit(solution)/shard_map/ppermute | solution.py:845
  776.6 15.9 %collective-permute-start.1 = (bf16[512,768]{0,1:T(8,128)(2,1)S(1)}, bf16[512,768]{0,1:T(8,128)(2,1)S(1)}, u32[]{:S(2)}, u32[]{:S(2)}) collective-permute-start(bf16[512,768]{0,1:T(8,128)(2,1)S(1)} %fusion.53), channel_id=1, source_target_pairs={{0,2},{1,3},{2,0},{3,1},{4,6},{5,7},{6,4},{7,5},{8,10},{9,11},{10,... | collective-permute-start | bytes 2359304 | tf_op jit(solution)/shard_map/ppermute | solution.py:845
  777.9 13.0 %collective-permute-start.4 = (bf16[512,256]{1,0:T(8,128)(2,1)S(1)}, bf16[512,256]{1,0:T(8,128)(2,1)S(1)}, u32[]{:S(2)}, u32[]{:S(2)}) collective-permute-start(bf16[512,256]{1,0:T(8,128)(2,1)S(1)} %fusion.63), channel_id=1, source_target_pairs={{0,16},{4,20},{8,24},{12,28},{16,0},{20,4},{24,8},{28,12},{1,17},{... | collective-permute-start | bytes 786440 | tf_op jit(solution)/shard_map/ppermute | solution.py:845
  808.7 7.7 copy-start.61
  808.7 7.7 copy-start.72
  811.8 8.1 copy-start.1
  (51 other events, 180.4 us)
Sparse Core Ops, SparseCore 0:
  10.2 73.4 all-gather.14
  85.8 27.2 all-gather.8
  179.4 33.5 reduce-scatter.4
  215.1 23.1 all-gather.16
  240.3 22.5 all-gather.10
  328.3 31.1 reduce-scatter.8
  364.8 22.8 all-gather.12
  464.7 105.9 reduce-scatter.10
  615.5 30.4 reduce-scatter.6

commit v3 on v2

--- a/solution.py
+++ b/solution.py
@@ -479,19 +479,6 @@
     return (jnp.cos(angles), jnp.sin(angles))
 
 
-def turn(values, cosine, sine_part):
-    half_dim = cosine.shape[-1]
-    cosine, sine_part = cosine[:, None, :], sine_part[:, None, :]
-    first_half, second_half = values[..., :half_dim], values[..., half_dim:]
-    return jnp.concatenate(
-        [
-            first_half * cosine - second_half * sine_part,
-            second_half * cosine + first_half * sine_part,
-        ],
-        axis=-1,
-    )
-
-
 def slot_of_pairs(route_ids, order_ids):
     pair_count = route_ids.shape[0] * route_ids.shape[1]
     expert_flat = route_ids.reshape(pair_count)
@@ -863,6 +850,601 @@
     return values
 
 
+def reduce_then_gather(partial, extras, out_shapes, chunk_math, name, collective_id):
+    fsdp = lax.axis_size("fsdp")
+    rows, width = partial.shape[0] // fsdp, partial.shape[1]
+    chunks = 4
+    size = rows // chunks
+    count = len(extras)
+
+    def kernel(*refs):
+        part_ref, extra_refs = refs[0], refs[1 : 1 + count]
+        all_ref, out_refs = refs[1 + count], refs[2 + count : 2 + count + len(out_shapes)]
+        near_own, near_far, far_sum, far_own, sems = refs[2 + count + len(out_shapes) :]
+        me, mine = lax.axis_index("ctx"), lax.axis_index("fsdp")
+        flip = 1 - 2 * lax.rem(mine, 2)
+        core = mine + flip
+        chip = lax.rem(mine + 2, fsdp)
+        diagonal = lax.rem(core + 2, fsdp)
+        greet([(me, core), (me, chip)])
+
+        def span(block, i):
+            return pl.ds(pl.multiple_of(block * rows + i * size, size), size)
+
+        def sem(kind, i):
+            return sems.at[2 * kind, i], sems.at[2 * kind + 1, i]
+
+        copies = []
+        from_core_far, from_core_own, from_chip = [], [], []
+        for i in range(chunks):
+            copy = send(
+                part_ref.at[span(diagonal, i), :], near_far.at[i], *sem(0, i), (me, core)
+            )
+            from_core_far.append(copy)
+        for i in range(chunks):
+            copy = send(part_ref.at[span(core, i), :], near_own.at[i], *sem(1, i), (me, core))
+            from_core_own.append(copy)
+        for i in range(chunks):
+            from_core_far[i].wait_recv()
+            both = part_ref[span(chip, i), :].astype(jnp.float32) + near_far[i].astype(jnp.float32)
+            far_sum[i] = both.astype(jnp.bfloat16)
+            from_chip.append(send(far_sum.at[i], far_own.at[i], *sem(2, i), (me, chip)))
+        to_chip = []
+        for i in range(chunks):
+            from_core_own[i].wait_recv()
+            from_chip[i].wait_recv()
+            total = (
+                part_ref[span(mine, i), :].astype(jnp.float32)
+                + near_own[i].astype(jnp.float32)
+                + far_own[i].astype(jnp.float32)
+            )
+            all_ref[span(mine, i), :] = chunk_math(
+                i, pl.ds(i * size, size), total, extra_refs, out_refs
+            ).astype(jnp.bfloat16)
+            own = all_ref.at[span(mine, i), :]
+            to_chip.append(send(own, own, *sem(3, i), (me, chip)))
+            copies.append(send(own, own, *sem(4, i), (me, core)))
+        for i in range(chunks):
+            to_chip[i].wait_recv()
+            other = all_ref.at[span(chip, i), :]
+            copies.append(send(other, other, *sem(5, i), (me, core)))
+        for copy in copies:
+            copy.wait_recv()
+        for copy in from_core_far + from_core_own + from_chip + to_chip + copies:
+            copy.wait_send()
+
+    return comm_call(
+        kernel,
+        name,
+        collective_id,
+        [jax.ShapeDtypeStruct(partial.shape, jnp.bfloat16)] + out_shapes,
+        [VMEM] * (1 + count),
+        [VMEM] * (1 + len(out_shapes)),
+        [
+            pltpu.VMEM((chunks, size, width), jnp.bfloat16),
+            pltpu.VMEM((chunks, size, width), jnp.bfloat16),
+            pltpu.VMEM((chunks, size, width), jnp.bfloat16),
+            pltpu.VMEM((chunks, size, width), jnp.bfloat16),
+            DMA((12, chunks)),
+        ],
+        100 * 2**20,
+    )(partial, *extras)
+
+
+def norm_chunk(index, span, total, extra_refs, out_refs):
+    tokens_ref, gain_ref = extra_refs
+    mixed = tokens_ref[span, :].astype(jnp.float32) + total
+    out_refs[0][span, :] = mixed
+    return mixed * rms_unit(mixed) * gain_ref[...]
+
+
+def norm_back_chunk(index, span, total, extra_refs, out_refs):
+    mixed_ref, gain_ref, dy_ref = extra_refs
+    mixed = mixed_ref[span, :]
+    scale = rms_unit(mixed)
+    unit = mixed * scale
+    pulled = total * gain_ref[...]
+    grad = dy_ref[span, :].astype(jnp.float32) + scale * (
+        pulled - unit * jnp.mean(unit * pulled, axis=-1, keepdims=True)
+    )
+    out_refs[0][span, :] = grad
+    gain_grad = jnp.sum(total * unit, axis=0, keepdims=True)
+    if index == 0:
+        out_refs[1][...] = gain_grad
+    else:
+        out_refs[1][...] += gain_grad
+    return grad
+
+
+ROUTER_ROWS = 16
+
+
+def one_hot(slots, capacity):
+    return lax.broadcasted_iota(jnp.int32, (capacity, slots.shape[1]), 0) == slots
+
+
+def run_experts(group, dy_all, slots, router, w_gate, w_up, w_down, blocks, capacity):
+    experts, width, units = w_gate.shape
+    total = group.shape[0]
+    rows = total // blocks
+    held = blocks * capacity
+    f32, bf16 = jnp.float32, jnp.bfloat16
+
+    def kernel(
+        group_ref,
+        dy_ref,
+        slots_ref,
+        router_ref,
+        gate_ref,
+        up_ref,
+        down_ref,
+        moved_ref,
+        grad_ref,
+        g_router_ref,
+        slot_ref,
+        disp,
+        ins,
+        dys,
+        probs,
+        prob_grad,
+    ):
+        expert = pl.program_id(0)
+
+        def block_rows(b):
+            return pl.ds(b * rows, rows)
+
+        @pl.when(expert == 0)
+        def _():
+            logits = lax.dot_general(
+                router_ref[...],
+                group_ref[...],
+                (((1,), (1,)), ((), ())),
+                preferred_element_type=f32,
+            )
+            real = lax.broadcasted_iota(jnp.int32, logits.shape, 0) < experts
+            logits = jnp.where(real, logits, MASKED)
+            weights = jnp.exp(logits - jnp.max(logits, axis=0, keepdims=True))
+            probs[...] = weights / jnp.sum(weights, axis=0, keepdims=True)
+            prob_grad[...] = jnp.zeros_like(prob_grad)
+            for b in range(blocks):
+                for e in range(experts):
+                    disp[b, pl.ds(e * capacity, capacity), :] = (
+                        one_hot(slots_ref[pl.ds(e, 1), block_rows(b)], capacity)
+                        .astype(f32)
+                        .astype(bf16)
+                    )
+                for source, target in ((group_ref, ins), (dy_ref, dys)):
+                    picked = jnp.dot(
+                        disp[b], source[block_rows(b), :], preferred_element_type=f32
+                    ).astype(bf16)
+                    for e in range(experts):
+                        target[e, pl.ds(b * capacity, capacity), :] = picked[
+                            e * capacity : (e + 1) * capacity
+                        ]
+
+        expert_in, slot_dy = ins[expert], dys[expert]
+        gate_matrix, up_matrix, down_matrix = gate_ref[0], up_ref[0], down_ref[0]
+        gate_pre = jnp.dot(expert_in, gate_matrix, preferred_element_type=f32)
+        up_pre = jnp.dot(expert_in, up_matrix, preferred_element_type=f32)
+        raw_grad = lax.dot_general(
+            slot_dy, down_matrix, (((1,), (1,)), ((), ())), preferred_element_type=f32
+        )
+        own_probs = probs[pl.ds(expert, 1), :]
+        own_slots = slots_ref[pl.ds(expert, 1), :]
+        hots = [
+            one_hot(own_slots[:, b * rows : (b + 1) * rows], capacity) for b in range(blocks)
+        ]
+        value = jnp.concatenate(
+            [
+                jnp.sum(
+                    jnp.where(hots[b], own_probs[:, b * rows : (b + 1) * rows], 0.0),
+                    axis=1,
+                    keepdims=True,
+                )
+                for b in range(blocks)
+            ],
+            axis=0,
+        )
+        sigma = 1.0 / (1.0 + jnp.exp(-gate_pre))
+        silu = gate_pre * sigma
+        hidden = (silu * up_pre).astype(bf16)
+        hidden_f = hidden.astype(f32)
+        value_grad = jnp.sum(hidden_f * raw_grad, axis=1, keepdims=True)
+        hidden_grad = raw_grad * value
+        gate_low = (hidden_grad * up_pre * sigma * (1.0 + gate_pre * (1.0 - sigma))).astype(bf16)
+        up_low = (hidden_grad * silu).astype(bf16)
+        scaled = (hidden_f * value).astype(bf16)
+        slot_ref[0, 0] = scaled
+        slot_ref[1, 0] = gate_low
+        slot_ref[2, 0] = up_low
+        for b in range(blocks):
+            prob_grad[expert, :, block_rows(b)] = jnp.sum(
+                jnp.where(hots[b], value_grad[b * capacity : (b + 1) * capacity], 0.0),
+                axis=0,
+                keepdims=True,
+            )
+        dys[expert] = jnp.dot(scaled, down_matrix, preferred_element_type=f32).astype(bf16)
+        ins[expert] = (
+            lax.dot_general(
+                gate_low, gate_matrix, (((1,), (1,)), ((), ())), preferred_element_type=f32
+            )
+            + lax.dot_general(
+                up_low, up_matrix, (((1,), (1,)), ((), ())), preferred_element_type=f32
+            )
+        ).astype(bf16)
+
+        @pl.when(expert == experts - 1)
+        def _():
+            grads = jnp.concatenate([prob_grad[e] for e in range(ROUTER_ROWS)], axis=0)
+            weights = probs[...]
+            logit_grad = (
+                weights * (grads - jnp.sum(weights * grads, axis=0, keepdims=True))
+            ).astype(bf16)
+            g_router_ref[...] = jnp.dot(logit_grad, group_ref[...], preferred_element_type=f32)
+            for b in range(blocks):
+                for source, target in ((dys, moved_ref), (ins, grad_ref)):
+                    gathered = jnp.concatenate(
+                        [source[e, pl.ds(b * capacity, capacity), :] for e in range(experts)],
+                        axis=0,
+                    )
+                    back = lax.dot_general(
+                        disp[b], gathered, (((0,), (0,)), ((), ())), preferred_element_type=f32
+                    )
+                    if target is grad_ref:
+                        back = back + lax.dot_general(
+                            logit_grad[:, b * rows : (b + 1) * rows],
+                            router_ref[...],
+                            (((0,), (0,)), ((), ())),
+                            preferred_element_type=f32,
+                        )
+                    target[block_rows(b), :] = back.astype(bf16)
+
+    def whole(shape):
+        return pl.BlockSpec(shape, lambda e: (0,) * len(shape))
+
+    def by_expert(shape):
+        return pl.BlockSpec((1,) + shape, lambda e: (e, 0, 0))
+
+    return pl.pallas_call(
+        kernel,
+        grid=(experts,),
+        out_shape=[
+            jax.ShapeDtypeStruct((total, width), bf16),
+            jax.ShapeDtypeStruct((total, width), bf16),
+            jax.ShapeDtypeStruct((ROUTER_ROWS, width), f32),
+            jax.ShapeDtypeStruct((3, experts, held, units), bf16),
+        ],
+        in_specs=[
+            whole((total, width)),
+            whole((total, width)),
+            whole((ROUTER_ROWS, total)),
+            whole((ROUTER_ROWS, width)),
+            by_expert((width, units)),
+            by_expert((width, units)),
+            by_expert((units, width)),
+        ],
+        out_specs=[
+            whole((total, width)),
+            whole((total, width)),
+            whole((ROUTER_ROWS, width)),
+            pl.BlockSpec((3, 1, held, units), lambda e: (0, e, 0, 0)),
+        ],
+        scratch_shapes=[
+            pltpu.VMEM((blocks, experts * capacity, rows), bf16),
+            pltpu.VMEM((experts, held, width), bf16),
+            pltpu.VMEM((experts, held, width), bf16),
+            pltpu.VMEM((ROUTER_ROWS, total), f32),
+            pltpu.VMEM((ROUTER_ROWS, 1, total), f32),
+        ],
+        compiler_params=pltpu.CompilerParams(vmem_limit_bytes=60 * 2**20),
+        cost_estimate=pl.CostEstimate(
+            flops=30 * 10**9, bytes_accessed=30 * 2**20, transcendentals=10**6
+        ),
+        name="run_experts",
+    )(group, dy_all, slots, router, w_gate, w_up, w_down)
+
+
+def expert_grads(slot_own, slot_other, in_own, in_other, dy_own, dy_other, slots_own, slots_other, blocks, capacity):
+    _, experts, held, units = slot_own.shape
+    total, half = in_own.shape
+    rows = total // blocks
+    ctx = lax.axis_size("ctx")
+    runs = ctx // 4
+    cols = half // (2 * runs)
+    f32, bf16 = jnp.float32, jnp.bfloat16
+
+    def kernel(
+        own_ref,
+        other_ref,
+        in_own_ref,
+        in_other_ref,
+        dy_own_ref,
+        dy_other_ref,
+        slots_own_ref,
+        slots_other_ref,
+        out_ref,
+        ins,
+        dys,
+    ):
+        expert = pl.program_id(0)
+
+        @pl.when(expert == 0)
+        def _():
+            for side, slots_ref, in_ref, dy_ref in (
+                (0, slots_own_ref, in_own_ref, dy_own_ref),
+                (1, slots_other_ref, in_other_ref, dy_other_ref),
+            ):
+                for b in range(blocks):
+                    span = pl.ds(b * rows, rows)
+                    disp = jnp.concatenate(
+                        [
+                            one_hot(slots_ref[pl.ds(e, 1), span], capacity).astype(f32)
+                            for e in range(experts)
+                        ],
+                        axis=0,
+                    ).astype(bf16)
+                    for source, target in ((in_ref, ins), (dy_ref, dys)):
+                        picked = jnp.dot(
+                            disp, source[span, :], preferred_element_type=f32
+                        ).astype(bf16)
+                        for e in range(experts):
+                            target[e, pl.ds(side * held + b * capacity, capacity), :] = picked[
+                                e * capacity : (e + 1) * capacity
+                            ]
+
+        keep_low = (lax.axis_index("ctx") // 2) % 2
+        stacked = [jnp.concatenate([own_ref[m, 0], other_ref[m, 0]], axis=0) for m in range(3)]
+        for low in range(2):
+            kept = jnp.where(keep_low == low, 1, 0)
+            for run in range(runs):
+                span = pl.ds((run * 2 + low) * cols, cols)
+                in_part, dy_part = ins[expert, :, span], dys[expert, :, span]
+                contract = (((0,), (0,)), ((), ()))
+                for m, (left, right) in enumerate(
+                    ((stacked[0], dy_part), (in_part, stacked[1]), (in_part, stacked[2]))
+                ):
+                    out_ref[m, pl.ds(kept, 1), 0, run] = lax.dot_general(
+                        left, right, contract, preferred_element_type=f32
+                    ).astype(bf16)[None]
+
+    def whole(shape):
+        return pl.BlockSpec(shape, lambda e: (0,) * len(shape))
+
+    slot_spec = pl.BlockSpec((3, 1, held, units), lambda e: (0, e, 0, 0))
+    return pl.pallas_call(
+        kernel,
+        grid=(experts,),
+        out_shape=jax.ShapeDtypeStruct((3, 2, experts, runs, units, cols), bf16),
+        in_specs=[slot_spec, slot_spec]
+        + [whole((total, half))] * 4
+        + [whole((ROUTER_ROWS, total))] * 2,
+        out_specs=pl.BlockSpec((3, 2, 1, runs, units, cols), lambda e: (0, 0, e, 0, 0, 0)),
+        scratch_shapes=[
+            pltpu.VMEM((experts, 2 * held, half), bf16),
+            pltpu.VMEM((experts, 2 * held, half), bf16),
+        ],
+        compiler_params=pltpu.CompilerParams(vmem_limit_bytes=60 * 2**20),
+        cost_estimate=pl.CostEstimate(
+            flops=20 * 10**9, bytes_accessed=30 * 2**20, transcendentals=0
+        ),
+        name="expert_grads",
+    )(slot_own, slot_other, in_own, in_other, dy_own, dy_other, slots_own, slots_other)
+
+
+def pick_half(values, parity_flip):
+    ctx = lax.axis_size("ctx")
+    total, width = values.shape
+    cols = width // ctx
+
+    def kernel(in_ref, out_ref):
+        parity = lax.rem(lax.axis_index("ctx") + parity_flip, 2)
+        for run in range(ctx // 2):
+            start = pl.multiple_of((2 * run + parity) * cols, cols)
+            out_ref[:, pl.ds(run * cols, cols)] = in_ref[:, pl.ds(start, cols)]
+
+    return pl.pallas_call(
+        kernel,
+        out_shape=jax.ShapeDtypeStruct((total, width // 2), values.dtype),
+        in_specs=[VMEM],
+        out_specs=VMEM,
+        cost_estimate=pl.CostEstimate(flops=0, bytes_accessed=2**22, transcendentals=0),
+        name="pick_half",
+    )(values)
+
+
+def roll_half(values):
+    return pltpu.roll(values, values.shape[1] // 2, 1)
+
+
+def allowed_keys(first_ref, last_ref, span, places):
+    return (places >= first_ref[span, :]) & (places <= last_ref[span, :])
+
+
+def attend(projected, scales, gains, cosine, sine_part, first, last, places, cols):
+    total = projected.shape[0]
+    head_dim = cosine.shape[1]
+    heads = cols // head_dim
+    size = math.gcd(total, 256)
+    score_scale = head_dim ** (-0.5)
+    f32, bf16 = jnp.float32, jnp.bfloat16
+
+    def kernel(
+        lin_ref,
+        scales_ref,
+        gains_ref,
+        cos_ref,
+        sin_ref,
+        first_ref,
+        last_ref,
+        places_ref,
+        low_ref,
+        attended_ref,
+        attended_low_ref,
+        top_ref,
+    ):
+        for kind in range(3):
+            for h in range(heads):
+                span = pl.ds(kind * cols + h * head_dim, head_dim)
+                values = lin_ref[:, span]
+                if kind < 2:
+                    values = values * scales_ref[:, kind : kind + 1] * gains_ref[:, span]
+                    values = values * cos_ref[...] + roll_half(values) * sin_ref[...]
+                low_ref[:, span] = values.astype(bf16)
+        for h in range(heads):
+            head = pl.ds(h * head_dim, head_dim)
+            keys = low_ref[:, pl.ds(cols + h * head_dim, head_dim)]
+            values = low_ref[:, pl.ds(2 * cols + h * head_dim, head_dim)]
+
+            def step(b, carry):
+                span = pl.ds(pl.multiple_of(b * size, size), size)
+                scores = lax.dot_general(
+                    low_ref[span, head],
+                    keys,
+                    (((1,), (1,)), ((), ())),
+                    preferred_element_type=f32,
+                )
+                allowed = allowed_keys(first_ref, last_ref, span, places_ref[...])
+                scores = jnp.where(allowed, scores * score_scale, MASKED)
+                top = jnp.max(scores, axis=1, keepdims=True)
+                weights = jnp.exp(scores - top)
+                sums = jnp.sum(weights, axis=1, keepdims=True)
+                probs = (weights * (1.0 / sums)).astype(bf16)
+                attended = jnp.dot(probs, values, preferred_element_type=f32)
+                attended_ref[span, head] = attended
+                attended_low_ref[span, head] = attended.astype(bf16)
+                top_ref[span, head] = jnp.broadcast_to(top + jnp.log(sums), (size, head_dim))
+                return carry
+
+            lax.fori_loop(0, total // size, step, 0)
+
+    return pl.pallas_call(
+        kernel,
+        out_shape=[
+            jax.ShapeDtypeStruct((total, 3 * cols), bf16),
+            jax.ShapeDtypeStruct((total, cols), f32),
+            jax.ShapeDtypeStruct((total, cols), bf16),
+            jax.ShapeDtypeStruct((total, cols), f32),
+        ],
+        in_specs=[VMEM] * 8,
+        out_specs=[VMEM] * 4,
+        compiler_params=pltpu.CompilerParams(vmem_limit_bytes=56 * 2**20),
+        cost_estimate=pl.CostEstimate(
+            flops=2 * 10**9, bytes_accessed=20 * 2**20, transcendentals=2 * 10**6
+        ),
+        name="attend",
+    )(projected, scales, gains, cosine, sine_part, first, last, places)
+
+
+def attend_back(
+    output_grad, low, attended, top, projected, scales, gains, cosine, sine_part, first, last, places
+):
+    total, cols = output_grad.shape
+    head_dim = cosine.shape[1]
+    heads = cols // head_dim
+    size = math.gcd(total, 256)
+    score_scale = head_dim ** (-0.5)
+    f32, bf16 = jnp.float32, jnp.bfloat16
+    contract_rows = (((0,), (0,)), ((), ()))
+
+    def kernel(
+        grad_ref,
+        low_ref,
+        attended_ref,
+        top_ref,
+        lin_ref,
+        scales_ref,
+        gains_ref,
+        cos_ref,
+        sin_ref,
+        first_ref,
+        last_ref,
+        places_ref,
+        back_ref,
+        value_ref,
+        gain_ref,
+        sums_ref,
+        query_grad,
+        key_grad,
+        value_grad,
+    ):
+        totals = [jnp.zeros((total, 1), f32) for _ in range(2)]
+        for h in range(heads):
+            head = pl.ds(h * head_dim, head_dim)
+            keys = low_ref[:, pl.ds(cols + h * head_dim, head_dim)]
+            values = low_ref[:, pl.ds(2 * cols + h * head_dim, head_dim)]
+            key_grad[...] = jnp.zeros_like(key_grad)
+            value_grad[...] = jnp.zeros_like(value_grad)
+
+            def step(b, carry):
+                span = pl.ds(pl.multiple_of(b * size, size), size)
+                queries, grads = low_ref[span, head], grad_ref[span, head]
+                scores = lax.dot_general(
+                    queries, keys, (((1,), (1,)), ((), ())), preferred_element_type=f32
+                )
+                allowed = allowed_keys(first_ref, last_ref, span, places_ref[...])
+                scores = jnp.where(allowed, scores * score_scale, MASKED)
+                probs = jnp.exp(scores - top_ref[span, head][:, :1])
+                prob_grad = lax.dot_general(
+                    grads, values, (((1,), (1,)), ((), ())), preferred_element_type=f32
+                )
+                delta = jnp.sum(
+                    grads.astype(f32) * attended_ref[span, head], axis=1, keepdims=True
+                )
+                score_grad = (probs * (prob_grad - delta)).astype(bf16)
+                query_grad[span, :] = (
+                    jnp.dot(score_grad, keys, preferred_element_type=f32) * score_scale
+                )
+                key_grad[...] += lax.dot_general(
+                    score_grad, queries, contract_rows, preferred_element_type=f32
+                )
+                value_grad[...] += lax.dot_general(
+                    probs.astype(bf16), grads, contract_rows, preferred_element_type=f32
+                )
+                return carry
+
+            lax.fori_loop(0, total // size, step, 0)
+            value_ref[:, head] = value_grad[...].astype(bf16)
+            for kind, grad in ((0, query_grad[...]), (1, key_grad[...] * score_scale)):
+                span = pl.ds(kind * cols + h * head_dim, head_dim)
+                unit = lin_ref[:, span] * scales_ref[:, kind : kind + 1]
+                grad = grad * cos_ref[...] - roll_half(grad) * sin_ref[...]
+                gain_ref[kind, :, head] = jnp.sum(grad * unit, axis=0, keepdims=True)
+                grad = grad * gains_ref[:, span]
+                back_ref[kind, :, head] = grad
+                totals[kind] = totals[kind] + jnp.sum(grad * unit, axis=1, keepdims=True)
+        for kind in range(2):
+            sums_ref[:, kind : kind + 1] = totals[kind]
+
+    return pl.pallas_call(
+        kernel,
+        out_shape=[
+            jax.ShapeDtypeStruct((2, total, cols), f32),
+            jax.ShapeDtypeStruct((total, cols), bf16),
+            jax.ShapeDtypeStruct((2, 1, cols), f32),
+            jax.ShapeDtypeStruct((total, 2), f32),
+        ],
+        in_specs=[VMEM] * 12,
+        out_specs=[VMEM] * 4,
+        scratch_shapes=[pltpu.VMEM((total, head_dim), f32)] * 3,
+        compiler_params=pltpu.CompilerParams(vmem_limit_bytes=56 * 2**20),
+        cost_estimate=pl.CostEstimate(flops=0, bytes_accessed=2**20, transcendentals=0),
+        name="attend_back",
+    )(
+        output_grad,
+        low,
+        attended,
+        top,
+        projected,
+        scales,
+        gains,
+        cosine,
+        sine_part,
+        first,
+        last,
+        places,
+    )
+
+
 def on_device_heads(
     tokens,
     doc_lengths,
@@ -884,11 +1466,9 @@
     ctx, fsdp = lax.axis_size("ctx"), lax.axis_size("fsdp")
     me = lax.axis_index("ctx")
     head_dim = width // HEADS
-    heads = HEADS // ctx
-    cols = heads * head_dim
+    cols = HEADS // ctx * head_dim
     part = width // fsdp
     total = rows * ctx
-    score_scale = head_dim ** (-0.5)
     lengths = doc_lengths[0]
     bf16, f32 = jnp.bfloat16, jnp.float32
 
@@ -913,180 +1493,109 @@
     stream_pos = dealt_position(jnp.arange(total, dtype=jnp.int32), rows, ctx)
     stream_doc, stream_inner = document_info(stream_pos, lengths)
     cosine, sine_part = rope_tables(stream_inner, head_dim)
+    turn_tables = (
+        jnp.concatenate([cosine, cosine], axis=1),
+        jnp.concatenate([-sine_part, sine_part], axis=1),
+    )
+    sight = (
+        (stream_pos - stream_inner).reshape(total, 1),
+        stream_pos.reshape(total, 1),
+        stream_pos.reshape(1, total),
+    )
     inputs_all = tokens_all.astype(f32)
     unit_all = inputs_all * rms_unit(inputs_all)
     normed_all = (unit_all * gain_one).astype(bf16)
     projected = dot32("td,de->te", normed_all, qkv_weight)
-    query_lin, key_lin = projected[:, :cols], projected[:, cols : 2 * cols]
-    value_low = projected[:, 2 * cols :].astype(bf16).reshape(total, heads, head_dim)
-    squares = jnp.stack(
-        [jnp.sum(query_lin * query_lin, axis=1), jnp.sum(key_lin * key_lin, axis=1)]
-    )
+    squares = jnp.sum((projected * projected)[:, : 2 * cols].reshape(total, 2, cols), axis=2).T
     squares = ctx_sum(squares.reshape(-1, 128), 1).reshape(2, total)
-    scales = lax.rsqrt(squares / width + EPSILON)
-    own_gain_query = lax.dynamic_slice_in_dim(gain_query, me * cols, cols, 0)
-    own_gain_key = lax.dynamic_slice_in_dim(gain_key, me * cols, cols, 0)
-    query_unit = query_lin * scales[0][:, None]
-    key_unit = key_lin * scales[1][:, None]
-
-    def by_head(values):
-        return values.reshape(total, heads, head_dim)
-
-    query_low = turn(by_head(query_unit * own_gain_query), cosine, sine_part).astype(bf16)
-    key_low = turn(by_head(key_unit * own_gain_key), cosine, sine_part).astype(bf16)
-    scores = masked_scores(
-        query_low, key_low, stream_pos, stream_doc, stream_pos, stream_doc, score_scale
-    )
-    weights = jnp.exp(scores - jnp.max(scores, axis=-1, keepdims=True))
-    probs = weights / jnp.sum(weights, axis=-1, keepdims=True)
-    prob_low = probs.astype(bf16)
-    attended = dot32("hqk,khd->qhd", prob_low, value_low)
-
-    attended_part = heads_to_rows(attended.reshape(total, cols).astype(bf16), 2)
+    scales = lax.rsqrt(squares / width + EPSILON).T
+    own_gains = [
+        lax.dynamic_slice_in_dim(gain, me * cols, cols, 0) for gain in (gain_query, gain_key)
+    ]
+    own_gains = jnp.concatenate(own_gains).reshape(1, 2 * cols)
+    low, attended, attended_low, tops = attend(
+        projected, scales, own_gains, *turn_tables, *sight, cols
+    )
+
+    attended_part = heads_to_rows(attended_low, 2)
     mixed_part = dot32("td,de->te", attended_part, w_out).astype(bf16)
     inputs = tokens[0].astype(f32)
-    mixed = inputs + lax.psum_scatter(
-        mixed_part, "fsdp", scatter_dimension=0, tiled=True
-    ).astype(f32)
-    scale_two = rms_unit(mixed)
-    unit_two = mixed * scale_two
-    normed_two = (unit_two * gain_two).astype(bf16)
-    group = lax.all_gather(normed_two, "fsdp", axis=0, tiled=True)
+    row_gain_two = gain_two.reshape(1, width)
+    group, mixed = reduce_then_gather(
+        mixed_part,
+        [tokens[0], row_gain_two],
+        [jax.ShapeDtypeStruct((rows, width), f32)],
+        norm_chunk,
+        "mix_and_norm",
+        6,
+    )
 
     experts = w_gate.shape[0]
     top = routes.shape[2]
     capacity = rows * top // experts
     expert_ids = jnp.arange(experts, dtype=jnp.int32)
-
-    def spread_of(pairs):
-        slots = jax.vmap(slot_of_pairs)(pairs[:, 0], pairs[:, 1])
-        chosen = pairs[:, 0][:, :, :, None] == expert_ids
-        slot_by_expert = jnp.sum(jnp.where(chosen, slots[..., None] + 1, 0), axis=2) - 1
-        return (
-            slot_by_expert.transpose(0, 2, 1)[:, :, None, :]
-            == jnp.arange(capacity, dtype=jnp.int32)[None, None, :, None]
-        )
-
-    spread = spread_of(pairs_all)
-    disp = spread.astype(bf16).reshape(fsdp, experts * capacity, rows)
-    logits = dot32("td,ed->te", group, router_weight)
-    router_probs = jax.nn.softmax(logits, axis=-1).reshape(fsdp, rows, experts)
-    slot_gate_value = jnp.sum(
-        jnp.where(spread, router_probs.transpose(0, 2, 1)[:, :, None, :], 0.0), axis=-1
-    )
-    slot_gate_value = slot_gate_value.transpose(1, 0, 2).reshape(experts, fsdp * capacity)
-
-    def dispatch(values):
-        picked = dot32("bst,btd->bsd", disp, values.reshape(fsdp, rows, width)).astype(bf16)
-        picked = picked.reshape(fsdp, experts, capacity, width).transpose(1, 0, 2, 3)
-        return picked.reshape(experts, fsdp * capacity, width)
-
-    def combine(values):
-        values = values.reshape(experts, fsdp, capacity, width).transpose(1, 0, 2, 3)
-        return dot32("bst,bsd->btd", disp, values.reshape(fsdp, experts * capacity, width))
-
-    expert_in = dispatch(group)
-    gate_pre = dot32("ecd,edh->ech", expert_in, w_gate)
-    up_pre = dot32("ecd,edh->ech", expert_in, w_up)
-    hidden = (jax.nn.silu(gate_pre) * up_pre).astype(bf16)
-    expert_out = dot32("ech,ehd->ecd", hidden, w_down) * slot_gate_value[..., None]
-    moved = lax.psum_scatter(
-        combine(expert_out.astype(bf16)).reshape(fsdp * rows, width).astype(bf16),
-        "fsdp",
-        scatter_dimension=0,
-        tiled=True,
-    )
+    slots = jax.vmap(slot_of_pairs)(pairs_all[:, 0], pairs_all[:, 1])
+    chosen = pairs_all[:, 0][:, :, :, None] == expert_ids
+    slot_by_expert = jnp.sum(jnp.where(chosen, slots[..., None] + 1, 0), axis=2) - 1
+    slot_by_expert = jnp.pad(
+        slot_by_expert.reshape(fsdp * rows, experts).T,
+        ((0, ROUTER_ROWS - experts), (0, 0)),
+        constant_values=-1,
+    )
+    router_rows = jnp.pad(router_weight, ((0, ROUTER_ROWS - experts), (0, 0)))
+    moved_part, group_grad, g_router, slot_pack = run_experts(
+        group, dy_all, slot_by_expert, router_rows, w_gate, w_up, w_down, fsdp, capacity
+    )
+    moved = lax.psum_scatter(moved_part, "fsdp", scatter_dimension=0, tiled=True)
     activations = (mixed + moved.astype(f32)).astype(bf16)
 
-    slot_dy = dispatch(dy_all)
-    raw_grad = dot32("ecd,ehd->ech", slot_dy, w_down)
-    slot_gate_grad = jnp.sum(hidden.astype(f32) * raw_grad, axis=-1)
-    hidden_grad = raw_grad * slot_gate_value[..., None]
-    gate_low, up_low = silu_parts(hidden_grad, gate_pre, up_pre)
-    in_grad = dot32("ech,edh->ecd", gate_low, w_gate) + dot32("ech,edh->ecd", up_low, w_up)
-    scaled_hidden = (hidden.astype(f32) * slot_gate_value[..., None]).astype(bf16)
-
-    def both(values):
-        return jnp.concatenate([values, swap(values, "ctx", 1)], axis=1)
-
-    def half(values, which):
-        values = values.reshape(-1, ctx // 2, 2, cols)
-        return lax.dynamic_index_in_dim(values, which, 2, keepdims=False).reshape(-1, width // 2)
-
-    def half_of_both(values):
-        other = swap(half(values, 1 - me % 2), "ctx", 1)
-        values = jnp.concatenate([half(values, me % 2), other], axis=0)
-        picked = dot32("bst,btd->bsd", disp_both, values.reshape(2 * fsdp, rows, width // 2))
-        picked = picked.astype(bf16).reshape(2 * fsdp, experts, capacity, width // 2)
-        return picked.transpose(1, 0, 2, 3).reshape(experts, 2 * fsdp * capacity, width // 2)
-
-    disp_both = jnp.concatenate(
-        [disp, spread_of(swap(pairs_all, "ctx", 1)).astype(bf16).reshape(disp.shape)], axis=0
+    packed = expert_grads(
+        slot_pack,
+        swap(slot_pack, "ctx", 1),
+        pick_half(group, 0),
+        swap(pick_half(group, 1), "ctx", 1),
+        pick_half(dy_all, 0),
+        swap(pick_half(dy_all, 1), "ctx", 1),
+        slot_by_expert,
+        swap(slot_by_expert, "ctx", 1),
+        fsdp,
+        capacity,
     )
     high_bits = [2**i for i in range(1, ctx.bit_length() - 1)]
-    half_in, half_dy = half_of_both(group), half_of_both(dy_all)
-    down_parts = scatter_sum(
-        dot32("ech,ecd->ehd", both(scaled_hidden), half_dy).astype(bf16), 2, "ctx", high_bits
-    )
-    gate_parts = scatter_sum(
-        dot32("ecd,ech->edh", half_in, both(gate_low)).astype(bf16), 1, "ctx", high_bits
-    )
-    up_parts = scatter_sum(
-        dot32("ecd,ech->edh", half_in, both(up_low)).astype(bf16), 1, "ctx", high_bits
-    )
-    prob_grad = jnp.sum(
-        jnp.where(
-            spread,
-            slot_gate_grad.reshape(experts, fsdp, capacity).transpose(1, 0, 2)[..., None],
-            0.0,
-        ),
-        axis=2,
-    ).transpose(0, 2, 1)
-    logit_grad = (
-        router_probs * (prob_grad - jnp.sum(router_probs * prob_grad, axis=-1, keepdims=True))
-    ).reshape(fsdp * rows, experts).astype(bf16)
-    group_grad = combine(in_grad.astype(bf16)).reshape(fsdp * rows, width) + dot32(
-        "te,ed->td", logit_grad, router_weight
-    )
-    g_router = dot32("te,td->ed", logit_grad, group)
-    normed_two_grad = lax.psum_scatter(
-        group_grad.astype(bf16), "fsdp", scatter_dimension=0, tiled=True
-    ).astype(f32)
-    g_ffn_gain = jnp.sum(normed_two_grad * unit_two, axis=0)
-    pulled = normed_two_grad * gain_two
-    out_grad = cotangent[0].astype(f32)
-    mixed_grad = out_grad + scale_two * (
-        pulled - unit_two * jnp.mean(unit_two * pulled, axis=-1, keepdims=True)
-    )
-    mixed_all = lax.all_gather(mixed_grad.astype(bf16), "fsdp", axis=0, tiled=True)
+
+    mixed_all, mixed_grad, g_ffn_gain = reduce_then_gather(
+        group_grad,
+        [mixed, row_gain_two, cotangent[0]],
+        [jax.ShapeDtypeStruct((rows, width), f32), jax.ShapeDtypeStruct((1, width), f32)],
+        norm_back_chunk,
+        "norm_back",
+        7,
+    )
+    g_ffn_gain = g_ffn_gain[0]
     output_part = dot32("te,de->td", mixed_all, w_out).astype(bf16)
     g_out = dot32("td,te->de", attended_part, mixed_all).astype(bf16)
-    output_grad = by_head(rows_to_heads(output_part, 3))
-
-    row_delta = jnp.sum(output_grad.astype(f32) * attended, axis=-1).T
-    prob_grad_attn = dot32("qhd,khd->hqk", output_grad, value_low)
-    score_grad = (probs * (prob_grad_attn - row_delta[..., None])).astype(bf16)
-    query_grad = dot32("hqk,khd->qhd", score_grad, key_low) * score_scale
-    key_grad = dot32("hqk,qhd->khd", score_grad, query_low) * score_scale
-    value_grad = dot32("hqk,qhd->khd", prob_low, output_grad)
-    query_back = turn(query_grad, cosine, -sine_part).reshape(total, cols)
-    key_back = turn(key_grad, cosine, -sine_part).reshape(total, cols)
-    own_g_query = jnp.sum(query_back * query_unit, axis=0)
-    own_g_key = jnp.sum(key_back * key_unit, axis=0)
-    query_back = query_back * own_gain_query
-    key_back = key_back * own_gain_key
-    inner_sums = jnp.stack(
-        [jnp.sum(query_back * query_unit, axis=1), jnp.sum(key_back * key_unit, axis=1)]
-    )
-    inner_sums = ctx_sum(inner_sums.reshape(-1, 128), 1).reshape(2, total) / width
-    proj_grad = jnp.concatenate(
-        [
-            scales[0][:, None] * (query_back - query_unit * inner_sums[0][:, None]),
-            scales[1][:, None] * (key_back - key_unit * inner_sums[1][:, None]),
-            value_grad.reshape(total, cols),
-        ],
-        axis=1,
-    ).astype(bf16)
+    output_grad, packed = lax.optimization_barrier((rows_to_heads(output_part, 3), packed))
+
+    def finish(kind):
+        values = packed[kind, 1].astype(f32) + swap(packed[kind, 0], "ctx", 2).astype(f32)
+        for bit in high_bits[1:]:
+            left = values.shape[1] // 2
+            values = halved(values.reshape((experts, left, 2) + values.shape[2:]), 2, "ctx", bit)
+        return values[:, 0]
+
+    down_parts, gate_parts, up_parts = (finish(kind) for kind in range(3))
+
+    back, value_grad, own_g_gains, inner_sums = attend_back(
+        output_grad, low, attended, tops, projected, scales, own_gains, *turn_tables, *sight
+    )
+    inner_sums = ctx_sum(inner_sums.T.reshape(-1, 128), 1).reshape(2, total).T / width
+
+    def norm_back(kind):
+        scale = scales[:, kind : kind + 1]
+        unit = projected[:, kind * cols : (kind + 1) * cols] * scale
+        return (scale * (back[kind] - unit * inner_sums[:, kind : kind + 1])).astype(bf16)
+
+    proj_grad = jnp.concatenate([norm_back(0), norm_back(1), value_grad], axis=1)
     g_qkv = dot32("td,te->de", normed_all, proj_grad).astype(bf16)
     normed_grad_part = dot32("te,de->td", proj_grad, qkv_weight)
     g_attn_gain = jnp.sum(normed_grad_part * unit_all, axis=0)
@@ -1110,8 +1619,8 @@
 
     sums = jnp.concatenate(
         [
-            jnp.stack([g_attn_gain, placed_cols(own_g_query), placed_cols(own_g_key), g_ffn_gain]),
-            g_router,
+            jnp.stack([g_attn_gain, placed_cols(own_g_gains[0, 0]), placed_cols(own_g_gains[1, 0]), g_ffn_gain]),
+            g_router[:experts],
         ],
         axis=0,
     )
@@ -1165,7 +1674,7 @@
         P(None, "fsdp", "ctx"),
     )
     ctx, fsdp = mesh.shape["ctx"], mesh.shape["fsdp"]
-    by_heads = HEADS % ctx == 0 and ctx % fsdp == 0 and ctx & (ctx - 1) == 0 and fsdp == 4
+    by_heads = HEADS % ctx == 0 and ctx == 8 and fsdp == 4
     body = on_device_heads if by_heads else on_device
     return jax.shard_map(
         body, mesh=mesh, in_specs=in_specs, out_specs=out_specs, check_vma=False

time: 838 us -> 750 us (0.89)
  the two profiles are of different devices: /device:TPU:5 before, /device:TPU:3 now
where the time goes in v3:
time: 750 us; the launch traced here: 740 us
  Pallas kernels  417 us (56%)
  waiting for transfers between devices  150 us (20%)
  local copies, waits for them, and re-layouts  49.9 us (7%)
  other arithmetic  45.2 us (6%)
  matrix products  27 us (4%)
  starting transfers between devices  24.2 us (3%)
  between operations  15 us (2%)
  blocking collectives  10.9 us (1%)
    pallas_call x1, Pallas kernels, deal_columns(): comm_call(kernel, 'deal_columns', collective_id, jax.ShapeDtypeStruct(val...  104 us
    pallas_call x1, Pallas kernels, mesh_sum(): comm_call(kernel, 'mesh_sum', collective_id, jax.ShapeDtypeStruct((rows,...  101 us
    pallas_call x2, Pallas kernels, reduce_then_gather(): comm_call(kernel, name, collective_id, [jax.ShapeDtypeStruct(partial.shap...  70.3 us
    ppermute x15, waiting for transfers between devices, swap(): lax.ppermute(values, axis, [(i, i ^ bit) for i in range(lax.axis_size(axi...  69.8 us
    all_gather x1, waiting for transfers between devices, on_device_heads(): tokens_all = lax.all_gather(tokens[0], 'ctx', axis=0, tiled=True)  50.5 us
    pallas_call x1, Pallas kernels, rows_to_heads(): comm_call(kernel, 'rows_to_heads', collective_id, jax.ShapeDtypeStruct((c...  33.5 us
    all_gather x1, waiting for transfers between devices, on_device_heads(): qkv_weight = lax.all_gather(own_cols, 'fsdp', axis=0, tiled=True)  28.4 us
    dot_general x6, matrix products, dot32(): return jnp.einsum(spec, left, right, preferred_element_type=jnp.float32)  27 us
  transfers between devices with their start and end apart: 20, of which 6 were waited for; matrix products, arithmetic and copies ran while one was open for 15% of the time, Pallas kernels for 53%

profile of v3, /device:TPU:3, one launch (start us, length us, event | category | flops | bytes accessed | tf_op | source)
XLA Modules:
  0.0 739.7 jit_solution(13446664328201157299)
XLA Ops:
  11.8 5.7 all_gather.19
  18.7 5.2 all-gather.2
  29.0 1.9 fusion.45
  30.9 1.3 pad_maximum_fusion.4
  32.2 50.5 %all-gather.9.cloned.1.call-done = bf16[1,1024,2048]{2,1,0:T(8,128)(2,1)} async-done(((bf16[1,128,2048]{2,1,0:T(8,128)(2,1)}), bf16[1,1024,2048]{2,1,0:T(8,128)(2,1)}) %all-gather.9.cloned.1.call-update) | async-done | bytes 4194320 | tf_op jit(solution)/shard_map/all_gather | solution.py:1475
  82.7 3.1 fusion.4
  85.8 28.4 %all-gather.7.cloned.1.call-done = bf16[2048,768]{1,0:T(8,128)(2,1)} async-done(((bf16[512,768]{1,0:T(8,128)(2,1)}), bf16[2048,768]{1,0:T(8,128)(2,1)}) %all-gather.7.cloned.1.call-update) | async-done | bytes 3145744 | tf_op jit(solution)/shard_map/all_gather | solution.py:1489
  114.2 8.4 %fusion.9 = f32[1024,768]{0,1:T(8,128)} fusion(bf16[2048,768]{1,0:T(8,128)(2,1)} %all-gather.7.cloned.1.call-done, bf16[1,1024,2048]{2,1,0:T(8,128)(2,1)} %all-gather.9.cloned.1.call-done, f32[2048]{0:T(1024)S(1)} %bitcast.143, f32[1024]{0:T(1024)S(1)} %add_rsqrt_fusion.1), kind=kOutput, calls=%fused_computation.37 | convolution fusion | flops 3229614080 | bytes 10498048 | tf_op jit(solution)/shard_map/td,de->te/dot_general | solution.py:493
  122.6 3.9 copy.73.lin_ref
  126.5 1.8 bitcast_reduce_fusion
  128.3 6.2 ctx_sum.2
  135.6 12.0 %attend.1 = (bf16[1024,768]{1,0:T(8,128)(2,1)}, f32[1024,256]{1,0:T(8,128)}, bf16[1024,256]{1,0:T(8,128)(2,1)}, f32[1024,256]{1,0:T(8,128)}) custom-call(f32[1024,768]{1,0:T(8,128)} %copy.73.lin_ref, f32[1024,2]{1,0:T(8,128)} %bitcast.134, f32[1,512]{1,0:T(1,128)} %bitcast.154, f32[1024,128]{1,0:T(8,128)} %get-tuple-element.123.cos_ref, ...), custom_call_target="tpu_custom_call" | custom-call | flops 2000000000 | bytes 20971520 | tf_op jit(solution)/shard_map/attend/pallas_call | solution.py:1320
  148.7 13.8 %heads_to_rows.1 = bf16[512,512]{1,0:T(8,128)(2,1)S(1)} custom-call(bf16[1024,256]{1,0:T(8,128)(2,1)S(1)} %copy-done.12), custom_call_target="tpu_custom_call" | custom-call | bytes 41943040 | tf_op jit(solution)/shard_map/heads_to_rows/pallas_call | solution.py:693
  163.8 28.5 %mix_and_norm.1 = (bf16[512,2048]{1,0:T(8,128)(2,1)S(1)}, f32[128,2048]{1,0:T(8,128)S(1)}) custom-call(bf16[512,2048]{1,0:T(8,128)(2,1)S(1)} %convolution_convert_fusion.2.refs_0_, bf16[128,2048]{1,0:T(8,128)(2,1)S(1)} %bitcast.128, f32[1,2048]{1,0:T(1,128)S(1)} %get-tuple-element.105.refs_2_), custom_call_target="tpu_custom_call" | custom-call | bytes 104857600 | tf_op jit(solution)/shard_map/mix_and_norm/pallas_call | solution.py:916
  192.3 1.3 copy-done.3
  194.7 25.2 %run_experts.1 = (bf16[512,2048]{1,0:T(8,128)(2,1)}, bf16[512,2048]{1,0:T(8,128)(2,1)}, f32[16,2048]{1,0:T(8,128)}, bf16[3,6,256,256]{3,2,1,0:T(8,128)(2,1)}) custom-call(bf16[512,2048]{1,0:T(8,128)(2,1)} %copy-done.3, bf16[512,2048]{1,0:T(8,128)(2,1)} %bitcast.131, s32[16,512]{1,0:T(8,128)} %pad.12.slots_ref.slots_own_ref, ...), custom_call_target="tpu_custom_call" | custom-call | flops 30000001024 | bytes 31457280 | tf_op jit(solution)/shard_map/run_experts/pallas_call | solution.py:1108
  220.2 2.8 pick_half.7
  224.1 2.7 pick_half.5
  228.3 2.8 pick_half.6.dy_own_ref
  231.1 10.8 %reduce-scatter.5.cloned.1.call-start = ((), (), s32[]{:S(2)}) async-start(), calls=%async_computation.4 | async-start | bytes 4718592 | tf_op jit(solution)/shard_map/reduce_scatter | solution.py:1602
  242.0 1.3 copy-done.5
  243.3 41.8 %norm_back.1 = (bf16[512,2048]{1,0:T(8,128)(2,1)S(1)}, f32[128,2048]{1,0:T(8,128)S(1)}, f32[1,2048]{1,0:T(1,128)S(1)}) custom-call(bf16[512,2048]{1,0:T(8,128)(2,1)} %get-tuple-element.35.refs_0_, f32[128,2048]{1,0:T(8,128)S(1)} %copy-done.5, f32[1,2048]{1,0:T(1,128)S(1)} %get-tuple-element.105.refs_2_, bf16[128,2048]{1,0:T(8,128)(2,1)S(1)} %bitcast.130), custom_call_target="tpu_custom_call" | custom-call | bytes 104857600 | tf_op jit(solution)/shard_map/norm_back/pallas_call | solution.py:916
  285.1 2.6 convolution_convert_fusion.1
  287.7 1.3 convolution_convert_fusion.3.own_ref
  289.5 2.8 pick_half.4.in_own_ref
  292.4 2.8 reshape.309
  295.2 33.5 %rows_to_heads.1.grad_ref = bf16[1024,256]{1,0:T(8,128)(2,1)S(1)} custom-call(bf16[512,512]{1,0:T(8,128)(2,1)S(1)} %convolution_convert_fusion.3.own_ref), custom_call_target="tpu_custom_call" | custom-call | bytes 41943040 | tf_op jit(solution)/shard_map/rows_to_heads/pallas_call | solution.py:767
  330.1 14.8 %expert_grads.1 = bf16[3,2,6,2,256,256]{5,4,3,2,1,0:T(8,128)(2,1)} custom-call(bf16[3,6,256,256]{3,2,1,0:T(8,128)(2,1)} %get-tuple-element.38.own_ref, bf16[3,6,256,256]{3,2,1,0:T(8,128)(2,1)} %collective-permute-done.other_ref, bf16[512,1024]{1,0:T(8,128)(2,1)} %pick_half.4.in_own_ref, bf16[512,1024]{1,0:T(8,128)(2,1)} %collective-permute-done.1.in_other_ref, ...), custom_call_target="tpu_custom_call" | custom-call | flops 20000000000 | bytes 31457280 | tf_op jit(solution)/shard_map/expert_grads/pallas_call | solution.py:1214
  344.9 16.5 %attend_back.1 = (f32[2,1024,256]{2,1,0:T(8,128)}, bf16[1024,256]{1,0:T(8,128)(2,1)}, f32[2,1,256]{2,1,0:T(1,128)}, f32[1024,2]{1,0:T(8,128)}) custom-call(bf16[1024,256]{1,0:T(8,128)(2,1)} %copy-done.8, bf16[1024,768]{1,0:T(8,128)(2,1)} %get-tuple-element.40.low_ref, f32[1024,256]{1,0:T(8,128)} %get-tuple-element.41.attended_ref, ...), custom_call_target="tpu_custom_call" | custom-call | bytes 1048576 | tf_op jit(solution)/shard_map/attend_back/pallas_call | solution.py:1418
  362.7 9.3 %ctx_sum.3 = f32[16,128]{1,0:T(8,128)S(1)} custom-call(f32[16,128]{1,0:T(8,128)S(1)} %reshape.306.own_ref), custom_call_target="tpu_custom_call" | custom-call | bytes 20971520 | tf_op jit(solution)/shard_map/ctx_sum/pallas_call | solution.py:545
  372.1 2.8 fusion.24
  375.6 7.2 fusion.3
  382.9 1.6 copy-done.13
  384.4 5.6 constant_dynamic-slice_fusion.1
  390.1 1.3 copy.103
  391.4 34.6 %collective-permute-done.6 = bf16[512,2,2,256]{3,0,1,2:T(8,128)(2,1)} collective-permute-done((bf16[512,2,2,256]{3,0,1,2:T(8,128)(2,1)}, bf16[512,2,2,256]{3,0,1,2:T(8,128)(2,1)}, u32[]{:S(2)}, u32[]{:S(2)}) %collective-permute-start.6) | collective-permute-done | bytes 1048608 | tf_op jit(solution)/shard_map/ppermute | solution.py:832
  426.0 1.7 convert_add_fusion.4
  427.7 1.3 copy-done.22
  429.1 1.3 collective-permute-start.7
  430.6 13.6 %collective-permute-done.7 = bf16[512,2,256]{2,0,1:T(8,128)(2,1)S(1)} collective-permute-done((bf16[512,2,256]{2,0,1:T(8,128)(2,1)S(1)}, bf16[512,2,256]{2,0,1:T(8,128)(2,1)S(1)}, u32[]{:S(2)}, u32[]{:S(2)}) %collective-permute-start.7) | collective-permute-done | bytes 524320 | tf_op jit(solution)/shard_map/ppermute | solution.py:832
  444.2 2.3 bitcast_add_fusion.1
  446.5 6.3 convolution_convert_fusion
  452.8 1.4 constant_dynamic-slice_fusion.3
  454.2 1.6 copy.87
  458.8 4.6 slice_bitcast_fusion
  465.9 17.9 %collective-permute-done.8 = bf16[512,256]{1,0:T(8,128)(2,1)S(1)} collective-permute-done((bf16[512,256]{1,0:T(8,128)(2,1)S(1)}, bf16[512,256]{1,0:T(8,128)(2,1)S(1)}, u32[]{:S(2)}, u32[]{:S(2)}) %collective-permute-start.8) | collective-permute-done | bytes 262176 | tf_op jit(solution)/shard_map/ppermute | solution.py:832
  484.7 1.7 copy.95
  486.9 100.9 %mesh_sum.1 = f32[16,512]{1,0:T(8,128)S(1)} custom-call(f32[16,2048]{1,0:T(8,128)S(1)} %pad.14.own_ref), custom_call_target="tpu_custom_call" | custom-call | bytes 31457280 | tf_op jit(solution)/shard_map/mesh_sum/pallas_call | solution.py:600
  589.1 1.9 convert_add_fusion.3
  591.1 1.3 collective-permute-start.5
  592.7 5.7 convert_add_fusion
  601.6 1.8 collective-permute-start.12
  604.1 1.9 fusion.42
  606.1 3.7 collective-permute-done.5
  609.8 1.9 fusion.5
  611.9 103.5 %deal_columns.1 = bf16[3,512,256]{2,1,0:T(8,128)(2,1)S(1)} custom-call(bf16[3,512,256]{2,1,0:T(8,128)(2,1)S(1)} %bitcast.129), custom_call_target="tpu_custom_call" | custom-call | bytes 41943040 | tf_op jit(solution)/shard_map/deal_columns/pallas_call | solution.py:819
  715.5 1.3 convert_bitcast_fusion
  716.8 1.9 copy.89
  718.6 1.6 copy.92
  720.3 3.1 add_bitcast_fusion.2
  723.4 2.6 add_bitcast_fusion.1
  726.0 2.6 add_bitcast_fusion
  728.6 1.4 fusion.11
  730.0 2.7 fusion.15
  (182 shorter events, 34.9 us)
Async XLA Ops:
  7.2 155.3 %copy-start = (bf16[512,2048]{1,0:T(8,128)(2,1)S(1)}, bf16[512,2048]{1,0:T(8,128)(2,1)}, u32[]{:S(2)}) copy-start(bf16[512,2048]{1,0:T(8,128)(2,1)} %param.23) | copy-start | bytes 6291460
  7.2 75.5 %all-gather.9.cloned.1.call-start = ((), (), s32[]{:S(2)}) async-start(), calls=%async_computation.5 | async-start | bytes 4718592 | tf_op jit(solution)/shard_map/all_gather | solution.py:1475
  7.9 106.3 %all-gather.7.cloned.1.call-start = ((), (), s32[]{:S(2)}) async-start(), calls=%async_computation.2 | async-start | bytes 3932160 | tf_op jit(solution)/shard_map/all_gather | solution.py:1489
  8.0 3.6 copy-start.34
  8.0 3.6 copy-start.35
  8.0 3.7 copy-start.36
  8.0 3.7 copy-start.37
  8.0 3.7 copy-start.30
  9.2 9.3 %copy-start.38 = (s32[1,16]{1,0:T(1,128)S(1)}, s32[1,16]{1,0:T(1,128)}, u32[]{:S(2)}) copy-start(s32[1,16]{1,0:T(1,128)} %param.16) | copy-start | bytes 196
  9.2 9.4 %copy-start.32 = (s32[1,128,3]{1,0,2:T(1,128)S(1)}, s32[1,128,3]{1,0,2:T(1,128)}, u32[]{:S(2)}) copy-start(s32[1,128,3]{1,0,2:T(1,128)} %param.17) | copy-start | bytes 4612
  9.3 9.4 %copy-start.33 = (s32[1,128,3]{1,0,2:T(1,128)S(1)}, s32[1,128,3]{1,0,2:T(1,128)}, u32[]{:S(2)}) copy-start(s32[1,128,3]{1,0,2:T(1,128)} %param.18) | copy-start | bytes 4612
  10.2 184.4 %all-gather.11.cloned.1.call-start = ((), (), s32[]{:S(2)}) async-start(), calls=%async_computation.6 | async-start | bytes 2621440 | tf_op jit(solution)/shard_map/all_gather | solution.py:1490
  11.0 593.2 %reduce-scatter.3.cloned.1.call-start = ((), (), s32[]{:S(2)}) async-start(), calls=%async_computation.3 | async-start | bytes 2621440 | tf_op jit(solution)/shard_map/reduce_scatter | solution.py:1549
  147.6 1.0 copy-start.12
  162.5 1.3 copy-start.10
  162.5 1.3 copy-start.2
  192.3 1.3 copy-start.3
  193.7 1.0 copy-start.4
  219.9 109.7 %collective-permute-start = (bf16[3,6,256,256]{3,2,1,0:T(8,128)(2,1)}, bf16[3,6,256,256]{3,2,1,0:T(8,128)(2,1)}, u32[]{:S(2)}, u32[]{:S(2)}) collective-permute-start(bf16[3,6,256,256]{3,2,1,0:T(8,128)(2,1)} %get-tuple-element.38.own_ref), channel_id=1, source_target_pairs={{0,4},{4,0},{8,12},{12,8},{16,20},{20,16},{24,28},{28,24},{1,5},{5... | collective-permute-start | bytes 7077896 | tf_op jit(solution)/shard_map/ppermute | solution.py:832
  223.0 4.2 copy-start.28
  223.0 106.5 %collective-permute-start.2 = (bf16[512,1024]{1,0:T(8,128)(2,1)}, bf16[512,1024]{1,0:T(8,128)(2,1)}, u32[]{:S(2)}, u32[]{:S(2)}) collective-permute-start(bf16[512,1024]{1,0:T(8,128)(2,1)} %pick_half.7), channel_id=1, source_target_pairs={{0,4},{4,0},{8,12},{12,8},{16,20},{20,16},{24,28},{28,24},{1,5},{5... | collective-permute-start | bytes 3145736 | tf_op jit(solution)/shard_map/ppermute | solution.py:832
  226.8 102.7 %collective-permute-start.1 = (bf16[512,1024]{1,0:T(8,128)(2,1)}, bf16[512,1024]{1,0:T(8,128)(2,1)}, u32[]{:S(2)}, u32[]{:S(2)}) collective-permute-start(bf16[512,1024]{1,0:T(8,128)(2,1)} %pick_half.5), channel_id=1, source_target_pairs={{0,4},{4,0},{8,12},{12,8},{16,20},{20,16},{24,28},{28,24},{1,5},{5... | collective-permute-start | bytes 3145736 | tf_op jit(solution)/shard_map/ppermute | solution.py:832
  227.2 102.3 %collective-permute-start.3 = (s32[16,512]{1,0:T(8,128)S(1)}, s32[16,512]{1,0:T(8,128)S(1)}, u32[]{:S(2)}, u32[]{:S(2)}) collective-permute-start(s32[16,512]{1,0:T(8,128)S(1)} %copy-done.28), channel_id=1, source_target_pairs={{0,4},{4,0},{8,12},{12,8},{16,20},{20,16},{24,28},{28,24},{1,5},{5... | collective-permute-start | bytes 98312 | tf_op jit(solution)/shard_map/ppermute | solution.py:832
  228.3 13.6 %copy-start.7 = (bf16[1,128,2048]{2,1,0:T(8,128)(2,1)S(1)}, bf16[1,128,2048]{2,1,0:T(8,128)(2,1)}, u32[]{:S(2)}) copy-start(bf16[1,128,2048]{2,1,0:T(8,128)(2,1)} %param.29) | copy-start | bytes 1572868
  231.1 497.5 %reduce-scatter.5.cloned.1.call-start = ((), (), s32[]{:S(2)}) async-start(), calls=%async_computation.4 | async-start | bytes 4718592 | tf_op jit(solution)/shard_map/reduce_scatter | solution.py:1602
  242.0 1.4 copy-start.5
  243.3 41.8 %copy-start.11 = (bf16[512,512]{1,0:T(8,128)(2,1)S(1)}, bf16[512,512]{1,0:T(8,128)(2,1)}, u32[]{:S(2)}) copy-start(bf16[512,512]{1,0:T(8,128)(2,1)} %copy-done.10) | copy-start | bytes 1572868
  285.1 2.6 copy-start.9
  287.7 1.3 copy-start.21
  289.0 3.3 copy-start.25
  328.7 0.8 copy-start.8
  329.5 0.6 copy-start.40
  372.1 3.5 copy-start.23
  372.1 3.6 copy-start.39
  374.8 8.0 %copy-start.26 = (bf16[1024,256]{1,0:T(8,128)(2,1)}, bf16[1024,256]{1,0:T(8,128)(2,1)S(1)}, u32[]{:S(2)}) copy-start(bf16[1024,256]{1,0:T(8,128)(2,1)S(1)} %get-tuple-element.100) | copy-start | bytes 1572868
  382.8 1.6 copy-start.13
  390.1 35.9 %copy-start.20 = (bf16[512,2,2,1,256]{4,3,2,1,0:T(2,128)(2,1)S(1)}, bf16[512,2,2,1,256]{4,3,2,1,0:T(2,128)(2,1)}, u32[]{:S(2)}) copy-start(bf16[512,2,2,1,256]{4,3,2,1,0:T(2,128)(2,1)} %get-tuple-element.103) | copy-start | bytes 3145732
  391.4 34.6 %collective-permute-start.6 = (bf16[512,2,2,256]{3,0,1,2:T(8,128)(2,1)}, bf16[512,2,2,256]{3,0,1,2:T(8,128)(2,1)}, u32[]{:S(2)}, u32[]{:S(2)}) collective-permute-start(bf16[512,2,2,256]{3,0,1,2:T(8,128)(2,1)} %bitcast.125), channel_id=1, source_target_pairs={{0,4},{4,0},{8,12},{12,8},{16,20},{20,16},{24,28},{28,24},{1,5},{5... | collective-permute-start | bytes 3145736 | tf_op jit(solution)/shard_map/ppermute | solution.py:832
  426.0 4.6 copy-start.29
  427.7 1.3 copy-start.22
  429.0 17.5 %copy-start.27 = (bf16[1024,256]{1,0:T(8,128)(2,1)S(1)}, bf16[1024,256]{1,0:T(8,128)(2,1)}, u32[]{:S(2)}) copy-start(bf16[1024,256]{1,0:T(8,128)(2,1)} %copy-done.26) | copy-start | bytes 1572868
  429.1 15.2 %collective-permute-start.7 = (bf16[512,2,256]{2,0,1:T(8,128)(2,1)S(1)}, bf16[512,2,256]{2,0,1:T(8,128)(2,1)S(1)}, u32[]{:S(2)}, u32[]{:S(2)}) collective-permute-start(bf16[512,2,256]{2,0,1:T(8,128)(2,1)S(1)} %fusion.43), channel_id=1, source_target_pairs={{0,8},{4,12},{8,0},{12,4},{16,24},{20,28},{24,16},{28,20},{1,9},{5... | collective-permute-start | bytes 1572872 | tf_op jit(solution)/shard_map/ppermute | solution.py:832
  455.7 133.3 %collective-permute-start.4 = (bf16[2,512,768]{1,2,0:T(8,128)(2,1)}, bf16[2,512,768]{1,2,0:T(8,128)(2,1)}, u32[]{:S(2)}, u32[]{:S(2)}) collective-permute-start(bf16[2,512,768]{1,2,0:T(8,128)(2,1)} %bitcast.141), channel_id=1, source_target_pairs={{0,1},{1,0},{2,3},{3,2},{4,5},{5,4},{6,7},{7,6},{8,9},{9,8},{10,11... | collective-permute-start | bytes 4718600 | tf_op jit(solution)/shard_map/ppermute | solution.py:832
  457.7 26.1 %copy-start.24 = (f32[512,2,256]{2,0,1:T(8,128)S(1)}, f32[512,2,256]{2,0,1:T(8,128)}, u32[]{:S(2)}) copy-start(f32[512,2,256]{2,0,1:T(8,128)} %bitcast_add_fusion.1) | copy-start | bytes 3145732
  457.8 26.1 %collective-permute-start.8 = (bf16[512,256]{1,0:T(8,128)(2,1)S(1)}, bf16[512,256]{1,0:T(8,128)(2,1)S(1)}, u32[]{:S(2)}, u32[]{:S(2)}) collective-permute-start(bf16[512,256]{1,0:T(8,128)(2,1)S(1)} %fusion.44), channel_id=1, source_target_pairs={{0,16},{4,20},{8,24},{12,28},{16,0},{20,4},{24,8},{28,12},{1,17},{... | collective-permute-start | bytes 786440 | tf_op jit(solution)/shard_map/ppermute | solution.py:832
  463.4 129.0 %collective-permute-start.13 = (bf16[6,2,256,256]{3,2,1,0:T(8,128)(2,1)}, bf16[6,2,256,256]{3,2,1,0:T(8,128)(2,1)}, u32[]{:S(2)}, u32[]{:S(2)}) collective-permute-start(bf16[6,2,256,256]{3,2,1,0:T(8,128)(2,1)} %get-tuple-element.91), channel_id=1, source_target_pairs={{0,8},{4,12},{8,0},{12,4},{16,24},{20,28},{24,16},{28,20},{1,9},{5... | collective-permute-start | bytes 4718600 | tf_op jit(solution)/shard_map/ppermute | solution.py:832
  464.5 128.0 %collective-permute-start.11 = (bf16[6,2,256,256]{3,2,1,0:T(8,128)(2,1)}, bf16[6,2,256,256]{3,2,1,0:T(8,128)(2,1)}, u32[]{:S(2)}, u32[]{:S(2)}) collective-permute-start(bf16[6,2,256,256]{3,2,1,0:T(8,128)(2,1)} %get-tuple-element.92), channel_id=1, source_target_pairs={{0,8},{4,12},{8,0},{12,4},{16,24},{20,28},{24,16},{28,20},{1,9},{5... | collective-permute-start | bytes 4718600 | tf_op jit(solution)/shard_map/ppermute | solution.py:832
  464.9 21.5 %copy-start.31 = (f32[2,1,256]{2,1,0:T(1,128)S(1)}, f32[2,1,256]{2,1,0:T(1,128)}, u32[]{:S(2)}) copy-start(f32[2,1,256]{2,1,0:T(1,128)} %get-tuple-element.46) | copy-start | bytes 6148
  464.9 127.8 %collective-permute-start.9 = (bf16[6,2,256,256]{3,2,1,0:T(8,128)(2,1)}, bf16[6,2,256,256]{3,2,1,0:T(8,128)(2,1)}, u32[]{:S(2)}, u32[]{:S(2)}) collective-permute-start(bf16[6,2,256,256]{3,2,1,0:T(8,128)(2,1)} %get-tuple-element.93), channel_id=1, source_target_pairs={{0,8},{4,12},{8,0},{12,4},{16,24},{20,28},{24,16},{28,20},{1,9},{5... | collective-permute-start | bytes 4718600 | tf_op jit(solution)/shard_map/ppermute | solution.py:832
  591.0 1.7 copy-start.19
  591.1 18.7 %collective-permute-start.5 = (bf16[512,768]{0,1:T(8,128)(2,1)S(1)}, bf16[512,768]{0,1:T(8,128)(2,1)}, u32[]{:S(2)}, u32[]{:S(2)}) collective-permute-start(bf16[512,768]{0,1:T(8,128)(2,1)S(1)} %fusion.29), channel_id=1, source_target_pairs={{0,2},{1,3},{2,0},{3,1},{4,6},{5,7},{6,4},{7,5},{8,10},{9,11},{10,... | collective-permute-start | bytes 2359304 | tf_op jit(solution)/shard_map/ppermute | solution.py:832
  598.4 1.9 copy-start.16
  598.4 3.2 copy-start.18
  598.4 5.1 copy-start.14
  598.4 5.7 copy-start.6
  599.4 120.8 %collective-permute-start.10 = (bf16[6,1,256,256]{3,2,1,0:T(8,128)(2,1)}, bf16[6,1,256,256]{3,2,1,0:T(8,128)(2,1)}, u32[]{:S(2)}, u32[]{:S(2)}) collective-permute-start(bf16[6,1,256,256]{3,2,1,0:T(8,128)(2,1)} %dynamic-slice_convert_fusion.2), channel_id=1, source_target_pairs={{0,16},{4,20},{8,24},{12,28},{16,0},{20,4},{24,8},{28,12},{1,17},{... | collective-permute-start | bytes 2359304 | tf_op jit(solution)/shard_map/ppermute | solution.py:832
  601.6 121.8 %collective-permute-start.12 = (bf16[6,1,256,256]{3,2,1,0:T(8,128)(2,1)}, bf16[6,1,256,256]{3,2,1,0:T(8,128)(2,1)}, u32[]{:S(2)}, u32[]{:S(2)}) collective-permute-start(bf16[6,1,256,256]{3,2,1,0:T(8,128)(2,1)} %dynamic-slice_convert_fusion.1), channel_id=1, source_target_pairs={{0,16},{4,20},{8,24},{12,28},{16,0},{20,4},{24,8},{28,12},{1,17},{... | collective-permute-start | bytes 2359304 | tf_op jit(solution)/shard_map/ppermute | solution.py:832
  603.5 122.5 %collective-permute-start.14 = (bf16[6,1,256,256]{3,2,1,0:T(8,128)(2,1)S(1)}, bf16[6,1,256,256]{3,2,1,0:T(8,128)(2,1)}, u32[]{:S(2)}, u32[]{:S(2)}) collective-permute-start(bf16[6,1,256,256]{3,2,1,0:T(8,128)(2,1)S(1)} %dynamic-slice_convert_fusion), channel_id=1, source_target_pairs={{0,16},{4,20},{8,24},{12,28},{16,0},{20,4},{24,8},{28,12},{1,17},{... | collective-permute-start | bytes 2359304 | tf_op jit(solution)/shard_map/ppermute | solution.py:832
  720.2 3.1 copy-start.17
  723.4 2.6 copy-start.15
  726.0 6.7 copy-start.1
Sparse Core Ops, SparseCore 0:
  10.2 72.5 all-gather.8
  84.8 29.2 all-gather.6
  115.8 22.5 all-gather.10
  231.3 46.6 reduce-scatter.2
  383.0 107.3 reduce-scatter.4

commit v4 on v3

--- a/solution.py
+++ b/solution.py
@@ -558,65 +558,6 @@
     )(values)
 
 
-def mesh_sum(values, collective_id):
-    ctx, fsdp = lax.axis_size("ctx"), lax.axis_size("fsdp")
-    rows, part = values.shape[0], values.shape[1] // fsdp
-
-    def kernel(own_ref, out_ref, parts, sums, held, part_send, part_recv, send_sems, recv_sems):
-        me, mine = lax.axis_index("ctx"), lax.axis_index("fsdp")
-        near = [lax.rem(mine + step, fsdp) for step in range(1, fsdp)]
-        peers = [(lax.rem(me + step, ctx), mine) for step in range(1, ctx)]
-        greet([(me, other) for other in near] + peers)
-
-        def columns(index):
-            return pl.ds(pl.multiple_of(index * part, part), part)
-
-        copies = [
-            send(
-                own_ref.at[:, columns(other)],
-                parts.at[i],
-                part_send.at[i],
-                part_recv.at[i],
-                (me, other),
-            )
-            for i, other in enumerate(near)
-        ]
-        total = own_ref[:, columns(mine)]
-        for i, copy in enumerate(copies):
-            copy.wait_recv()
-            total = total + parts[i]
-        sums[...] = total
-        wide = [
-            send(sums, held.at[i], send_sems.at[i], recv_sems.at[i], peer)
-            for i, peer in enumerate(peers)
-        ]
-        for i, copy in enumerate(wide):
-            copy.wait_recv()
-            total = total + held[i]
-        out_ref[...] = total
-        for copy in copies + wide:
-            copy.wait_send()
-
-    return comm_call(
-        kernel,
-        "mesh_sum",
-        collective_id,
-        jax.ShapeDtypeStruct((rows, part), values.dtype),
-        [VMEM],
-        VMEM,
-        [
-            pltpu.VMEM((fsdp - 1, rows, part), values.dtype),
-            pltpu.VMEM((rows, part), values.dtype),
-            pltpu.VMEM((ctx - 1, rows, part), values.dtype),
-            DMA((fsdp - 1,)),
-            DMA((fsdp - 1,)),
-            DMA((ctx - 1,)),
-            DMA((ctx - 1,)),
-        ],
-        30 * 2**20,
-    )(values)
-
-
 def heads_to_rows(values, collective_id):
     ctx, fsdp = lax.axis_size("ctx"), lax.axis_size("fsdp")
     rows, cols = values.shape[0] // ctx, values.shape[1]
@@ -776,78 +717,8 @@
     )(values)
 
 
-def deal_columns(values, collective_id):
-    ctx = lax.axis_size("ctx")
-    kinds = values.shape[0]
-
-    def kernel(own_ref, out_ref, send_sems, recv_sems):
-        me, mine = lax.axis_index("ctx"), lax.axis_index("fsdp")
-        greet([(lax.rem(me + step, ctx), mine) for step in range(1, ctx)])
-
-        def copy_to(kind):
-            index = kind * ctx + me
-            return pltpu.make_async_remote_copy(
-                own_ref.at[kind],
-                out_ref.at[lax.rem(index, kinds)],
-                send_sems.at[kind],
-                recv_sems.at[lax.rem(index, kinds)],
-                device_id=(index // kinds, mine),
-                device_id_type=MESH,
-            )
-
-        def keep(kind):
-            slot = lax.rem(kind * ctx + me, kinds)
-            return pltpu.make_async_copy(own_ref.at[kind], out_ref.at[slot], send_sems.at[kind])
-
-        def is_far(kind):
-            return (kind * ctx + me) // kinds != me
-
-        for kind in range(kinds):
-            pl.when(is_far(kind))(copy_to(kind).start)
-            pl.when(jnp.logical_not(is_far(kind)))(keep(kind).start)
-        for kind in range(kinds):
-            pl.when(is_far(kind))(copy_to(kind).wait_send)
-            pl.when(jnp.logical_not(is_far(kind)))(keep(kind).wait)
-        for slot in range(kinds):
-
-            @pl.when(lax.rem(me * kinds + slot, ctx) != me)
-            def _():
-                pltpu.make_async_copy(
-                    own_ref.at[slot], out_ref.at[slot], recv_sems.at[slot]
-                ).wait()
-
-    return comm_call(
-        kernel,
-        "deal_columns",
-        collective_id,
-        jax.ShapeDtypeStruct(values.shape, values.dtype),
-        [ANY],
-        ANY,
-        [DMA((kinds,)), DMA((kinds,))],
-        40 * 2**20,
-    )(values)
-
-
 def swap(values, axis, bit):
     return lax.ppermute(values, axis, [(i, i ^ bit) for i in range(lax.axis_size(axis))])
-
-
-def halved(values, dim, axis, bit):
-    own = (lax.axis_index(axis) // bit) % 2
-    given = lax.dynamic_index_in_dim(values, 1 - own, dim, keepdims=False).astype(jnp.bfloat16)
-    kept = lax.dynamic_index_in_dim(values, own, dim, keepdims=False)
-    return kept.astype(jnp.float32) + swap(given, axis, bit).astype(jnp.float32)
-
-
-def scatter_sum(values, dim, axis, bits):
-    count = len(bits)
-    shape = values.shape
-    values = values.reshape(
-        shape[:dim] + (2,) * count + (shape[dim] // 2**count,) + shape[dim + 1 :]
-    )
-    for left in range(count - 1, -1, -1):
-        values = halved(values, dim + left, axis, bits[count - 1 - left])
-    return values
 
 
 def reduce_then_gather(partial, extras, out_shapes, chunk_math, name, collective_id):
@@ -1445,6 +1316,331 @@
     )
 
 
+def flipped(index, bit):
+    return index + bit * (1 - 2 * lax.rem(index // bit, 2))
+
+
+def add_into(target, *sources):
+    step = target.shape[0] if len(target.shape) == 3 else target.shape[0] // 64
+
+    def body(i, carry):
+        span = i if len(target.shape) == 3 else pl.ds(pl.multiple_of(i * 64, 64), 64)
+        total = sources[0][span].astype(jnp.float32)
+        for source in sources[1:]:
+            total = total + source[span].astype(jnp.float32)
+        target[span] = total.astype(target.dtype)
+        return carry
+
+    lax.fori_loop(0, step, body, 0)
+
+
+def finish_sums(packed, normed_part, out_part, qkv_part, small, tokens, mixed_grad, gain, collective_id):
+    ctx, fsdp = lax.axis_size("ctx"), lax.axis_size("fsdp")
+    kinds, _, experts, _, units, cols = packed.shape
+    rows, width = tokens.shape
+    part = out_part.shape[0]
+    f32, bf16 = jnp.float32, jnp.bfloat16
+    small_rows, small_cols = small.shape[0], small.shape[1] // fsdp
+    copies_most = 64
+
+    def kernel(
+        packed_ref,
+        normed_ref,
+        g_out_ref,
+        g_qkv_ref,
+        small_ref,
+        tokens_ref,
+        mixed_ref,
+        gain_ref,
+        grads_ref,
+        input_ref,
+        out_ref,
+        qkv_ref,
+        sums_ref,
+        kept,
+        kept_low,
+        kept_high,
+        normed_own,
+        normed_x,
+        normed_low,
+        normed_high,
+        out_own,
+        out_x,
+        out_low,
+        out_high,
+        qkv_own,
+        qkv_core,
+        qkv_chip,
+        qkv_sum,
+        dealt,
+        small_parts,
+        small_sum,
+        small_held,
+        sends,
+        recvs,
+        locals_,
+        deal_sems,
+    ):
+        me, mine = lax.axis_index("ctx"), lax.axis_index("fsdp")
+        x, low, high = lax.rem(me, 2), lax.rem(me // 2, 2), me // 4
+        to_x, to_low, to_high = ((flipped(me, bit), mine) for bit in (1, 2, 4))
+        core, chip = flipped(mine, 1), flipped(mine, 2)
+        diagonal = flipped(core, 2)
+        ctx_peers = [(lax.rem(me + step, ctx), mine) for step in range(1, ctx)]
+        near = [lax.rem(mine + step, fsdp) for step in range(1, fsdp)]
+        greet(ctx_peers + [(me, other) for other in near])
+        used, used_local, all_sends, loads = [0], [0], [], {}
+
+        def push(source, target, peer):
+            i = used[0]
+            used[0] += 1
+            copy = send(source, target, sends.at[i], recvs.at[i], peer)
+            all_sends.append(copy)
+            return copy
+
+        def load(source, target):
+            i = used_local[0]
+            used_local[0] += 1
+            copy = pltpu.make_async_copy(source, target, locals_.at[i])
+            copy.start()
+            return copy
+
+        def normed_block(a, b, other):
+            side = 1 - x if other else x
+            block = (high + a - 2 * a * high) * 4 + (low + b - 2 * b * low) * 2 + side
+            return normed_ref.at[pl.ds(pl.multiple_of(block * rows, rows), rows), :]
+
+        def out_block(a, b, other):
+            side = 1 - x if other else x
+            block = (high + a - 2 * a * high) * 4 + (low + b - 2 * b * low) * 2 + side
+            return g_out_ref.at[:, pl.ds(pl.multiple_of(block * cols, cols), cols)]
+
+        def run(a):
+            return high + a - 2 * a * high
+
+        def qkv_block(index):
+            return g_qkv_ref.at[pl.ds(pl.multiple_of(index * part, part), part), :]
+
+        def columns(index):
+            return pl.ds(pl.multiple_of(index * small_cols, small_cols), small_cols)
+
+        order = ((1, 1), (0, 1), (1, 0), (0, 0))
+        small_copies = [
+            push(small_ref.at[:, columns(other)], small_parts.at[i], (me, other))
+            for i, other in enumerate(near)
+        ]
+        normed_copies = {
+            ab: push(normed_block(*ab, True), normed_x.at[ab[0], ab[1]], to_x) for ab in order
+        }
+
+        def push_low(kind, a):
+            return push(packed_ref.at[kind, 0, :, run(a)], kept_low.at[kind, a], to_low)
+
+        low_copies = {(0, a): push_low(0, a) for a in (1, 0)}
+        qkv_copies = [
+            push(qkv_block(diagonal), qkv_core.at[1], (me, core)),
+            push(qkv_block(core), qkv_core.at[0], (me, core)),
+        ]
+        qkv_loads = [
+            load(qkv_block(chip), qkv_own.at[1]),
+            load(qkv_block(mine), qkv_own.at[0]),
+        ]
+        normed_loads = {
+            ab: load(normed_block(*ab, False), normed_own.at[ab[0], ab[1]]) for ab in order
+        }
+        kept_loads = {
+            (kind, a): load(packed_ref.at[kind, 1, :, run(a)], kept.at[kind, a])
+            for kind in range(kinds)
+            for a in (1, 0)
+        }
+        out_loads = {ab: load(out_block(*ab, False), out_own.at[ab[0], ab[1]]) for ab in order}
+
+        total = small_ref[:, columns(mine)]
+        for i, copy in enumerate(small_copies):
+            copy.wait_recv()
+            total = total + small_parts[i]
+        small_sum[...] = total
+        small_wide = [push(small_sum, small_held.at[i], peer) for i, peer in enumerate(ctx_peers)]
+
+        qkv_copies[0].wait_recv()
+        qkv_loads[0].wait()
+        add_into(qkv_core.at[1], qkv_own.at[1], qkv_core.at[1])
+        chip_copy = push(qkv_core.at[1], qkv_chip, (me, chip))
+
+        def to_low_side(copies, loads, own, from_x, from_low, a):
+            copies[a, 1].wait_recv()
+            loads[a, 1].wait()
+            add_into(from_x.at[a, 1], own.at[a, 1], from_x.at[a, 1])
+            return push(from_x.at[a, 1], from_low.at[a], to_low)
+
+        def to_high_side(copies, loads, lows, own, from_x, from_low, from_high):
+            copies[1, 0].wait_recv()
+            loads[1, 0].wait()
+            lows[1].wait_recv()
+            add_into(from_x.at[1, 0], own.at[1, 0], from_x.at[1, 0], from_low.at[1])
+            return push(from_x.at[1, 0], from_high, to_high)
+
+        def experts_high(kind):
+            low_copies[kind, 1].wait_recv()
+            kept_loads[kind, 1].wait()
+            add_into(kept_low.at[kind, 1], kept.at[kind, 1], kept_low.at[kind, 1])
+            return push(kept_low.at[kind, 1], kept_high.at[kind], to_high)
+
+        normed_args = (normed_copies, normed_loads)
+        normed_lows = {1: to_low_side(*normed_args, normed_own, normed_x, normed_low, 1)}
+        high_copies = {0: experts_high(0)}
+        low_copies.update({(1, a): push_low(1, a) for a in (1, 0)})
+        normed_lows[0] = to_low_side(*normed_args, normed_own, normed_x, normed_low, 0)
+        out_copies = {ab: push(out_block(*ab, True), out_x.at[ab[0], ab[1]], to_x) for ab in order}
+
+        qkv_copies[1].wait_recv()
+        qkv_loads[1].wait()
+        chip_copy.wait_recv()
+        add_into(qkv_sum, qkv_own.at[0], qkv_core.at[0], qkv_chip)
+
+        def deal(kind):
+            index = kind * ctx + me
+            return pltpu.make_async_remote_copy(
+                qkv_sum.at[:, pl.ds(kind * cols, cols)],
+                dealt.at[lax.rem(index, kinds)],
+                deal_sems.at[0, kind],
+                deal_sems.at[1, lax.rem(index, kinds)],
+                device_id=(index // kinds, mine),
+                device_id_type=MESH,
+            )
+
+        def keep(kind):
+            return pltpu.make_async_copy(
+                qkv_sum.at[:, pl.ds(kind * cols, cols)],
+                dealt.at[lax.rem(kind * ctx + me, kinds)],
+                deal_sems.at[0, kind],
+            )
+
+        def is_far(kind):
+            return (kind * ctx + me) // kinds != me
+
+        for kind in range(kinds):
+            pl.when(is_far(kind))(deal(kind).start)
+            pl.when(jnp.logical_not(is_far(kind)))(keep(kind).start)
+
+        normed_high_copy = to_high_side(
+            *normed_args, normed_lows, normed_own, normed_x, normed_low, normed_high
+        )
+        high_copies[1] = experts_high(1)
+        low_copies.update({(2, a): push_low(2, a) for a in (1, 0)})
+        out_args = (out_copies, out_loads)
+        out_lows = {a: to_low_side(*out_args, out_own, out_x, out_low, a) for a in (1, 0)}
+
+        def experts_end(kind):
+            low_copies[kind, 0].wait_recv()
+            kept_loads[kind, 0].wait()
+            high_copies[kind].wait_recv()
+            add_into(grads_ref.at[kind], kept.at[kind, 0], kept_low.at[kind, 0], kept_high.at[kind])
+
+        experts_end(0)
+
+        normed_copies[0, 0].wait_recv()
+        normed_loads[0, 0].wait()
+        normed_lows[0].wait_recv()
+        normed_high_copy.wait_recv()
+
+        def norm_step(i, carry):
+            span = pl.ds(pl.multiple_of(i * 16, 16), 16)
+            grad = (
+                normed_own[0, 0, span, :].astype(f32)
+                + normed_x[0, 0, span, :].astype(f32)
+                + normed_low[0, span, :].astype(f32)
+                + normed_high[span, :].astype(f32)
+            )
+            values = tokens_ref[span, :].astype(f32)
+            scale = rms_unit(values)
+            unit = values * scale
+            pulled = grad * gain_ref[...]
+            input_ref[span, :] = mixed_ref[span, :] + scale * (
+                pulled - unit * jnp.mean(unit * pulled, axis=-1, keepdims=True)
+            )
+            return carry
+
+        lax.fori_loop(0, rows // 16, norm_step, 0)
+
+        out_high_copy = to_high_side(*out_args, out_lows, out_own, out_x, out_low, out_high)
+        high_copies[2] = experts_high(2)
+        experts_end(1)
+
+        total = small_sum[...]
+        for i, copy in enumerate(small_wide):
+            copy.wait_recv()
+            total = total + small_held[i]
+        sums_ref[...] = total
+
+        for kind in range(kinds):
+            pl.when(is_far(kind))(deal(kind).wait_send)
+            pl.when(jnp.logical_not(is_far(kind)))(keep(kind).wait)
+        for slot in range(kinds):
+
+            @pl.when(lax.rem(me * kinds + slot, ctx) != me)
+            def _():
+                pltpu.make_async_copy(
+                    dealt.at[slot], dealt.at[slot], deal_sems.at[1, slot]
+                ).wait()
+
+            add_into(qkv_ref.at[:, pl.ds(slot * cols, cols)], dealt.at[slot])
+
+        out_copies[0, 0].wait_recv()
+        out_loads[0, 0].wait()
+        out_lows[0].wait_recv()
+        out_high_copy.wait_recv()
+        add_into(out_ref, out_own.at[0, 0], out_x.at[0, 0], out_low.at[0], out_high)
+        experts_end(2)
+        for copy in all_sends:
+            copy.wait_send()
+
+    def block(*shape):
+        return pltpu.VMEM(shape, bf16)
+
+    gradient = (experts, units, cols)
+    return comm_call(
+        kernel,
+        "finish_sums",
+        collective_id,
+        [
+            jax.ShapeDtypeStruct((kinds,) + gradient, f32),
+            jax.ShapeDtypeStruct((rows, width), f32),
+            jax.ShapeDtypeStruct((part, cols), f32),
+            jax.ShapeDtypeStruct((part, kinds * cols), f32),
+            jax.ShapeDtypeStruct((small_rows, small_cols), f32),
+        ],
+        [ANY] * 4 + [VMEM] * 4,
+        [VMEM] * 5,
+        [
+            block(kinds, 2, *gradient),
+            block(kinds, 2, *gradient),
+            block(kinds, *gradient),
+            block(2, 2, rows, width),
+            block(2, 2, rows, width),
+            block(2, rows, width),
+            block(rows, width),
+            block(2, 2, part, cols),
+            block(2, 2, part, cols),
+            block(2, part, cols),
+            block(part, cols),
+            block(2, part, kinds * cols),
+            block(2, part, kinds * cols),
+            block(part, kinds * cols),
+            block(part, kinds * cols),
+            block(kinds, part, cols),
+            pltpu.VMEM((fsdp - 1, small_rows, small_cols), f32),
+            pltpu.VMEM((small_rows, small_cols), f32),
+            pltpu.VMEM((ctx - 1, small_rows, small_cols), f32),
+            DMA((copies_most,)),
+            DMA((copies_most,)),
+            DMA((32,)),
+            DMA((2, kinds)),
+        ],
+        700 * 2**20,
+    )(packed, normed_part, out_part, qkv_part, small, tokens, mixed_grad, gain)
+
+
 def on_device_heads(
     tokens,
     doc_lengths,
@@ -1561,8 +1757,6 @@
         fsdp,
         capacity,
     )
-    high_bits = [2**i for i in range(1, ctx.bit_length() - 1)]
-
     mixed_all, mixed_grad, g_ffn_gain = reduce_then_gather(
         group_grad,
         [mixed, row_gain_two, cotangent[0]],
@@ -1576,15 +1770,6 @@
     g_out = dot32("td,te->de", attended_part, mixed_all).astype(bf16)
     output_grad, packed = lax.optimization_barrier((rows_to_heads(output_part, 3), packed))
 
-    def finish(kind):
-        values = packed[kind, 1].astype(f32) + swap(packed[kind, 0], "ctx", 2).astype(f32)
-        for bit in high_bits[1:]:
-            left = values.shape[1] // 2
-            values = halved(values.reshape((experts, left, 2) + values.shape[2:]), 2, "ctx", bit)
-        return values[:, 0]
-
-    down_parts, gate_parts, up_parts = (finish(kind) for kind in range(3))
-
     back, value_grad, own_g_gains, inner_sums = attend_back(
         output_grad, low, attended, tops, projected, scales, own_gains, *turn_tables, *sight
     )
@@ -1599,21 +1784,6 @@
     g_qkv = dot32("td,te->de", normed_all, proj_grad).astype(bf16)
     normed_grad_part = dot32("te,de->td", proj_grad, qkv_weight)
     g_attn_gain = jnp.sum(normed_grad_part * unit_all, axis=0)
-    normed_grad = lax.psum_scatter(
-        normed_grad_part.astype(bf16), "ctx", scatter_dimension=0, tiled=True
-    ).astype(f32)
-    scale_one = rms_unit(inputs)
-    unit_one = inputs * scale_one
-    pulled_one = normed_grad * gain_one
-    input_grad = mixed_grad + scale_one * (
-        pulled_one - unit_one * jnp.mean(unit_one * pulled_one, axis=-1, keepdims=True)
-    )
-
-    out_part = scatter_sum(g_out, 1, "ctx", [1] + high_bits)
-    qkv_shard = scatter_sum(g_qkv, 0, "fsdp", [2**i for i in range(fsdp.bit_length() - 1)])
-    qkv_shard = qkv_shard.astype(bf16).reshape(part, 3, cols).transpose(1, 0, 2)
-    qkv_part = deal_columns(qkv_shard, 4).transpose(1, 0, 2).reshape(part, 3 * cols).astype(f32)
-
     def placed_cols(values):
         return lax.dynamic_update_slice_in_dim(jnp.zeros((width,), f32), values, me * cols, 0)
 
@@ -1624,7 +1794,17 @@
         ],
         axis=0,
     )
-    sums = mesh_sum(jnp.pad(sums, ((0, -sums.shape[0] % 8), (0, 0))), 5)
+    grads, input_grad, out_part, qkv_part, sums = finish_sums(
+        packed,
+        normed_grad_part.astype(bf16),
+        g_out,
+        g_qkv,
+        jnp.pad(sums, ((0, -sums.shape[0] % 8), (0, 0))),
+        tokens[0],
+        mixed_grad,
+        gain_one.reshape(1, width),
+        8,
+    )
     return (
         activations[None],
         input_grad[None],
@@ -1635,9 +1815,9 @@
         out_part,
         sums[3],
         sums[4 : 4 + experts].T,
-        gate_parts,
-        up_parts,
-        down_parts,
+        grads[1],
+        grads[2],
+        grads[0],
     )
 
 

time: 750 us -> 676 us (0.901)
  the two profiles are of different devices: /device:TPU:3 before, /device:TPU:5 now
where the time goes in v4:
time: 676 us; the launch traced here: 666 us
  Pallas kernels  481 us (71%)
  waiting for transfers between devices  79.3 us (12%)
  local copies, waits for them, and re-layouts  31.5 us (5%)
  matrix products  28.6 us (4%)
  other arithmetic  16.9 us (2%)
  between operations  14.6 us (2%)
  blocking collectives  10.9 us (2%)
    pallas_call x1, Pallas kernels, finish_sums(): comm_call(kernel, 'finish_sums', collective_id, [jax.ShapeDtypeStruct((ki...  242 us
    pallas_call x1, Pallas kernels, rows_to_heads(): comm_call(kernel, 'rows_to_heads', collective_id, jax.ShapeDtypeStruct((c...  60.6 us
    pallas_call x2, Pallas kernels, reduce_then_gather(): comm_call(kernel, name, collective_id, [jax.ShapeDtypeStruct(partial.shap...  59 us
    all_gather x1, waiting for transfers between devices, on_device_heads(): tokens_all = lax.all_gather(tokens[0], 'ctx', axis=0, tiled=True)  51.6 us
    pallas_call x1, Pallas kernels, run_experts(): pl.pallas_call(kernel, grid=(experts,), out_shape=[jax.ShapeDtypeStruct((...  36.1 us
    dot_general x6, matrix products, dot32(): return jnp.einsum(spec, left, right, preferred_element_type=jnp.float32)  28.6 us
    all_gather x1, waiting for transfers between devices, on_device_heads(): qkv_weight = lax.all_gather(own_cols, 'fsdp', axis=0, tiled=True)  26.3 us
    pallas_call x1, Pallas kernels, attend_back(): pl.pallas_call(kernel, out_shape=[jax.ShapeDtypeStruct((2, total, cols),...  16.5 us
  transfers between devices with their start and end apart: 8, of which 2 were waited for; matrix products, arithmetic and copies ran while one was open for 9% of the time, Pallas kernels for 67%

profile of v4, /device:TPU:5, one launch (start us, length us, event | category | flops | bytes accessed | tf_op | source)
XLA Modules:
  0.0 665.5 jit_solution(10737502390579088516)
XLA Ops:
  7.3 0.7 all-gather.9.cloned.1.call-update
  8.1 1.2 constant_dynamic-slice_fusion.4
  9.2 0.9 pad_maximum_fusion.1
  10.2 0.7 all-gather.11.cloned.1.call-update
  11.0 0.6 compare_select_fusion.places_ref
  11.8 5.7 all_gather.19
  17.6 0.9 fusion.26.last_ref
  18.7 5.2 all-gather.2
  24.7 0.8 convert_reduce_fusion
  26.0 1.0 copy.58.first_ref
  27.1 0.6 pad_maximum_fusion.6
  27.6 0.6 pad.13.router_ref
  28.3 0.6 pad.12.slots_ref.slots_own_ref
  28.9 1.9 fusion.33
  30.8 1.3 pad_maximum_fusion.4
  32.1 51.6 %all-gather.9.cloned.1.call-done = bf16[1,1024,2048]{2,1,0:T(8,128)(2,1)} async-done(((bf16[1,128,2048]{2,1,0:T(8,128)(2,1)}), bf16[1,1024,2048]{2,1,0:T(8,128)(2,1)}) %all-gather.9.cloned.1.call-update) | async-done | bytes 4194320 | tf_op jit(solution)/shard_map/all_gather | solution.py:1671
  83.7 3.1 fusion.4
  86.8 26.3 %all-gather.7.cloned.1.call-done = bf16[2048,768]{1,0:T(8,128)(2,1)} async-done(((bf16[512,768]{1,0:T(8,128)(2,1)}), bf16[2048,768]{1,0:T(8,128)(2,1)}) %all-gather.7.cloned.1.call-update) | async-done | bytes 3145744 | tf_op jit(solution)/shard_map/all_gather | solution.py:1685
  113.1 8.4 %fusion.6 = f32[1024,768]{0,1:T(8,128)} fusion(bf16[2048,768]{1,0:T(8,128)(2,1)} %all-gather.7.cloned.1.call-done, bf16[1,1024,2048]{2,1,0:T(8,128)(2,1)} %all-gather.9.cloned.1.call-done, f32[2048]{0:T(1024)S(1)} %bitcast.81, f32[1024]{0:T(1024)S(1)} %add_rsqrt_fusion.1), kind=kOutput, calls=%fused_computation.18 | convolution fusion | flops 3229614080 | bytes 10498048 | tf_op jit(solution)/shard_map/td,de->te/dot_general | solution.py:493
  121.6 3.7 copy.57.lin_ref
  125.2 1.8 bitcast_reduce_fusion
  127.1 6.4 ctx_sum.2
  133.5 1.0 copy.56
  134.5 12.0 %attend.1 = (bf16[1024,768]{1,0:T(8,128)(2,1)}, f32[1024,256]{1,0:T(8,128)}, bf16[1024,256]{1,0:T(8,128)(2,1)}, f32[1024,256]{1,0:T(8,128)}) custom-call(f32[1024,768]{1,0:T(8,128)} %copy.57.lin_ref, f32[1024,2]{1,0:T(8,128)} %bitcast.86, f32[1,512]{1,0:T(1,128)} %bitcast.98, f32[1024,128]{1,0:T(8,128)} %get-tuple-element.90.cos_ref, ...), custom_call_target="tpu_custom_call" | custom-call | flops 2000000000 | bytes 20971520 | tf_op jit(solution)/shard_map/attend/pallas_call | solution.py:1191
  146.5 1.0 copy-done.19
  147.6 14.7 %heads_to_rows.1 = bf16[512,512]{1,0:T(8,128)(2,1)S(1)} custom-call(bf16[1024,256]{1,0:T(8,128)(2,1)S(1)} %copy-done.19), custom_call_target="tpu_custom_call" | custom-call | bytes 41943040 | tf_op jit(solution)/shard_map/heads_to_rows/pallas_call | solution.py:634
  162.3 1.3 convolution_convert_fusion.2.refs_0_
  163.6 28.1 %mix_and_norm.1 = (bf16[512,2048]{1,0:T(8,128)(2,1)S(1)}, f32[128,2048]{1,0:T(8,128)S(1)}) custom-call(bf16[512,2048]{1,0:T(8,128)(2,1)S(1)} %convolution_convert_fusion.2.refs_0_, bf16[128,2048]{1,0:T(8,128)(2,1)S(1)} %bitcast.77, f32[1,2048]{1,0:T(1,128)S(1)} %get-tuple-element.72.refs_2_), custom_call_target="tpu_custom_call" | custom-call | bytes 104857600 | tf_op jit(solution)/shard_map/mix_and_norm/pallas_call | solution.py:787
  191.7 1.4 copy-done.2
  193.1 1.0 copy-done.4
  194.1 36.1 %run_experts.1 = (bf16[512,2048]{1,0:T(8,128)(2,1)}, bf16[512,2048]{1,0:T(8,128)(2,1)}, f32[16,2048]{1,0:T(8,128)}, bf16[3,6,256,256]{3,2,1,0:T(8,128)(2,1)}) custom-call(bf16[512,2048]{1,0:T(8,128)(2,1)} %copy-done.2, bf16[512,2048]{1,0:T(8,128)(2,1)} %bitcast.83, s32[16,512]{1,0:T(8,128)} %pad.12.slots_ref.slots_own_ref, bf16[16,2048]{1,0:T(8,128)(2,1)} %pad.13.router_ref, ...), custom_call_target="tpu_custom_call" | custom-call | flops 30000001024 | bytes 31457280 | tf_op jit(solution)/shard_map/run_experts/pallas_call | solution.py:979
  230.2 1.3 collective-permute-start
  231.5 2.7 pick_half.7
  234.4 2.7 pick_half.5
  237.1 1.2 collective-permute-start.1
  238.6 2.7 pick_half.6.dy_own_ref
  241.4 1.2 copy-done.5
  242.6 30.9 %norm_back.1 = (bf16[512,2048]{1,0:T(8,128)(2,1)S(1)}, f32[128,2048]{1,0:T(8,128)S(1)}, f32[1,2048]{1,0:T(1,128)S(1)}) custom-call(bf16[512,2048]{1,0:T(8,128)(2,1)} %get-tuple-element.40.refs_0_, f32[128,2048]{1,0:T(8,128)S(1)} %copy-done.5, f32[1,2048]{1,0:T(1,128)S(1)} %get-tuple-element.72.refs_2_, bf16[128,2048]{1,0:T(8,128)(2,1)S(1)} %bitcast.79), custom_call_target="tpu_custom_call" | custom-call | bytes 104857600 | tf_op jit(solution)/shard_map/norm_back/pallas_call | solution.py:787
  273.5 2.7 convolution_convert_fusion.1.g_out_ref
  276.2 1.3 convolution_convert_fusion.3.own_ref
  278.0 2.7 pick_half.4.in_own_ref
  280.8 60.6 %rows_to_heads.1.grad_ref = bf16[1024,256]{1,0:T(8,128)(2,1)S(1)} custom-call(bf16[512,512]{1,0:T(8,128)(2,1)S(1)} %convolution_convert_fusion.3.own_ref), custom_call_target="tpu_custom_call" | custom-call | bytes 41943040 | tf_op jit(solution)/shard_map/rows_to_heads/pallas_call | solution.py:708
  341.3 0.8 copy-done.8
  342.2 0.6 copy-done.33
  342.7 14.8 %expert_grads.1.packed_ref = bf16[3,2,6,2,256,256]{5,4,3,2,1,0:T(8,128)(2,1)} custom-call(bf16[3,6,256,256]{3,2,1,0:T(8,128)(2,1)} %get-tuple-element.42.own_ref, bf16[3,6,256,256]{3,2,1,0:T(8,128)(2,1)} %collective-permute-done.other_ref, bf16[512,1024]{1,0:T(8,128)(2,1)} %pick_half.4.in_own_ref, bf16[512,1024]{1,0:T(8,128)(2,1)} %collective-permute-done.1.in_other_ref, ...), custom_call_target="tpu_custom_call" | custom-call | flops 20000000000 | bytes 31457280 | tf_op jit(solution)/shard_map/expert_grads/pallas_call | solution.py:1085
  357.6 16.5 %attend_back.1 = (f32[2,1024,256]{2,1,0:T(8,128)}, bf16[1024,256]{1,0:T(8,128)(2,1)}, f32[2,1,256]{2,1,0:T(1,128)}, f32[1024,2]{1,0:T(8,128)}) custom-call(bf16[1024,256]{1,0:T(8,128)(2,1)} %copy-done.8, bf16[1024,768]{1,0:T(8,128)(2,1)} %get-tuple-element.45.low_ref, f32[1024,256]{1,0:T(8,128)} %get-tuple-element.46.attended_ref, ...), custom_call_target="tpu_custom_call" | custom-call | bytes 1048576 | tf_op jit(solution)/shard_map/attend_back/pallas_call | solution.py:1289
  374.1 1.3 copy.68
  375.4 7.8 %ctx_sum.3 = f32[16,128]{1,0:T(8,128)S(1)} custom-call(f32[16,128]{1,0:T(8,128)S(1)} %reshape.249.own_ref), custom_call_target="tpu_custom_call" | custom-call | bytes 20971520 | tf_op jit(solution)/shard_map/ctx_sum/pallas_call | solution.py:545
  383.2 0.8 constant_dynamic-update-slice_fusion
  384.1 0.9 constant_dynamic-update-slice_fusion.1
  385.0 2.6 fusion.15
  387.6 7.0 %fusion.3 = (f32[2048]{0:T(1024)S(1)}, bf16[1024,2048]{1,0:T(8,128)(2,1)}) fusion(bf16[1,1024,2048]{2,1,0:T(8,128)(2,1)S(1)} %copy-done.21, f32[1024]{0:T(1024)S(1)} %add_rsqrt_fusion.1, bf16[2048,768]{1,0:T(8,128)(2,1)} %all-gather.7.cloned.1.call-done, bf16[1024,256]{1,0:T(8,128)(2,1)S(1)} %copy-done.32, bf16[1024,256]{1,0:T(8,128)(2,1)S(1)} %get-tuple-element.68, ...), kind=kOutput, calls=%fused_computation.5 | convolution fusion | flops 3236427776 | bytes 13119488 | tf_op jit(solution)/shard_map/te,de->td/dot_general | solution.py:493
  395.0 8.0 %convolution_convert_fusion.g_qkv_ref = bf16[2048,768]{1,0:T(8,128)(2,1)} fusion(bf16[1,1024,2048]{2,1,0:T(8,128)(2,1)} %all-gather.9.cloned.1.call-done, f32[2048]{0:T(1024)S(1)} %bitcast.82, f32[1024]{0:T(1024)S(1)} %add_rsqrt_fusion.1, bf16[1024,256]{1,0:T(8,128)(2,1)} %get-tuple-element.50, bf16[1024,256]{1,0:T(8,128)(2,1)S(1)} %get-tuple-element.68, ...), kind=kOutput, calls=%fused_computation.7 | convolution fusion | flops 3235905536 | bytes 8925184 | tf_op jit(solution)/shard_map/td,te->de/dot_general | solution.py:493
  403.0 241.8 %finish_sums.1 = (f32[3,6,256,256]{3,2,1,0:T(8,128)}, f32[128,2048]{1,0:T(8,128)S(1)}, f32[512,256]{1,0:T(8,128)S(1)}, f32[512,768]{1,0:T(8,128)S(1)}, f32[16,512]{1,0:T(8,128)S(1)}) custom-call(bf16[3,2,6,2,256,256]{5,4,3,2,1,0:T(8,128)(2,1)} %expert_grads.1.packed_ref, bf16[1024,2048]{1,0:T(8,128)(2,1)} %get-tuple-element.63.normed_ref, ...), custom_call_target="tpu_custom_call" | custom-call | bytes 734003200 | tf_op jit(solution)/shard_map/finish_sums/pallas_call | solution.py:1602
  644.8 1.1 copy-done.9
  645.9 1.0 copy-done.13
  646.9 0.8 copy-done.17
  647.7 0.6 fusion.53
  648.3 0.6 slice_bitcast_fusion.3
  648.9 4.9 slice_bitcast_fusion
  653.8 2.1 fusion.32
  655.9 1.0 copy.81
  656.8 1.1 copy.82
  658.0 0.8 copy.83
  (115 shorter events, 3.5 us)
Async XLA Ops:
  7.2 155.1 %copy-start = (bf16[512,2048]{1,0:T(8,128)(2,1)S(1)}, bf16[512,2048]{1,0:T(8,128)(2,1)}, u32[]{:S(2)}) copy-start(bf16[512,2048]{1,0:T(8,128)(2,1)} %param.23) | copy-start | bytes 6291460
  7.2 4.4 copy-start.27
  7.2 4.4 copy-start.28
  7.2 4.4 copy-start.29
  7.2 4.4 copy-start.30
  7.2 4.4 copy-start.24
  7.2 11.3 %copy-start.31 = (s32[1,16]{1,0:T(1,128)S(1)}, s32[1,16]{1,0:T(1,128)}, u32[]{:S(2)}) copy-start(s32[1,16]{1,0:T(1,128)} %param.16) | copy-start | bytes 196
  7.3 11.4 %copy-start.25 = (s32[1,128,3]{1,0,2:T(1,128)S(1)}, s32[1,128,3]{1,0,2:T(1,128)}, u32[]{:S(2)}) copy-start(s32[1,128,3]{1,0,2:T(1,128)} %param.17) | copy-start | bytes 4612
  7.3 11.4 %copy-start.26 = (s32[1,128,3]{1,0,2:T(1,128)S(1)}, s32[1,128,3]{1,0,2:T(1,128)}, u32[]{:S(2)}) copy-start(s32[1,128,3]{1,0,2:T(1,128)} %param.18) | copy-start | bytes 4612
  7.3 76.5 %all-gather.9.cloned.1.call-start = ((), (), s32[]{:S(2)}) async-start(), calls=%async_computation.3 | async-start | bytes 4718592 | tf_op jit(solution)/shard_map/all_gather | solution.py:1671
  8.0 105.1 %all-gather.7.cloned.1.call-start = ((), (), s32[]{:S(2)}) async-start(), calls=%async_computation.1 | async-start | bytes 3932160 | tf_op jit(solution)/shard_map/all_gather | solution.py:1685
  10.2 183.9 %all-gather.11.cloned.1.call-start = ((), (), s32[]{:S(2)}) async-start(), calls=%async_computation.4 | async-start | bytes 2621440 | tf_op jit(solution)/shard_map/all_gather | solution.py:1686
  10.9 642.8 %reduce-scatter.2.cloned.1.call-start = ((), (), s32[]{:S(2)}) async-start(), calls=%async_computation.2 | async-start | bytes 2621440 | tf_op jit(solution)/shard_map/reduce_scatter | solution.py:1745
  146.5 1.0 copy-start.19
  162.3 1.3 copy-start.15
  162.3 1.3 copy-start.3
  191.7 1.4 copy-start.2
  193.1 1.0 copy-start.4
  230.2 8.2 %copy-start.22 = (s32[16,512]{1,0:T(8,128)S(1)}, s32[16,512]{1,0:T(8,128)}, u32[]{:S(2)}) copy-start(s32[16,512]{1,0:T(8,128)} %pad.12.slots_ref.slots_own_ref) | copy-start | bytes 98308
  230.2 112.0 %collective-permute-start = (bf16[3,6,256,256]{3,2,1,0:T(8,128)(2,1)}, bf16[3,6,256,256]{3,2,1,0:T(8,128)(2,1)}, u32[]{:S(2)}, u32[]{:S(2)}) collective-permute-start(bf16[3,6,256,256]{3,2,1,0:T(8,128)(2,1)} %get-tuple-element.42.own_ref), channel_id=1, source_target_pairs={{0,4},{4,0},{8,12},{12,8},{16,20},{20,16},{24,28},{28,24},{1,5},{5... | collective-permute-start | bytes 7077896 | tf_op jit(solution)/shard_map/ppermute | solution.py:721
  234.2 7.2 %copy-start.7 = (bf16[1,128,2048]{2,1,0:T(8,128)(2,1)S(1)}, bf16[1,128,2048]{2,1,0:T(8,128)(2,1)}, u32[]{:S(2)}) copy-start(bf16[1,128,2048]{2,1,0:T(8,128)(2,1)} %param.29) | copy-start | bytes 1572868
  234.2 108.0 %collective-permute-start.2 = (bf16[512,1024]{1,0:T(8,128)(2,1)}, bf16[512,1024]{1,0:T(8,128)(2,1)}, u32[]{:S(2)}, u32[]{:S(2)}) collective-permute-start(bf16[512,1024]{1,0:T(8,128)(2,1)} %pick_half.7), channel_id=1, source_target_pairs={{0,4},{4,0},{8,12},{12,8},{16,20},{20,16},{24,28},{28,24},{1,5},{5... | collective-permute-start | bytes 3145736 | tf_op jit(solution)/shard_map/ppermute | solution.py:721
  237.1 105.0 %collective-permute-start.1 = (bf16[512,1024]{1,0:T(8,128)(2,1)}, bf16[512,1024]{1,0:T(8,128)(2,1)}, u32[]{:S(2)}, u32[]{:S(2)}) collective-permute-start(bf16[512,1024]{1,0:T(8,128)(2,1)} %pick_half.5), channel_id=1, source_target_pairs={{0,4},{4,0},{8,12},{12,8},{16,20},{20,16},{24,28},{28,24},{1,5},{5... | collective-permute-start | bytes 3145736 | tf_op jit(solution)/shard_map/ppermute | solution.py:721
  238.4 103.8 %collective-permute-start.3 = (s32[16,512]{1,0:T(8,128)S(1)}, s32[16,512]{1,0:T(8,128)S(1)}, u32[]{:S(2)}, u32[]{:S(2)}) collective-permute-start(s32[16,512]{1,0:T(8,128)S(1)} %copy-done.22), channel_id=1, source_target_pairs={{0,4},{4,0},{8,12},{12,8},{16,20},{20,16},{24,28},{28,24},{1,5},{5... | collective-permute-start | bytes 98312 | tf_op jit(solution)/shard_map/ppermute | solution.py:721
  241.4 1.2 copy-start.5
  242.6 30.9 %copy-start.16 = (bf16[512,512]{1,0:T(8,128)(2,1)S(1)}, bf16[512,512]{1,0:T(8,128)(2,1)}, u32[]{:S(2)}) copy-start(bf16[512,512]{1,0:T(8,128)(2,1)} %copy-done.15) | copy-start | bytes 1572868
  273.5 4.0 copy-start.11
  276.2 1.3 copy-start.20
  277.5 3.2 copy-start.23
  341.3 0.8 copy-start.8
  342.1 0.6 copy-start.33
  374.1 13.5 %copy-start.32 = (bf16[1024,256]{1,0:T(8,128)(2,1)S(1)}, bf16[1024,256]{1,0:T(8,128)(2,1)}, u32[]{:S(2)}) copy-start(bf16[1024,256]{1,0:T(8,128)(2,1)} %get-tuple-element.50) | copy-start | bytes 1572868
  383.2 4.4 copy-start.21
  395.0 8.0 %copy-start.12 = (f32[128,2048]{1,0:T(8,128)S(1)}, f32[128,2048]{1,0:T(8,128)}, u32[]{:S(2)}) copy-start(f32[128,2048]{1,0:T(8,128)} %copy-done.11) | copy-start | bytes 3145732
  644.8 1.1 copy-start.9
  645.9 1.0 copy-start.13
  646.9 0.8 copy-start.17
  648.9 4.9 copy-start.6
  648.9 6.9 %copy-start.14 = (f32[128,2048]{1,0:T(8,128)S(1)}, f32[128,2048]{1,0:T(8,128)}, u32[]{:S(2)}) copy-start(f32[128,2048]{1,0:T(8,128)} %copy-done.13) | copy-start | bytes 3145732
  653.8 3.0 copy-start.10
  655.9 2.1 copy-start.18
  655.9 2.9 copy-start.1
Sparse Core Ops, SparseCore 0:
  10.2 73.4 all-gather.8
  85.9 27.2 all-gather.6
  114.7 22.5 all-gather.10
  280.9 34.2 reduce-scatter.1
